TPU v7x, 128 devices: a whole 4x4x4 slice. The times are simulated.
128 devices in a mesh: section: 2 (over core), seq: 4 (over z), shard: 16 (over y, x).
Axes of the slice: x: 4, y: 4, z: 4, core: 2. Of those that a mesh axis runs over, the one named last changes fastest.
Arguments:
- acts_in: bfloat16 [2, 16, 288, 1024], P(None, 'shard', 'seq'), may hold values from -6 to 6
- cotangent: bfloat16 [2, 16, 288, 1024], P(None, 'shard', 'seq'), may hold values from -6 to 6
- qkv_weight: bfloat16 [2, 1024, 3072], P('section', 'shard'), may hold values from -0.1875 to 0.1875
- out_weight: bfloat16 [2, 1024, 1024], P('section', 'shard'), may hold values from -0.75 to 0.75
- up_weight: bfloat16 [2, 1024, 4096], P('section', 'shard'), may hold values from -0.1875 to 0.1875
- down_weight: bfloat16 [2, 4096, 1024], P('section', 'shard'), may hold values from -0.09375 to 0.09375
- vectors: bfloat16 [2, 4, 1024], P('section', None, 'shard'), may hold values from 0.25 to 1.75
- image_ids: int32 [2, 16, 288], P(None, 'shard'), may hold values from 0 to 2, as said below
Outputs:
- layer_out: bfloat16 [2, 2, 16, 288, 1024], P('section', None, 'shard', 'seq')
- grad_in: bfloat16 [2, 2, 16, 288, 1024], P('section', None, 'shard', 'seq')
- qkv_grad: float32 [2, 1024, 3072], P('section', 'shard')
- out_grad: float32 [2, 1024, 1024], P('section', 'shard')
- up_grad: float32 [2, 1024, 4096], P('section', 'shard')
- down_grad: float32 [2, 4096, 1024], P('section', 'shard')
- vector_grad: float32 [2, 4, 1024], P('section', None, 'shard')
Inputs may be any that keep to these rules, and one draw needn't show every extreme that they name: `image_ids`: in every pack the ids never fall and begin at 0. In micro-batch 0 a pack holds the tail of an image, then one whole crop of 257 tokens (id 1), then the head of the next image; in micro-batch 1 it holds the tail of an image, then a piece of another (id 1) that fills the pack. In every pack one image begins within the first 72 tokens and ends within the last 72.
All inputs are finite; a program needn't handle non-finite values.
Results may differ from a plain program's by a relative error of at most 0.023.
Values may be sent and summed in bfloat16 or wider, within the bound.
A program may use at most 192 MiB of HBM per device.

v0:
```python
import jax
import jax.numpy as jnp
from jax import lax
from jax.sharding import PartitionSpec as P

HEAD_DIM = 64


EPS = 1e-06
NEG = -1e30


def from_behind(value, axis, by):
    peers = lax.axis_size(axis)
    pairs = [(i, i + by) for i in range(peers) if 0 <= i + by < peers]
    return lax.ppermute(value, axis, pairs)


def shortened(value):
    return jax.tree.map(lambda a: a.astype(jnp.bfloat16) if a.dtype == jnp.float32 else a, value)


def layer_norm(values, gain):
    centre = values - jnp.mean(values, axis=-1, keepdims=True)
    spread = jnp.mean(centre * centre, axis=-1, keepdims=True)
    return centre * lax.rsqrt(spread + EPS) * gain


def gelu_exact(values):
    return jax.nn.gelu(values, approximate=False)


def inner_rows(left_mat, right_mat):
    return lax.dot_general(
        left_mat, right_mat, (((0,), (0,)), ((), ())), preferred_element_type=jnp.float32
    )


def inner_cols(left_mat, right_mat):
    return lax.dot_general(
        left_mat, right_mat, (((1,), (1,)), ((), ())), preferred_element_type=jnp.float32
    )


def head_scores(queries, keys_all, image_row):
    scores = jnp.einsum(
        "qhd,khd->hqk", queries, keys_all, preferred_element_type=jnp.float32
    ) * HEAD_DIM ** (-0.5)
    same_image = image_row[:, None] == image_row[None, :]
    return jnp.where(same_image[None], scores, NEG)


def layer_forward(tokens, image_row, weights):
    w_qkv, w_out, w_up, w_down, vecs = weights
    gain_rows = vecs.astype(jnp.float32)
    seq_count = lax.axis_size("seq")
    row_count = tokens.shape[0]
    pack_len = row_count * seq_count
    head_cols = w_qkv.shape[1] // (3 * seq_count)
    local_heads = head_cols // HEAD_DIM
    normed = layer_norm(tokens, gain_rows[0]).astype(jnp.bfloat16)
    packed = jnp.dot(normed, w_qkv, preferred_element_type=jnp.float32).astype(jnp.bfloat16)
    regrouped = lax.all_to_all(
        packed.reshape(row_count, 3, seq_count, head_cols),
        "seq",
        split_axis=2,
        concat_axis=0,
        tiled=True,
    )
    queries = regrouped[:, 0, 0].reshape(pack_len, local_heads, HEAD_DIM)
    keys_all = regrouped[:, 1, 0].reshape(pack_len, local_heads, HEAD_DIM)
    values_all = regrouped[:, 2, 0].reshape(pack_len, local_heads, HEAD_DIM)
    scores = head_scores(queries, keys_all, image_row)
    row_max = jnp.max(scores, axis=-1, keepdims=True)
    raised = jnp.exp(scores - row_max)
    row_total = jnp.sum(raised, axis=-1, keepdims=True)
    soft_weights = (raised / row_total).astype(jnp.bfloat16)
    log_total = row_max + jnp.log(row_total)
    attended = jnp.einsum(
        "hqk,khd->qhd", soft_weights, values_all, preferred_element_type=jnp.float32
    )
    attended = attended.reshape(pack_len, 1, head_cols).astype(jnp.bfloat16)
    joined = lax.all_to_all(attended, "seq", split_axis=0, concat_axis=1, tiled=True).reshape(
        row_count, seq_count * head_cols
    )
    branch = jnp.dot(joined, w_out, preferred_element_type=jnp.float32)
    middle = tokens + gain_rows[1] * branch
    hidden_in = layer_norm(middle, gain_rows[2]).astype(jnp.bfloat16)
    pre_act = jnp.dot(hidden_in, w_up, preferred_element_type=jnp.float32)
    activated = gelu_exact(pre_act).astype(jnp.bfloat16)
    result = jnp.dot(activated, w_down, preferred_element_type=jnp.float32)
    output = middle + gain_rows[3] * result
    stored = (
        tokens,
        image_row,
        normed,
        queries,
        keys_all,
        values_all,
        log_total,
        joined,
        branch,
        middle,
        hidden_in,
        pre_act,
        activated,
        result,
    )
    return (output, stored)


def layer_backward(grad_out, stored, weights):
    (
        tokens,
        image_row,
        normed,
        queries,
        keys_all,
        values_all,
        log_total,
        joined,
        branch,
        middle,
        hidden_in,
        pre_act,
        activated,
        result,
    ) = stored
    w_qkv, w_out, w_up, w_down, vecs = weights
    gain_rows = vecs.astype(jnp.float32)
    seq_count = lax.axis_size("seq")
    row_count = grad_out.shape[0]
    pack_len = row_count * seq_count
    head_cols = w_qkv.shape[1] // (3 * seq_count)
    local_heads = head_cols // HEAD_DIM
    grad_result = (grad_out * gain_rows[3]).astype(jnp.bfloat16)
    gain_mlp = jnp.sum(grad_out * result, axis=0)
    down_part = inner_rows(activated, grad_result)
    grad_activ = inner_cols(grad_result, w_down)
    _, gelu_pull = jax.vjp(gelu_exact, pre_act)
    grad_pre = gelu_pull(grad_activ)[0].astype(jnp.bfloat16)
    up_part = inner_rows(hidden_in, grad_pre)
    grad_hidden = inner_cols(grad_pre, w_up)
    _, second_pull = jax.vjp(layer_norm, middle, gain_rows[2])
    grad_mid_norm, gain_second = second_pull(grad_hidden)
    grad_middle = grad_out + grad_mid_norm
    grad_branch = (grad_middle * gain_rows[1]).astype(jnp.bfloat16)
    gain_attn = jnp.sum(grad_middle * branch, axis=0)
    out_part = inner_rows(joined, grad_branch)
    grad_joined = inner_cols(grad_branch, w_out).astype(jnp.bfloat16)
    grad_heads = lax.all_to_all(
        grad_joined.reshape(row_count, seq_count, head_cols),
        "seq",
        split_axis=1,
        concat_axis=0,
        tiled=True,
    )
    grad_heads = grad_heads.reshape(pack_len, local_heads, HEAD_DIM)
    scores = head_scores(queries, keys_all, image_row)
    soft_full = jnp.exp(scores - log_total)
    grad_soft = jnp.einsum(
        "qhd,khd->hqk", grad_heads, values_all, preferred_element_type=jnp.float32
    )
    grad_values = jnp.einsum(
        "hqk,qhd->khd",
        soft_full.astype(jnp.bfloat16),
        grad_heads,
        preferred_element_type=jnp.float32,
    )
    row_dot = jnp.sum(soft_full * grad_soft, axis=-1, keepdims=True)
    grad_scores = (soft_full * (grad_soft - row_dot)).astype(jnp.bfloat16)
    grad_queries = jnp.einsum(
        "hqk,khd->qhd", grad_scores, keys_all, preferred_element_type=jnp.float32
    ) * HEAD_DIM ** (-0.5)
    grad_keys = jnp.einsum(
        "hqk,qhd->khd", grad_scores, queries, preferred_element_type=jnp.float32
    ) * HEAD_DIM ** (-0.5)
    grad_stack = jnp.stack([grad_queries, grad_keys, grad_values], axis=1).astype(jnp.bfloat16)
    grad_stack = grad_stack.reshape(pack_len, 3, 1, head_cols)
    grad_packed = lax.all_to_all(
        grad_stack, "seq", split_axis=0, concat_axis=2, tiled=True
    ).reshape(row_count, 3 * seq_count * head_cols)
    qkv_part = inner_rows(normed, grad_packed)
    grad_normed = inner_cols(grad_packed, w_qkv)
    _, first_pull = jax.vjp(layer_norm, tokens, gain_rows[0])
    grad_tok_norm, gain_first = first_pull(grad_normed)
    grad_tokens = grad_middle + grad_tok_norm
    vector_part = jnp.stack([gain_first, gain_attn, gain_second, gain_mlp])
    return (grad_tokens, (qkv_part, out_part, up_part, down_part, vector_part))


def local(acts_in, cotangent, qkv_weight, out_weight, up_weight, down_weight, vectors, image_ids):
    on_first = lax.axis_index("section") == 0
    micro_count = acts_in.shape[0]
    row_count = acts_in.shape[2]
    own_rows = (qkv_weight[0], out_weight[0], up_weight[0], down_weight[0], vectors[0])
    weights = (
        lax.all_gather(own_rows[0], "shard", axis=0, tiled=True),
        lax.all_gather(own_rows[1], "shard", axis=0, tiled=True),
        lax.all_gather(own_rows[2], "shard", axis=0, tiled=True),
        lax.all_gather(own_rows[3], "shard", axis=0, tiled=True),
        lax.all_gather(own_rows[4], "shard", axis=1, tiled=True),
    )
    received = jnp.zeros(acts_in.shape[2:], jnp.bfloat16)
    outputs = []
    stored_all = []
    for moment in range(micro_count + 1):
        early_m = min(moment, micro_count - 1)
        late_m = max(moment - 1, 0)
        tokens = jnp.where(
            on_first, acts_in[early_m, 0].astype(jnp.float32), received.astype(jnp.float32)
        )
        image_row = jnp.where(on_first, image_ids[early_m, 0], image_ids[late_m, 0])
        output, stored = layer_forward(tokens, image_row, weights)
        sending = output.astype(jnp.bfloat16)
        outputs.append(sending)
        stored_all.append(stored)
        if moment < micro_count:
            received = from_behind(sending, "section", 1)
    layer_out = jnp.stack(
        [
            jnp.where(on_first, outputs[micro_m], outputs[micro_m + 1])
            for micro_m in range(micro_count)
        ]
    )
    weights = (
        lax.all_gather(own_rows[0], "shard", axis=0, tiled=True),
        lax.all_gather(own_rows[1], "shard", axis=0, tiled=True),
        lax.all_gather(own_rows[2], "shard", axis=0, tiled=True),
        lax.all_gather(own_rows[3], "shard", axis=0, tiled=True),
        lax.all_gather(own_rows[4], "shard", axis=1, tiled=True),
    )
    incoming = jnp.zeros(acts_in.shape[2:], jnp.bfloat16)
    summed = None
    grads_sent = []
    for moment in range(micro_count + 1):
        stored = stored_all[micro_count - moment]
        late_cot = cotangent[max(micro_count - 1 - moment, 0), 0].astype(jnp.float32)
        grad_out = jnp.where(on_first, incoming.astype(jnp.float32), late_cot)
        grad_tokens, parts = layer_backward(grad_out, stored, weights)
        usable = jnp.where(on_first, moment >= 1, moment < micro_count)
        parts = tuple((jnp.where(usable, member, 0.0) for member in parts))
        sending = grad_tokens.astype(jnp.bfloat16)
        grads_sent.append(sending)
        if moment < micro_count:
            incoming = from_behind(sending, "section", -1)
        if summed is None:
            summed = parts
        else:
            summed = tuple((earlier + later_v for earlier, later_v in zip(summed, parts)))
    summed = (
        lax.psum_scatter(
            summed[0].astype(jnp.bfloat16), "shard", scatter_dimension=0, tiled=True
        ).astype(jnp.float32),
        lax.psum_scatter(
            summed[1].astype(jnp.bfloat16), "shard", scatter_dimension=0, tiled=True
        ).astype(jnp.float32),
        lax.psum_scatter(
            summed[2].astype(jnp.bfloat16), "shard", scatter_dimension=0, tiled=True
        ).astype(jnp.float32),
        lax.psum_scatter(
            summed[3].astype(jnp.bfloat16), "shard", scatter_dimension=0, tiled=True
        ).astype(jnp.float32),
        lax.psum_scatter(
            summed[4].astype(jnp.bfloat16), "shard", scatter_dimension=1, tiled=True
        ).astype(jnp.float32),
    )
    summed = jax.tree.map(lambda part: part.astype(jnp.float32), lax.psum(shortened(summed), "seq"))
    grad_in = jnp.stack(
        [
            jnp.where(
                on_first, grads_sent[micro_count - micro_m], grads_sent[micro_count - 1 - micro_m]
            )
            for micro_m in range(micro_count)
        ]
    )
    width_all = acts_in.shape[3]
    layer_out = layer_out.reshape(1, micro_count, 1, row_count, width_all)
    grad_in = grad_in.reshape(1, micro_count, 1, row_count, width_all)
    return (
        layer_out,
        grad_in,
        summed[0][None],
        summed[1][None],
        summed[2][None],
        summed[3][None],
        summed[4][None],
    )


def solution(mesh):
    placed = (
        P(None, "shard", "seq", None),
        P(None, "shard", "seq", None),
        P("section", "shard", None),
        P("section", "shard", None),
        P("section", "shard", None),
        P("section", "shard", None),
        P("section", None, "shard"),
        P(None, "shard", None),
    )
    return jax.shard_map(
        local,
        mesh=mesh,
        in_specs=placed,
        out_specs=(
            P("section", None, "shard", "seq", None),
            P("section", None, "shard", "seq", None),
            P("section", "shard", None),
            P("section", "shard", None),
            P("section", "shard", None),
            P("section", "shard", None),
            P("section", None, "shard"),
        ),
        check_vma=False,
    )
```

profile of v0, /device:TPU:1, one launch (start us, length us, event | category | flops | bytes accessed | tf_op | source)
XLA Modules:
  0.0 1002.9 jit_solution(1838740305421215929)
XLA Ops:
  10.1 21.0 %all-gather = bf16[1,4,1024]{1,0,2:T(2,128)(2,1)S(1)} all-gather(bf16[1,4,64]{1,0,2:T(2,128)(2,1)S(1)} %copy.145), channel_id=2, replica_groups=mesh['section'=2,'seq'=4,'shard'=16] {'shard'}, dimensions={2}, use_global_device_ids=true | all-gather | bytes 8704 | tf_op jit(solution)/shard_map/all_gather | solution.py:202
  32.0 21.7 %slice_reduce_fusion.1 = (f32[1024]{0:T(1024)S(1)}, f32[1024]{0:T(1024)S(1)}, f32[1024]{0:T(1024)S(1)}, f32[1024]{0:T(1024)S(1)}) fusion(f32[1,4,1024]{1,0,2:T(1,128)S(1)} %convert_element_type.341), kind=kLoop, calls=%fused_computation.158 | loop fusion | bytes 32768 | tf_op jit(solution)/shard_map/slice | solution.py:92
  53.7 21.3 %all-gather.10.cloned.1.call-done = bf16[1,1024,3072]{2,1,0:T(8,128)(2,1)} async-done(((bf16[1,64,3072]{2,1,0:T(8,128)(2,1)}), bf16[1,1024,3072]{2,1,0:T(8,128)(2,1)}) %all-gather.10.cloned.1.call-update) | async-done | bytes 6291472 | tf_op jit(solution)/shard_map/all_gather | solution.py:198
  84.6 7.2 all-to-all-done
  95.7 7.4 all_to_all.189
  103.4 17.5 %all-gather.12.cloned.1.call-done = bf16[1,1024,1024]{2,1,0:T(8,128)(2,1)} async-done(((bf16[1,64,1024]{2,1,0:T(8,128)(2,1)}), bf16[1,1024,1024]{2,1,0:T(8,128)(2,1)}) %all-gather.12.cloned.1.call-update) | async-done | bytes 2097168 | tf_op jit(solution)/shard_map/all_gather | solution.py:199
  124.1 69.9 %all-gather.14.cloned.1.call-done = bf16[1,1024,4096]{2,1,0:T(8,128)(2,1)} async-done(((bf16[1,64,4096]{2,1,0:T(8,128)(2,1)}), bf16[1,1024,4096]{2,1,0:T(8,128)(2,1)}) %all-gather.14.cloned.1.call-update) | async-done | bytes 8388624 | tf_op jit(solution)/shard_map/all_gather | solution.py:200
  199.0 67.3 %all-gather.16.cloned.1.call-done = bf16[1,4096,1024]{2,1,0:T(8,128)(2,1)} async-done(((bf16[1,256,1024]{2,1,0:T(8,128)(2,1)}), bf16[1,4096,1024]{2,1,0:T(8,128)(2,1)}) %all-gather.16.cloned.1.call-update) | async-done | bytes 8388624 | tf_op jit(solution)/shard_map/all_gather | solution.py:201
  266.3 6.9 add_convert_fusion.12
  283.6 8.1 all-to-all-done.2
  295.0 7.4 all_to_all.190
  310.5 6.5 fusion.8
  329.2 11.0 %all_to_all.191 = bf16[72,3,4,256]{3,0,1,2:T(8,128)(2,1)S(1)} all-to-all(bf16[72,3,4,256]{3,0,1,2:T(8,128)(2,1)S(1)} %copy.162), channel_id=1, replica_groups=mesh['section'=2,'seq'=4,'shard'=16] {'seq'}, dimensions={2} | all-to-all | bytes 884736 | tf_op jit(solution)/shard_map/all_to_all | solution.py:63
  352.7 8.0 all_to_all.192
  369.6 8.5 add_convert_fusion.6
  415.0 7.3 all-to-all-done.7
  439.4 8.6 add_convert_fusion.5
  509.3 8.5 add_convert_fusion.4
  534.6 7.7 fusion.157
  568.7 12.4 %add_convert_fusion.2 = bf16[1024,3072]{1,0:T(8,128)(2,1)} fusion(f32[1024,3072]{1,0:T(8,128)} %fusion.156, f32[1024,3072]{1,0:T(8,128)} %fusion.157, bf16[72,3072]{1,0:T(8,128)(2,1)S(1)} %reshape.633, pred[]{:T(512)S(6)} %eq.34, pred[]{:T(512)S(6)} %select_n.193, f32[1024]{0:T(1024)S(1)} %get-tuple-element.48, f32[72]{0:T(128)S(1)} %copy-done.115, ...), kind=kOutput, calls=%fused_computation.2 | convolution fusion | flops 469155840 | bytes 32053760 | tf_op jit(solution)/shard_map/dot_general | solution.py:34
  582.4 8.3 fusion.132
  590.7 8.3 fusion.139
  598.9 16.9 %add_convert_fusion = bf16[4096,1024]{1,0:T(8,128)(2,1)} fusion(f32[4096,1024]{1,0:T(8,128)} %fusion.139, f32[4096,1024]{1,0:T(8,128)} %fusion.132, pred[]{:T(512)S(6)} %eq.34, pred[]{:T(512)S(6)} %select_n.193, bf16[72,1024]{1,0:T(8,128)(2,1)S(1)} %copy-done.129, f32[1024]{0:T(1024)S(1)} %copy-done.90, bf16[2,1,72,1024]{3,2,1,0:T(8,128)(2,1)S(1)} %copy-done.48, ...), kind=kOutput, calls=%fused_computation | convolution fusion | flops 644489216 | bytes 43423232 | tf_op jit(solution)/shard_map/dot_general | solution.py:34
  616.9 8.4 fusion.154
  625.4 8.3 fusion.153
  633.6 10.0 add_convert_fusion.1
  650.3 33.5 %reduce-scatter.8.cloned.1.call-done = bf16[64,3072]{1,0:T(8,128)(2,1)} async-done(((bf16[1024,3072]{1,0:T(8,128)(2,1)}), bf16[64,3072]{1,0:T(8,128)(2,1)}) %reduce-scatter.8.cloned.1.call-update) | async-done | bytes 393232 | tf_op jit(solution)/shard_map/reduce_scatter | solution.py:252
  683.8 87.7 %reduce-scatter.14.cloned.1.call-done = bf16[256,1024]{1,0:T(8,128)(2,1)} async-done(((bf16[4096,1024]{1,0:T(8,128)(2,1)}), bf16[256,1024]{1,0:T(8,128)(2,1)}) %reduce-scatter.14.cloned.1.call-update) | async-done | bytes 524304 | tf_op jit(solution)/shard_map/reduce_scatter | solution.py:261
  771.5 89.0 %reduce-scatter.12.cloned.1.call-done = bf16[64,4096]{1,0:T(8,128)(2,1)} async-done(((bf16[1024,4096]{1,0:T(8,128)(2,1)}), bf16[64,4096]{1,0:T(8,128)(2,1)}) %reduce-scatter.12.cloned.1.call-update) | async-done | bytes 524304 | tf_op jit(solution)/shard_map/reduce_scatter | solution.py:258
  863.1 72.3 %reduce-scatter.16.cloned.1.call-done = bf16[64,4]{1,0:T(8,128)(2,1)} async-done(((bf16[1024,4]{1,0:T(8,128)(2,1)}), bf16[64,4]{1,0:T(8,128)(2,1)}) %reduce-scatter.16.cloned.1.call-update) | async-done | bytes 528
  936.2 8.6 psum.39
  945.5 44.6 %all-reduce.3.cloned.1.call-done = (bf16[1,64,3072]{2,1,0:T(8,128)(2,1)}, bf16[1,64,1024]{2,1,0:T(8,128)(2,1)}, bf16[1,64,4096]{2,1,0:T(8,128)(2,1)}, bf16[1,256,1024]{2,1,0:T(8,128)(2,1)}) async-done(((bf16[1,64,3072]{2,1,0:T(8,128)(2,1)}, bf16[1,64,1024]{2,1,0:T(8,128)(2,1)}, bf16[1,64,4096]{2,1,0:T(8,128)(2,1)}, bf16[1,256,1024]{2,1,0:T(8,128)(2,1)}), (bf16[1,64,3072]{2,1,0:T(8,128)(2,1)}, ...) | async-done | bytes 1572880 | tf_op jit(solution)/shard_map/psum | solution.py:268
  (518 shorter events, 256.2 us)
Async XLA Ops:
  7.2 67.9 %all-gather.10.cloned.1.call-start = ((), (), s32[]{:S(2)}) async-start(), calls=%async_computation.21 | async-start | bytes 6684672 | tf_op jit(solution)/shard_map/all_gather | solution.py:198
  7.9 113.0 %all-gather.12.cloned.1.call-start = ((), (), s32[]{:S(2)}) async-start(), calls=%async_computation.22 | async-start | bytes 2228224 | tf_op jit(solution)/shard_map/all_gather | solution.py:199
  8.7 185.3 %all-gather.14.cloned.1.call-start = ((), (), s32[]{:S(2)}) async-start(), calls=%async_computation.23 | async-start | bytes 8912896 | tf_op jit(solution)/shard_map/all_gather | solution.py:200
  9.4 256.9 %all-gather.16.cloned.1.call-start = ((), (), s32[]{:S(2)}) async-start(), calls=%async_computation.24 | async-start | bytes 8912896 | tf_op jit(solution)/shard_map/all_gather | solution.py:201
  31.8 47.3 %copy-start.101 = (f32[72]{0:T(128)}, f32[72]{0:T(128)S(1)}, u32[]{:S(2)}) copy-start(f32[72]{0:T(128)S(1)} %broadcast_multiply_fusion.5) | copy-start | bytes 868
  32.0 43.1 %copy-start.118 = (f32[72]{0:T(128)}, f32[72]{0:T(128)S(1)}, u32[]{:S(2)}) copy-start(f32[72]{0:T(128)S(1)} %multiply_reduce_fusion.25) | copy-start | bytes 868
  32.0 47.1 %copy-start.114 = (f32[72]{0:T(128)}, f32[72]{0:T(128)S(1)}, u32[]{:S(2)}) copy-start(f32[72]{0:T(128)S(1)} %fusion.143) | copy-start | bytes 868
  53.7 212.6 %copy-start.88 = (f32[1024]{0:T(1024)}, f32[1024]{0:T(1024)S(1)}, u32[]{:S(2)}) copy-start(f32[1024]{0:T(1024)S(1)} %get-tuple-element.47) | copy-start | bytes 12292
  80.3 11.6 %all-to-all-start = ((bf16[72,3,4,256]{3,0,1,2:T(8,128)(2,1)}), bf16[72,3,4,256]{3,0,1,2:T(8,128)(2,1)S(1)}, u32[]{:S(2)}, u32[]{:S(2)}) async-start(bf16[72,3,4,256]{3,0,1,2:T(8,128)(2,1)} %copy.146), calls=%async_computation | async-start | bytes 884736 | tf_op jit(solution)/shard_map/all_to_all | solution.py:63
  123.8 75.1 %copy-start.91 = (f32[72]{0:T(128)}, f32[72]{0:T(128)S(1)}, u32[]{:S(2)}) copy-start(f32[72]{0:T(128)S(1)} %broadcast_multiply_fusion.4) | copy-start | bytes 868
  124.0 74.9 %copy-start.120 = (f32[72]{0:T(128)}, f32[72]{0:T(128)S(1)}, u32[]{:S(2)}) copy-start(f32[72]{0:T(128)S(1)} %multiply_reduce_fusion.24) | copy-start | bytes 868
  124.1 74.9 %copy-start.103 = (f32[72]{0:T(128)}, f32[72]{0:T(128)S(1)}, u32[]{:S(2)}) copy-start(f32[72]{0:T(128)S(1)} %fusion.144) | copy-start | bytes 868
  199.0 74.2 %copy-start.50 = (f32[72,4096]{1,0:T(8,128)}, f32[72,4096]{1,0:T(8,128)S(1)}, u32[]{:S(2)}) copy-start(f32[72,4096]{1,0:T(8,128)S(1)} %fusion.22) | copy-start | bytes 3538948
  273.2 3.3 collective-permute-start
  279.3 12.4 %all-to-all-start.2 = ((bf16[72,3,4,256]{3,0,1,2:T(8,128)(2,1)}), bf16[72,3,4,256]{3,0,1,2:T(8,128)(2,1)S(1)}, u32[]{:S(2)}, u32[]{:S(2)}) async-start(bf16[72,3,4,256]{3,0,1,2:T(8,128)(2,1)} %copy.154), calls=%async_computation.2 | async-start | bytes 884736 | tf_op jit(solution)/shard_map/all_to_all | solution.py:63
  317.8 4.6 collective-permute-start.1
  383.2 9.1 all-to-all-start.6
  410.8 11.5 %all-to-all-start.7 = ((bf16[288,3,1,256]{3,1,2,0:T(4,128)(2,1)}), bf16[288,3,1,256]{3,1,2,0:T(4,128)(2,1)}, u32[]{:S(2)}, u32[]{:S(2)}) async-start(bf16[288,3,1,256]{3,1,2,0:T(4,128)(2,1)} %pad_maximum_fusion), calls=%async_computation.7 | async-start | bytes 1179648 | tf_op jit(solution)/shard_map/all_to_all | solution.py:180
  432.0 7.3 collective-permute-start.2
  452.7 9.0 all-to-all-start.8
  480.2 12.6 %all-to-all-start.9 = ((bf16[288,3,1,256]{3,1,2,0:T(4,128)(2,1)}), bf16[288,3,1,256]{3,1,2,0:T(4,128)(2,1)}, u32[]{:S(2)}, u32[]{:S(2)}) async-start(bf16[288,3,1,256]{3,1,2,0:T(4,128)(2,1)} %pad_maximum_fusion.1), calls=%async_computation.9 | async-start | bytes 1179648 | tf_op jit(solution)/shard_map/all_to_all | solution.py:180
  484.4 165.9 %reduce-scatter.10.cloned.1.call-start = ((), (), s32[]{:S(2)}) async-start(), calls=%async_computation.18 | async-start | bytes 2228224 | tf_op jit(solution)/shard_map/reduce_scatter | solution.py:255
  503.2 6.0 collective-permute-start.3
  531.3 11.1 %all-to-all-start.10 = ((bf16[72,4,256]{2,0,1:T(8,128)(2,1)}), bf16[72,4,256]{2,0,1:T(8,128)(2,1)S(1)}, u32[]{:S(2)}, u32[]{:S(2)}) async-start(bf16[72,4,256]{2,0,1:T(8,128)(2,1)} %bitcast.383), calls=%async_computation.10 | async-start | bytes 294912 | tf_op jit(solution)/shard_map/all_to_all | solution.py:151
  554.7 13.4 %all-to-all-start.11 = ((bf16[288,3,1,256]{3,1,2,0:T(4,128)(2,1)}), bf16[288,3,1,256]{3,1,2,0:T(4,128)(2,1)S(1)}, u32[]{:S(2)}, u32[]{:S(2)}) async-start(bf16[288,3,1,256]{3,1,2,0:T(4,128)(2,1)} %pad_maximum_fusion.2), calls=%async_computation.11 | async-start | bytes 1179648 | tf_op jit(solution)/shard_map/all_to_all | solution.py:180
  558.9 124.9 %reduce-scatter.8.cloned.1.call-start = ((), (), s32[]{:S(2)}) async-start(), calls=%async_computation.17 | async-start | bytes 6684672 | tf_op jit(solution)/shard_map/reduce_scatter | solution.py:252
  581.1 190.4 %reduce-scatter.14.cloned.1.call-start = ((), (), s32[]{:S(2)}) async-start(), calls=%async_computation.20 | async-start | bytes 8912896 | tf_op jit(solution)/shard_map/reduce_scatter | solution.py:261
  615.9 244.6 %reduce-scatter.12.cloned.1.call-start = ((), (), s32[]{:S(2)}) async-start(), calls=%async_computation.19 | async-start | bytes 8912896 | tf_op jit(solution)/shard_map/reduce_scatter | solution.py:258
  643.7 291.8 %reduce-scatter.16.cloned.1.call-start = ((), (), s32[]{:S(2)}) async-start(), calls=%async_computation.25 | async-start | bytes 278528
  649.2 211.3 %copy-start.68 = (bf16[72,1024]{1,0:T(8,128)(2,1)S(1)}, bf16[72,1024]{1,0:T(8,128)(2,1)}, u32[]{:S(2)}) copy-start(bf16[72,1024]{1,0:T(8,128)(2,1)} %copy-done.67) | copy-start | bytes 442372
  649.2 211.3 %copy-start.77 = (f32[72,1024]{1,0:T(8,128)S(1)}, f32[72,1024]{1,0:T(8,128)}, u32[]{:S(2)}) copy-start(f32[72,1024]{1,0:T(8,128)} %get-tuple-element.116) | copy-start | bytes 884740
  650.2 339.8 %all-reduce.3.cloned.1.call-start = ((), (), s32[]{:S(2)}) async-start(), calls=%async_computation.26 | async-start | bytes 3145728 | tf_op jit(solution)/shard_map/psum | solution.py:268
  (133 other events, 667.8 us)
Sparse Core Ops, SparseCore 0:
  10.1 64.8 all-gather.9
  77.2 43.6 all-gather.11
  123.0 70.8 all-gather.13
  195.9 70.3 all-gather.15
  528.8 69.9 reduce-scatter.9
  602.5 81.2 reduce-scatter.7
  687.6 83.8 reduce-scatter.13
  775.3 85.1 reduce-scatter.11
  864.6 70.8 reduce-scatter.15
  937.9 52.0 all-reduce.2
where the time goes:
time: 1010 us; the launch traced here: 1000 us
  waiting for transfers between devices  551 us (55%)
  matrix products  214 us (21%)
  local copies, waits for them, and re-layouts  83.4 us (8%)
  blocking collectives  63.4 us (6%)
  starting transfers between devices  47.5 us (5%)
  other arithmetic  26.7 us (3%)
  between operations  16.6 us (2%)
    dot_general x12, matrix products, inner_rows(): lax.dot_general(left_mat, right_mat, (((0,), (0,)), ((), ())), preferred_...  93.5 us
    reduce_scatter x1, waiting for transfers between devices, local(): lax.psum_scatter(summed[2].astype(jnp.bfloat16), 'shard', scatter_dimensi...  89 us
    reduce_scatter x1, waiting for transfers between devices, local(): lax.psum_scatter(summed[3].astype(jnp.bfloat16), 'shard', scatter_dimensi...  87.7 us
    unnamed x11, waiting for transfers between devices  75 us
    all_gather x1, waiting for transfers between devices, local(): lax.all_gather(own_rows[2], 'shard', axis=0, tiled=True)  69.9 us
    all_gather x1, waiting for transfers between devices, local(): lax.all_gather(own_rows[3], 'shard', axis=0, tiled=True)  67.3 us
    dot_general x12, matrix products, inner_cols(): lax.dot_general(left_mat, right_mat, (((1,), (1,)), ((), ())), preferred_...  53.4 us
    psum x1, waiting for transfers between devices, local(): lax.psum(shortened(summed), 'seq')  44.6 us
  transfers between devices with their start and end apart: 22, of which 19 were waited for; matrix products, arithmetic and copies ran while one was open for 15% of the time, Pallas kernels for 0%

commit v1 on v0

v1 whole, which is shorter than its diff:
```python
import jax
import jax.numpy as jnp
from jax import lax
from jax.sharding import PartitionSpec as P

HEAD_DIM = 64
EPS = 1e-06
NEG = -1e30
BF = jnp.bfloat16
F32 = jnp.float32


def dot(a, b):
    return jnp.dot(a, b, preferred_element_type=F32)


def dot_rows(a, b):
    return lax.dot_general(a, b, (((0,), (0,)), ((), ())), preferred_element_type=F32)


def dot_cols(a, b):
    return lax.dot_general(a, b, (((1,), (1,)), ((), ())), preferred_element_type=F32)


def normalise(values):
    centre = values - jnp.mean(values, axis=-1, keepdims=True)
    scale = lax.rsqrt(jnp.mean(centre * centre, axis=-1, keepdims=True) + EPS)
    return centre * scale, scale


def norm_back(grad, values, gain):
    xhat, scale = normalise(values)
    f = grad * gain
    dv = scale * (
        f
        - jnp.mean(f, axis=-1, keepdims=True)
        - xhat * jnp.mean(f * xhat, axis=-1, keepdims=True)
    )
    return dv, jnp.sum(grad * xhat, axis=0)


def gelu_parts(u):
    cdf = 0.5 * (1.0 + lax.erf(u * 0.7071067811865476))
    slope = cdf + u * jnp.exp(-0.5 * u * u) * 0.3989422804014327
    return u * cdf, slope


def gather_tokens(rows):
    return lax.all_gather(rows, "seq", axis=0, tiled=True)


def scatter_tokens(partial):
    return lax.psum_scatter(partial.astype(BF), "seq", scatter_dimension=0, tiled=True).astype(F32)


def split_heads(packed):
    n = packed.shape[0]
    g = packed.reshape(n, 2, 3, 2, HEAD_DIM)
    return [g[:, :, t].reshape(n, 4, HEAD_DIM) for t in range(3)]


def attn_forward(x, ids, w, vec):
    xhat, _ = normalise(x)
    h1 = gather_tokens((xhat * vec[0]).astype(BF))
    packed = dot(h1, w["qkv"]).astype(BF)
    q, k, v = split_heads(packed)
    s = jnp.einsum("qhd,khd->hqk", q, k, preferred_element_type=F32) * HEAD_DIM**-0.5
    s = jnp.where((ids[:, None] == ids[None, :])[None], s, NEG)
    top = jnp.max(s, axis=-1, keepdims=True)
    e = jnp.exp(s - top)
    total = jnp.sum(e, axis=-1, keepdims=True)
    o = jnp.einsum(
        "hqk,khd->qhd", (e / total).astype(BF), v, preferred_element_type=F32
    ).astype(BF)
    o = o.reshape(o.shape[0], 4 * HEAD_DIM)
    joined = lax.all_to_all(o, "seq", split_axis=0, concat_axis=1, tiled=True)
    a = dot(joined, w["out"])
    y1 = x + vec[1] * a
    return y1, (x, h1, q, k, v, top + jnp.log(total), joined, a)


def mlp_forward(y1, w, vec):
    yhat, _ = normalise(y1)
    h2 = gather_tokens((yhat * vec[2]).astype(BF))
    u = dot(h2, w["up"])
    g, slope = gelu_parts(u)
    g = g.astype(BF)
    m = scatter_tokens(dot(g, w["down"]))
    return y1 + vec[3] * m, (y1, h2, slope.astype(BF), g, m)


def mlp_backward(dz, kept, w, vec):
    y1, h2, slope, g, m = kept
    dm = gather_tokens((vec[3] * dz).astype(BF))
    dc2 = jnp.sum(dz * m, axis=0)
    d_down = dot_rows(g, dm)
    du = (slope * dot_cols(dm, w["down"])).astype(BF)
    d_up = dot_rows(h2, du)
    dh2 = scatter_tokens(dot_cols(du, w["up"]))
    dn, dg2 = norm_back(dh2, y1, vec[2])
    return dz + dn, d_up, d_down, dg2, dc2


def attn_backward(dy1, ids, kept, w, vec):
    x, h1, q, k, v, logsum, joined, a = kept
    da = (vec[1] * dy1).astype(BF)
    dc1 = jnp.sum(dy1 * a, axis=0)
    d_out = dot_rows(joined, da)
    do = dot_cols(da, w["out"]).astype(BF)
    do = lax.all_to_all(do, "seq", split_axis=1, concat_axis=0, tiled=True)
    n = do.shape[0]
    do = do.reshape(n, 4, HEAD_DIM)
    s = jnp.einsum("qhd,khd->hqk", q, k, preferred_element_type=F32) * HEAD_DIM**-0.5
    s = jnp.where((ids[:, None] == ids[None, :])[None], s, NEG)
    p = jnp.exp(s - logsum)
    dp = jnp.einsum("qhd,khd->hqk", do, v, preferred_element_type=F32)
    dv = jnp.einsum("hqk,qhd->khd", p.astype(BF), do, preferred_element_type=F32)
    ds = (p * (dp - jnp.sum(p * dp, axis=-1, keepdims=True))).astype(BF)
    dq = jnp.einsum("hqk,khd->qhd", ds, k, preferred_element_type=F32) * HEAD_DIM**-0.5
    dk = jnp.einsum("hqk,qhd->khd", ds, q, preferred_element_type=F32) * HEAD_DIM**-0.5
    grads = jnp.stack([t.reshape(n, 2, 128) for t in (dq, dk, dv)], axis=2).astype(BF)
    grads = grads.reshape(n, 768)
    d_qkv = dot_rows(h1, grads)
    dh1 = scatter_tokens(dot_cols(grads, w["qkv"]))
    dn, dg1 = norm_back(dh1, x, vec[0])
    return dy1 + dn, d_qkv, d_out, dg1, dc1


def gather_weights(qkv, out, up, down, vec, z):
    parts = (
        lax.dynamic_index_in_dim(qkv.reshape(64, 3, 4, 2, 128), z, 2, False).transpose(2, 0, 1, 3),
        out.reshape(64, 2, 512).transpose(1, 0, 2),
        lax.dynamic_index_in_dim(up.reshape(64, 16, 4, 2, 32), z, 2, False).transpose(2, 0, 1, 3),
        lax.dynamic_index_in_dim(down.reshape(4, 2, 32, 1024), z, 0, False),
    )
    shapes = ((64, 384), (64, 512), (64, 512), (32, 1024))
    parts = [p.reshape((2,) + s) for p, s in zip(parts, shapes)]
    parts = [lax.all_to_all(p, "section", split_axis=0, concat_axis=0, tiled=True) for p in parts]
    layers = []
    vecs = lax.all_gather(vec, ("section", "shard"), axis=0)
    vecs = vecs.reshape(2, 16, 4, 64).transpose(0, 2, 1, 3).reshape(2, 4, 1024).astype(F32)
    for layer in range(2):
        w = {}
        for name, p, axis in zip(("qkv", "out", "up", "down"), parts, (1, 1, 1, 0)):
            whole = lax.all_gather(p[layer], "shard", axis=0, tiled=True)
            w[name] = lax.all_gather(whole, "section", axis=axis, tiled=True)
        layers.append(w)
    return layers, vecs


def reduce_pieces(pieces, c):
    flats = []
    for p, axis in zip(pieces, (1, 1, 1, 0)):
        half = lax.psum_scatter(p.astype(BF), "section", scatter_dimension=axis, tiled=True)
        own = lax.psum_scatter(half, "shard", scatter_dimension=0, tiled=True)
        flats.append(own.reshape(-1))
    return flats


def local(acts_in, cotangent, qkv_weight, out_weight, up_weight, down_weight, vectors, image_ids):
    c = lax.axis_index("section")
    z = lax.axis_index("seq")
    layers, vecs = gather_weights(
        qkv_weight[0], out_weight[0], up_weight[0], down_weight[0], vectors[0], z
    )
    x = lax.dynamic_index_in_dim(acts_in, c, 0, False)[0].astype(F32)
    dz = lax.dynamic_index_in_dim(cotangent, c, 0, False)[0].astype(F32)
    ids = lax.dynamic_index_in_dim(image_ids, c, 0, False)[0]
    kept = []
    outs = []
    for layer in range(2):
        w, vec = layers[layer], vecs[layer]
        y1, kept_a = attn_forward(x, ids, w, vec)
        y2, kept_m = mlp_forward(y1, w, vec)
        kept.append((kept_a, kept_m))
        sent = y2.astype(BF)
        outs.append(sent)
        x = sent.astype(F32)
    grads = [None, None]
    flats = [None, None]
    vparts = [None, None]
    for layer in (1, 0):
        w, vec = layers[layer], vecs[layer]
        kept_a, kept_m = kept[layer]
        dy1, d_up, d_down, dg2, dc2 = mlp_backward(dz, kept_m, w, vec)
        dx, d_qkv, d_out, dg1, dc1 = attn_backward(dy1, ids, kept_a, w, vec)
        grads[layer] = dx.astype(BF)
        dz = grads[layer].astype(F32)
        flats[layer] = reduce_pieces((d_qkv, d_out, d_up, d_down), c)
        vparts[layer] = jnp.stack([dg1, dc1, dg2, dc2])
    vown = lax.psum_scatter(
        jnp.stack(vparts).astype(BF), "shard", scatter_dimension=2, tiled=True
    )
    both = jnp.stack(
        [jnp.concatenate(flats[l] + [vown[l].reshape(-1)]) for l in range(2)]
    )
    mine = lax.all_to_all(both, "section", split_axis=0, concat_axis=0, tiled=True)
    every = lax.all_gather(mine, "seq", axis=0)
    every = every.astype(F32)
    sizes = (64 * 384, 64 * 512, 64 * 512, 32 * 1024, 256)
    at = 0
    cut = []
    for s in sizes:
        cut.append(every[:, :, at : at + s])
        at += s
    g_qkv = cut[0].reshape(4, 2, 64, 3, 128).transpose(2, 3, 0, 1, 4).reshape(64, 3072)
    g_out = jnp.sum(cut[1].reshape(4, 2, 64, 512), axis=0).transpose(1, 0, 2).reshape(64, 1024)
    g_up = cut[2].reshape(4, 2, 64, 16, 32).transpose(2, 3, 0, 1, 4).reshape(64, 4096)
    g_down = cut[3].reshape(256, 1024)
    g_vec = jnp.sum(cut[4].reshape(8, 4, 64), axis=0)
    pair = jnp.stack(outs + grads)[:, None]
    pair = pair.reshape(2, 2, 72, 1024).transpose(1, 0, 2, 3)
    pair = lax.all_to_all(pair, "section", split_axis=0, concat_axis=0, tiled=True)
    layer_out = pair[:, 0][None, :, None]
    grad_in = pair[:, 1][None, :, None]
    return (layer_out, grad_in, g_qkv[None], g_out[None], g_up[None], g_down[None], g_vec[None])


def solution(mesh):
    placed = (
        P(None, "shard", "seq", None),
        P(None, "shard", "seq", None),
        P("section", "shard", None),
        P("section", "shard", None),
        P("section", "shard", None),
        P("section", "shard", None),
        P("section", None, "shard"),
        P(None, "shard", None),
    )
    return jax.shard_map(
        local,
        mesh=mesh,
        in_specs=placed,
        out_specs=(
            P("section", None, "shard", "seq", None),
            P("section", None, "shard", "seq", None),
            P("section", "shard", None),
            P("section", "shard", None),
            P("section", "shard", None),
            P("section", "shard", None),
            P("section", None, "shard"),
        ),
        check_vma=False,
    )
```

time: 1010 us -> 1550 us (1.53)
  waiting for transfers between devices: 551 us -> 1110 us
  blocking collectives: 63.4 us -> 206 us
  matrix products: 214 us -> 71.9 us
  starting transfers between devices: 47.5 us -> 16.7 us
    reduce_scatter x4 -> x20, waiting for transfers between devices: 210 us -> 799 us  [the longest x8 598 us: reduce_pieces(): own = lax.psum_scatter(half, 'shard', scatter_dimension=0, tiled=True)]
    all_gather x1 -> x9, blocking collectives: 21 us -> 179 us  [the longest x6 71.5 us: gather_tokens(): return lax.all_gather(rows, 'seq', axis=0, tiled=True)]
    dot_general x54 -> x36, matrix products: 214 us -> 71.9 us  [the longest x8 24.5 us: dot(): return jnp.dot(a, b, preferred_element_type=F32)]
    psum x1 -> x0, waiting for transfers between devices: 44.6 us -> none  [local(): lax.psum(shortened(summed), 'seq')]
    unnamed x11 -> x41, waiting for transfers between devices: 75 us -> 104 us
    all_to_all x8 -> x4, waiting for transfers between devices: 39.8 us -> 13.3 us  [the longest x2 9 us: attn_backward(): do = lax.all_to_all(do, 'seq', split_axis=1, concat_axis=0, tiled=True)]
    slice x14 -> x10, local copies, waits for them, and re-layouts: 28.1 us -> 2.8 us  [the longest x4 1.99 us: gather_weights(): whole = lax.all_gather(p[layer], 'shard', axis=0, tiled=True)]
    all_gather x4 -> x15, waiting for transfers between devices: 176 us -> 196 us  [the longest x6 153 us: gather_weights(): whole = lax.all_gather(p[layer], 'shard', axis=0, tiled=True)]
  transfers between devices with their start and end apart: 22 -> 42, of which waited for: 19 -> 32; matrix products, arithmetic and copies ran while one was open for 15% -> 5% of each run, Pallas kernels for 0% -> 0%
where the time goes in v1:
time: 1550 us; the launch traced here: 1540 us
  waiting for transfers between devices  1110 us (72%)
  blocking collectives  206 us (13%)
  local copies, waits for them, and re-layouts  75.3 us (5%)
  matrix products  71.9 us (5%)
  other arithmetic  40.9 us (3%)
  starting transfers between devices  16.7 us (1%)
  between operations  16.4 us (1%)
    reduce_scatter x8, waiting for transfers between devices, reduce_pieces(): own = lax.psum_scatter(half, 'shard', scatter_dimension=0, tiled=True)  598 us
    all_gather x6, waiting for transfers between devices, gather_weights(): whole = lax.all_gather(p[layer], 'shard', axis=0, tiled=True)  153 us
    reduce_scatter x6, waiting for transfers between devices, scatter_tokens(): lax.psum_scatter(partial.astype(BF), 'seq', scatter_dimension=0, tiled=True)  113 us
    unnamed x41, waiting for transfers between devices  104 us
    reduce_scatter x6, waiting for transfers between devices, reduce_pieces(): lax.psum_scatter(p.astype(BF), 'section', scatter_dimension=axis, tiled=T...  88.1 us
    all_gather x6, blocking collectives, gather_tokens(): return lax.all_gather(rows, 'seq', axis=0, tiled=True)  71.5 us
    all_gather x1, blocking collectives, gather_weights(): vecs = lax.all_gather(vec, ('section', 'shard'), axis=0)  65.5 us
    all_gather x2, blocking collectives, gather_weights(): whole = lax.all_gather(p[layer], 'shard', axis=0, tiled=True)  41.9 us
  transfers between devices with their start and end apart: 42, of which 32 were waited for; matrix products, arithmetic and copies ran while one was open for 5% of the time, Pallas kernels for 0%

profile of v1, /device:TPU:1, one launch (start us, length us, event | category | flops | bytes accessed | tf_op | source)
XLA Modules:
  0.0 1539.0 jit_solution(4482854235451070223)
XLA Ops:
  29.2 22.2 %all-gather = bf16[1,1024,384]{2,1,0:T(8,128)(2,1)} all-gather(bf16[1,64,384]{2,1,0:T(8,128)(2,1)S(1)} %get-tuple-element.79), channel_id=2, replica_groups=mesh['section'=2,'seq'=4,'shard'=16] {'shard'}, dimensions={1}, use_global_device_ids=true | all-gather | bytes 835584 | tf_op jit(solution)/shard_map/all_gather | solution.py:145
  58.9 43.4 %all-gather.39.cloned.1.call-done = bf16[1,1024,512]{2,1,0:T(8,128)(2,1)} async-done(((bf16[1,64,512]{2,1,0:T(8,128)(2,1)}), bf16[1,1024,512]{2,1,0:T(8,128)(2,1)}) %all-gather.39.cloned.1.call-update) | async-done | bytes 1048592 | tf_op jit(solution)/shard_map/all_gather | solution.py:145
  102.3 44.5 %all-gather.43.cloned.1.call-done = bf16[1,512,1024]{2,1,0:T(8,128)(2,1)} async-done(((bf16[1,32,1024]{2,1,0:T(8,128)(2,1)}), bf16[1,512,1024]{2,1,0:T(8,128)(2,1)}) %all-gather.43.cloned.1.call-update) | async-done | bytes 1048592 | tf_op jit(solution)/shard_map/all_gather | solution.py:145
  148.7 65.5 %all_gather.75 = bf16[32,4,64]{2,1,0:T(4,128)(2,1)S(1)} all-gather(bf16[1,4,64]{2,1,0:T(4,128)(2,1)S(1)} %copy-done.85), channel_id=1, replica_groups=mesh['section'=2,'seq'=4,'shard'=16] {'section','shard'}, dimensions={0}, use_global_device_ids=true | all-gather | bytes 16896 | tf_op jit(solution)/shard_map/all_gather | solution.py:140
  215.2 12.2 all_gather.76
  264.7 19.7 %all-gather.8 = bf16[1,1024,384]{2,1,0:T(8,128)(2,1)} all-gather(bf16[1,64,384]{2,1,0:T(8,128)(2,1)S(1)} %get-tuple-element.78), channel_id=10, replica_groups=mesh['section'=2,'seq'=4,'shard'=16] {'shard'}, dimensions={1}, use_global_device_ids=true | all-gather | bytes 835584 | tf_op jit(solution)/shard_map/all_gather | solution.py:145
  285.2 14.2 all-gather.53.cloned.1.call-done
  300.2 43.1 %all-gather.57.cloned.1.call-done = bf16[1,512,1024]{2,1,0:T(8,128)(2,1)} async-done(((bf16[1,32,1024]{2,1,0:T(8,128)(2,1)}), bf16[1,512,1024]{2,1,0:T(8,128)(2,1)}) %all-gather.57.cloned.1.call-update) | async-done | bytes 1048592 | tf_op jit(solution)/shard_map/all_gather | solution.py:145
  343.4 23.8 %reduce-scatter.30.cloned.1.call-done = bf16[72,1024]{1,0:T(8,128)(2,1)} async-done(((bf16[288,1024]{1,0:T(8,128)(2,1)}), bf16[72,1024]{1,0:T(8,128)(2,1)}) %reduce-scatter.30.cloned.1.call-update) | async-done | bytes 147472 | tf_op jit(solution)/shard_map/reduce_scatter | solution.py:53
  397.2 14.5 all_gather.96
  441.0 22.5 %reduce-scatter.34.cloned.1.call-done = bf16[72,1024]{1,0:T(8,128)(2,1)} async-done(((bf16[288,1024]{1,0:T(8,128)(2,1)}), bf16[72,1024]{1,0:T(8,128)(2,1)}) %reduce-scatter.34.cloned.1.call-update) | async-done | bytes 147472 | tf_op jit(solution)/shard_map/reduce_scatter | solution.py:53
  465.8 21.3 %reduce-scatter.32.cloned.1.call-done = bf16[72,1024]{1,0:T(8,128)(2,1)} async-done(((bf16[288,1024]{1,0:T(8,128)(2,1)}), bf16[72,1024]{1,0:T(8,128)(2,1)}) %reduce-scatter.32.cloned.1.call-update) | async-done | bytes 147472 | tf_op jit(solution)/shard_map/reduce_scatter | solution.py:53
  515.9 22.2 %reduce-scatter.36.cloned.1.call-done = bf16[72,1024]{1,0:T(8,128)(2,1)} async-done(((bf16[288,1024]{1,0:T(8,128)(2,1)}), bf16[72,1024]{1,0:T(8,128)(2,1)}) %reduce-scatter.36.cloned.1.call-update) | async-done | bytes 147472 | tf_op jit(solution)/shard_map/reduce_scatter | solution.py:53
  557.8 23.3 %reduce-scatter.38.cloned.1.call-done = bf16[72,1024]{1,0:T(8,128)(2,1)} async-done(((bf16[288,1024]{1,0:T(8,128)(2,1)}), bf16[72,1024]{1,0:T(8,128)(2,1)}) %reduce-scatter.38.cloned.1.call-update) | async-done | bytes 147472 | tf_op jit(solution)/shard_map/reduce_scatter | solution.py:53
  646.8 11.6 reduce-scatter.62.cloned.1.call-done
  658.5 15.9 %reduce-scatter.66.cloned.1.call-done = bf16[512,1024]{1,0:T(8,128)(2,1)} async-done(((bf16[1024,1024]{1,0:T(8,128)(2,1)}), bf16[512,1024]{1,0:T(8,128)(2,1)}) %reduce-scatter.66.cloned.1.call-update) | async-done | bytes 1048592 | tf_op jit(solution)/shard_map/reduce_scatter | solution.py:154
  674.5 16.0 %reduce-scatter.58.cloned.1.call-done = bf16[1024,512]{1,0:T(8,128)(2,1)} async-done(((bf16[1024,1024]{1,0:T(8,128)(2,1)}), bf16[1024,512]{1,0:T(8,128)(2,1)}) %reduce-scatter.58.cloned.1.call-update) | async-done | bytes 1048592 | tf_op jit(solution)/shard_map/reduce_scatter | solution.py:154
  690.5 15.3 reduce-scatter.70.cloned.1.call-done
  708.2 13.7 reduce-scatter.48.cloned.1.call-done
  722.0 15.8 %reduce-scatter.52.cloned.1.call-done = bf16[512,1024]{1,0:T(8,128)(2,1)} async-done(((bf16[1024,1024]{1,0:T(8,128)(2,1)}), bf16[512,1024]{1,0:T(8,128)(2,1)}) %reduce-scatter.52.cloned.1.call-update) | async-done | bytes 1048592 | tf_op jit(solution)/shard_map/reduce_scatter | solution.py:154
  737.9 75.1 %reduce-scatter.72.cloned.1.call-done = bf16[64,8]{1,0:T(8,128)(2,1)} async-done(((bf16[1024,8]{1,0:T(8,128)(2,1)}), bf16[64,8]{1,0:T(8,128)(2,1)}) %reduce-scatter.72.cloned.1.call-update) | async-done | bytes 1040
  814.2 74.6 %reduce-scatter.56.cloned.1.call-done = bf16[64,384]{1,0:T(8,128)(2,1)} async-done(((bf16[1024,384]{1,0:T(8,128)(2,1)}), bf16[64,384]{1,0:T(8,128)(2,1)}) %reduce-scatter.56.cloned.1.call-update) | async-done | bytes 49168 | tf_op jit(solution)/shard_map/reduce_scatter | solution.py:155
  889.6 15.1 reduce-scatter.44.cloned.1.call-done
  904.8 75.6 %reduce-scatter.64.cloned.1.call-done = bf16[64,512]{1,0:T(8,128)(2,1)} async-done(((bf16[1024,512]{1,0:T(8,128)(2,1)}), bf16[64,512]{1,0:T(8,128)(2,1)}) %reduce-scatter.64.cloned.1.call-update) | async-done | bytes 65552 | tf_op jit(solution)/shard_map/reduce_scatter | solution.py:155
  981.3 74.7 %reduce-scatter.68.cloned.1.call-done = bf16[32,1024]{1,0:T(8,128)(2,1)} async-done(((bf16[512,1024]{1,0:T(8,128)(2,1)}), bf16[32,1024]{1,0:T(8,128)(2,1)}) %reduce-scatter.68.cloned.1.call-update) | async-done | bytes 65552 | tf_op jit(solution)/shard_map/reduce_scatter | solution.py:155
  1056.8 74.7 %reduce-scatter.60.cloned.1.call-done = bf16[64,512]{1,0:T(8,128)(2,1)} async-done(((bf16[1024,512]{1,0:T(8,128)(2,1)}), bf16[64,512]{1,0:T(8,128)(2,1)}) %reduce-scatter.60.cloned.1.call-update) | async-done | bytes 65552 | tf_op jit(solution)/shard_map/reduce_scatter | solution.py:155
  1132.7 74.5 %reduce-scatter.42.cloned.1.call-done = bf16[64,384]{1,0:T(8,128)(2,1)} async-done(((bf16[1024,384]{1,0:T(8,128)(2,1)}), bf16[64,384]{1,0:T(8,128)(2,1)}) %reduce-scatter.42.cloned.1.call-update) | async-done | bytes 49168 | tf_op jit(solution)/shard_map/reduce_scatter | solution.py:155
  1208.1 74.6 %reduce-scatter.50.cloned.1.call-done = bf16[64,512]{1,0:T(8,128)(2,1)} async-done(((bf16[1024,512]{1,0:T(8,128)(2,1)}), bf16[64,512]{1,0:T(8,128)(2,1)}) %reduce-scatter.50.cloned.1.call-update) | async-done | bytes 65552 | tf_op jit(solution)/shard_map/reduce_scatter | solution.py:155
  1283.6 74.7 %reduce-scatter.54.cloned.1.call-done = bf16[32,1024]{1,0:T(8,128)(2,1)} async-done(((bf16[512,1024]{1,0:T(8,128)(2,1)}), bf16[32,1024]{1,0:T(8,128)(2,1)}) %reduce-scatter.54.cloned.1.call-update) | async-done | bytes 65552 | tf_op jit(solution)/shard_map/reduce_scatter | solution.py:155
  1359.1 74.4 %reduce-scatter.46.cloned.1.call-done = bf16[64,512]{1,0:T(8,128)(2,1)} async-done(((bf16[1024,512]{1,0:T(8,128)(2,1)}), bf16[64,512]{1,0:T(8,128)(2,1)}) %reduce-scatter.46.cloned.1.call-update) | async-done | bytes 65552 | tf_op jit(solution)/shard_map/reduce_scatter | solution.py:155
  1453.6 40.2 %all-gather.61.cloned.1.call-done = bf16[8,1,123136]{2,1,0:T(2,128)(2,1)} async-done(((bf16[2,1,123136]{2,1,0:T(2,128)(2,1)}), bf16[8,1,123136]{2,1,0:T(2,128)(2,1)}) %all-gather.61.cloned.1.call-update) | async-done | bytes 1970192 | tf_op jit(solution)/shard_map/all_gather | solution.py:198
  1493.9 14.3 convert_reduce_fusion
  (482 shorter events, 299.3 us)
Async XLA Ops:
  13.9 88.4 %all-gather.39.cloned.1.call-start = ((), (), s32[]{:S(2)}) async-start(), calls=%async_computation.56 | async-start | bytes 1114112 | tf_op jit(solution)/shard_map/all_gather | solution.py:145
  20.2 126.7 %all-gather.43.cloned.1.call-start = ((), (), s32[]{:S(2)}) async-start(), calls=%async_computation.58 | async-start | bytes 1114112 | tf_op jit(solution)/shard_map/all_gather | solution.py:145
  24.8 202.7 %all-gather.33.cloned.1.call-start = ((), (), s32[]{:S(2)}) async-start(), calls=%async_computation.53 | async-start | bytes 2359296 | tf_op jit(solution)/shard_map/all_gather | solution.py:146
  51.4 191.2 %all-gather.37.cloned.1.call-start = ((), (), s32[]{:S(2)}) async-start(), calls=%async_computation.55 | async-start | bytes 3145728 | tf_op jit(solution)/shard_map/all_gather | solution.py:146
  58.8 198.6 %all-gather.41.cloned.1.call-start = ((), (), s32[]{:S(2)}) async-start(), calls=%async_computation.57 | async-start | bytes 3145728 | tf_op jit(solution)/shard_map/all_gather | solution.py:146
  102.3 159.0 %all-gather.45.cloned.1.call-start = ((), (), s32[]{:S(2)}) async-start(), calls=%async_computation.59 | async-start | bytes 3145728 | tf_op jit(solution)/shard_map/all_gather | solution.py:146
  146.9 137.6 %all-gather.49.cloned.1.call-start = ((), (), s32[]{:S(2)}) async-start(), calls=%async_computation.61 | async-start | bytes 1114112 | tf_op jit(solution)/shard_map/all_gather | solution.py:145
  147.6 151.8 %all-gather.53.cloned.1.call-start = ((), (), s32[]{:S(2)}) async-start(), calls=%async_computation.63 | async-start | bytes 1114112 | tf_op jit(solution)/shard_map/all_gather | solution.py:145
  237.6 105.7 %all-gather.57.cloned.1.call-start = ((), (), s32[]{:S(2)}) async-start(), calls=%async_computation.65 | async-start | bytes 1114112 | tf_op jit(solution)/shard_map/all_gather | solution.py:145
  238.2 129.0 %reduce-scatter.30.cloned.1.call-start = ((), (), s32[]{:S(2)}) async-start(), calls=%async_computation.33 | async-start | bytes 737280 | tf_op jit(solution)/shard_map/reduce_scatter | solution.py:53
  264.7 118.1 %all-gather.47.cloned.1.call-start = ((), (), s32[]{:S(2)}) async-start(), calls=%async_computation.60 | async-start | bytes 2359296 | tf_op jit(solution)/shard_map/all_gather | solution.py:146
  284.4 128.8 %all-gather.51.cloned.1.call-start = ((), (), s32[]{:S(2)}) async-start(), calls=%async_computation.62 | async-start | bytes 3145728 | tf_op jit(solution)/shard_map/all_gather | solution.py:146
  285.2 142.6 %all-gather.55.cloned.1.call-start = ((), (), s32[]{:S(2)}) async-start(), calls=%async_computation.64 | async-start | bytes 3145728 | tf_op jit(solution)/shard_map/all_gather | solution.py:146
  299.5 132.3 %all-gather.59.cloned.1.call-start = ((), (), s32[]{:S(2)}) async-start(), calls=%async_computation.66 | async-start | bytes 3145728 | tf_op jit(solution)/shard_map/all_gather | solution.py:146
  397.2 66.3 %reduce-scatter.34.cloned.1.call-start = ((), (), s32[]{:S(2)}) async-start(), calls=%async_computation.35 | async-start | bytes 737280 | tf_op jit(solution)/shard_map/reduce_scatter | solution.py:53
  515.8 65.2 %reduce-scatter.38.cloned.1.call-start = ((), (), s32[]{:S(2)}) async-start(), calls=%async_computation.37 | async-start | bytes 737280 | tf_op jit(solution)/shard_map/reduce_scatter | solution.py:53
  610.6 63.8 %reduce-scatter.66.cloned.1.call-start = ((), (), s32[]{:S(2)}) async-start(), calls=%async_computation.51 | async-start | bytes 3145728 | tf_op jit(solution)/shard_map/reduce_scatter | solution.py:154
  614.5 76.0 %reduce-scatter.58.cloned.1.call-start = ((), (), s32[]{:S(2)}) async-start(), calls=%async_computation.47 | async-start | bytes 3145728 | tf_op jit(solution)/shard_map/reduce_scatter | solution.py:154
  617.5 88.4 %reduce-scatter.70.cloned.1.call-start = ((), (), s32[]{:S(2)}) async-start(), calls=%async_computation.68 | async-start | bytes 2359296
  620.5 101.5 %reduce-scatter.48.cloned.1.call-start = ((), (), s32[]{:S(2)}) async-start(), calls=%async_computation.42 | async-start | bytes 3145728 | tf_op jit(solution)/shard_map/reduce_scatter | solution.py:154
  624.3 113.5 %reduce-scatter.52.cloned.1.call-start = ((), (), s32[]{:S(2)}) async-start(), calls=%async_computation.44 | async-start | bytes 3145728 | tf_op jit(solution)/shard_map/reduce_scatter | solution.py:154
  628.2 184.7 %reduce-scatter.72.cloned.1.call-start = ((), (), s32[]{:S(2)}) async-start(), calls=%async_computation.69 | async-start | bytes 278528
  631.9 256.9 %reduce-scatter.56.cloned.1.call-start = ((), (), s32[]{:S(2)}) async-start(), calls=%async_computation.46 | async-start | bytes 835584 | tf_op jit(solution)/shard_map/reduce_scatter | solution.py:155
  644.5 260.2 %reduce-scatter.44.cloned.1.call-start = ((), (), s32[]{:S(2)}) async-start(), calls=%async_computation.40 | async-start | bytes 3145728 | tf_op jit(solution)/shard_map/reduce_scatter | solution.py:154
  646.7 333.7 %reduce-scatter.64.cloned.1.call-start = ((), (), s32[]{:S(2)}) async-start(), calls=%async_computation.50 | async-start | bytes 1114112 | tf_op jit(solution)/shard_map/reduce_scatter | solution.py:155
  658.4 397.5 %reduce-scatter.68.cloned.1.call-start = ((), (), s32[]{:S(2)}) async-start(), calls=%async_computation.52 | async-start | bytes 1114112 | tf_op jit(solution)/shard_map/reduce_scatter | solution.py:155
  674.4 457.1 %reduce-scatter.60.cloned.1.call-start = ((), (), s32[]{:S(2)}) async-start(), calls=%async_computation.48 | async-start | bytes 1114112 | tf_op jit(solution)/shard_map/reduce_scatter | solution.py:155
  690.5 516.8 %reduce-scatter.42.cloned.1.call-start = ((), (), s32[]{:S(2)}) async-start(), calls=%async_computation.39 | async-start | bytes 835584 | tf_op jit(solution)/shard_map/reduce_scatter | solution.py:155
  708.2 574.5 %reduce-scatter.50.cloned.1.call-start = ((), (), s32[]{:S(2)}) async-start(), calls=%async_computation.43 | async-start | bytes 1114112 | tf_op jit(solution)/shard_map/reduce_scatter | solution.py:155
  722.0 636.3 %reduce-scatter.54.cloned.1.call-start = ((), (), s32[]{:S(2)}) async-start(), calls=%async_computation.45 | async-start | bytes 1114112 | tf_op jit(solution)/shard_map/reduce_scatter | solution.py:155
  737.8 695.7 %reduce-scatter.46.cloned.1.call-start = ((), (), s32[]{:S(2)}) async-start(), calls=%async_computation.41 | async-start | bytes 1114112 | tf_op jit(solution)/shard_map/reduce_scatter | solution.py:155
  904.8 589.1 %all-gather.61.cloned.1.call-start = ((), (), s32[]{:S(2)}) async-start(), calls=%async_computation.67 | async-start | bytes 4925440 | tf_op jit(solution)/shard_map/all_gather | solution.py:198
  (105 other events, 2239.3 us)
Sparse Core Ops, SparseCore 0:
  14.0 44.7 all-gather.34
  61.5 40.7 all-gather.38
  105.0 41.8 all-gather.42
  163.5 14.6 all-gather.36
  179.7 14.6 all-gather.40
  196.0 14.6 all-gather.44
  213.3 42.0 all-gather.48
  257.6 41.8 all-gather.52
  301.4 41.8 all-gather.56
  346.3 20.8 reduce-scatter.29
  368.7 14.0 all-gather.46
  384.4 14.6 all-gather.50
  400.6 14.6 all-gather.54
  416.7 14.6 all-gather.58
  437.6 25.7 reduce-scatter.33
  465.7 21.3 reduce-scatter.31
  515.9 22.0 reduce-scatter.35
  557.9 23.0 reduce-scatter.37
  604.1 22.0 reduce-scatter.39
  644.7 13.7 reduce-scatter.61
  708.2 13.7 reduce-scatter.47
  741.9 71.0 reduce-scatter.71
  816.7 72.0 reduce-scatter.55
  891.0 13.6 reduce-scatter.43
  908.3 72.1 reduce-scatter.63
  983.6 72.2 reduce-scatter.67
  1059.3 72.1 reduce-scatter.59
  1135.3 71.8 reduce-scatter.41
  1210.4 72.2 reduce-scatter.49
  1286.1 72.1 reduce-scatter.53
  1361.3 72.1 reduce-scatter.45
  1448.3 45.4 all-gather.60
  (6 shorter events, 80.7 us)

commit v2 on v1

v2 whole, which is shorter than its diff:
```python
import jax
import jax.numpy as jnp
from jax import lax
from jax.experimental import pallas as pl
from jax.experimental.pallas import tpu as pltpu
from jax.sharding import PartitionSpec as P

EPS = 1e-06
NEG = -1e30
BF = jnp.bfloat16
F32 = jnp.float32
MESH = pl.DeviceIdType.MESH
D = 1024
ROWS = 80
TOK = 72
N = 4 * ROWS
TENSORS = {"q": (0, 384, True), "o": (384, 512, False), "u": (896, 512, True), "d": (1408, 512, False)}
HALF = 1920


def dot(a, b):
    return lax.dot_general(a, b, (((1,), (0,)), ((), ())), preferred_element_type=F32)


def dot_rows(a, b):
    return lax.dot_general(a, b, (((0,), (0,)), ((), ())), preferred_element_type=F32)


def dot_cols(a, b):
    return lax.dot_general(a, b, (((1,), (1,)), ((), ())), preferred_element_type=F32)


def normalise(values):
    centre = values - jnp.mean(values, axis=-1, keepdims=True)
    scale = lax.rsqrt(jnp.mean(centre * centre, axis=-1, keepdims=True) + EPS)
    return centre * scale, scale


def norm_back(grad, values, gain):
    xhat, scale = normalise(values)
    f = grad * gain
    dv = scale * (
        f
        - jnp.mean(f, axis=-1, keepdims=True)
        - xhat * jnp.mean(f * xhat, axis=-1, keepdims=True)
    )
    return dv, jnp.sum(grad * xhat, axis=0, keepdims=True)


def gelu_parts(u):
    cdf = 0.5 * (1.0 + lax.erf(u * 0.7071067811865476))
    slope = cdf + u * jnp.exp(-0.5 * u * u) * 0.3989422804014327
    return u * cdf, slope


SCRATCH = dict(
    own=((2, 64, HALF), BF),
    wq=((2, 4, 4, 64, 768), BF),
    wo=((2, 4, 4, 64, D), BF),
    wu=((2, 4, 4, 64, D), BF),
    wd=((2, 4, 4, 64, D), BF),
    vsend=((6, 8, D), F32),
    vrecv=((17, 8, D), F32),
    vec=((8, D), F32),
    vgrad=((8, D), F32),
    x=((80, D), BF),
    h1=((2, 4, ROWS, D), BF),
    qkv=((2, 4, ROWS, 768), BF),
    prob=((2, 4, N, N), BF),
    osend=((2, 4, ROWS, 256), BF),
    ojoin=((2, 4, ROWS, 256), BF),
    a=((2, ROWS, D), F32),
    y1=((2, ROWS, D), F32),
    h2=((2, 4, ROWS, D), BF),
    slope=((2, 4, ROWS, D), BF),
    g=((2, 4, ROWS, D), BF),
    stage=((2, 4, ROWS, D), BF),
    part=((6, 3, ROWS, D), BF),
    mine=((ROWS, D), F32),
    m=((2, ROWS, D), F32),
    dm=((2, 4, ROWS, D), BF),
    du=((4, ROWS, D), BF),
    dy1=((ROWS, D), F32),
    da=((ROWS, D), BF),
    dosend=((2, 4, ROWS, 256), BF),
    dojoin=((2, 4, ROWS, 256), BF),
    dqkv=((4, ROWS, 768), BF),
    zout=((2, ROWS, D), BF),
    gout=((2, ROWS, D), BF),
    zother=((ROWS, D), BF),
    gother=((ROWS, D), BF),
    fin=((2, 4, 64, HALF), BF),
    fother=((4, 64, HALF), BF),
)
for _t, (_, _h, _x) in TENSORS.items():
    SCRATCH["gs" + _t] = ((4, 4, 64, _h), BF)
    SCRATCH["ra" + _t] = ((2, 4, 4, 64, _h), BF)
    SCRATCH["rb" + _t] = ((2, 3, 4, 64, _h), BF)
    SCRATCH["rc" + _t] = ((2, 3, 64, _h), BF)

GROUPS = (
    ["A", "Alocal", "va", "vx", "vy", "ga", "gx", "gy", "gz", "zo", "go", "fo"]
    + [n + t + str(l) for n in ("B", "Bl", "C", "D", "ga", "gb", "gc", "ge") for t in "qoud" for l in (0, 1)]
    + [n + str(l) for n in ("h1", "h2", "o", "m", "dm", "dh2", "do", "dh1") for l in (0, 1)]
)
GROUP = {n: i for i, n in enumerate(dict.fromkeys(GROUPS))}


class Refs:
    pass


def kernel(x_in, dz_in, wown, vin, idc, idr, lo_ref, gi_ref, gq_ref, go_ref, gu_ref, gd_ref, gv_ref, *scratch):
    r = Refs()
    for name, ref in zip(SCRATCH, scratch):
        setattr(r, name, ref)
    ssem, rsem = scratch[len(SCRATCH) :]
    c = lax.axis_index("section")
    z = lax.axis_index("seq")
    p = lax.axis_index("shard")
    y, x = p // 4, p % 4
    sib = {"section": 1 - c}

    def zpeer(k):
        return {"seq": (z + k) % 4}

    def xpeer(k):
        return {"shard": y * 4 + (x + k) % 4}

    def ypeer(k):
        return {"shard": ((y + k) % 4) * 4 + x}

    pending = {}

    def copy(group, slot, src, dst, dev):
        return pltpu.make_async_remote_copy(
            src_ref=src,
            dst_ref=dst,
            send_sem=ssem.at[GROUP[group], slot],
            recv_sem=rsem.at[GROUP[group], slot],
            device_id=dev,
            device_id_type=MESH,
        )

    def push(group, slot, src, dst, dev):
        copy(group, slot, src, dst, dev).start()
        pending[(group, slot)] = (src, dev)

    def sent(group):
        for key in [k for k in pending if k[0] == group]:
            src, dev = pending.pop(key)
            copy(group, key[1], src, src, dev).wait_send()

    def arrived(group, slot, dst):
        copy(group, slot, dst, dst, sib).wait_recv()

    barrier = pltpu.get_barrier_semaphore()
    for dev in [sib] + [f(k) for f in (xpeer, ypeer, zpeer) for k in (1, 2, 3)]:
        pl.semaphore_signal(barrier, inc=1, device_id=dev, device_id_type=MESH)
    pl.semaphore_wait(barrier, 10)

    def half(h, which):
        return pl.ds(pl.multiple_of(which * h, 128), h)

    push("A", 0, wown.at[1 - c], r.own.at[c], sib)
    own_copy = pltpu.make_async_copy(wown.at[c], r.own.at[c], ssem.at[GROUP["Alocal"], 0])
    own_copy.start()
    push("va", 0, vin, r.vrecv.at[0], sib)

    def wref(t):
        return getattr(r, "w" + t)

    def local_copy(t, l):
        off, h, _ = TENSORS[t]
        return pltpu.make_async_copy(
            r.own.at[l, :, pl.ds(off, h)],
            wref(t).at[l, y, x, :, half(h, c)],
            ssem.at[GROUP["Bl" + t + str(l)], 0],
        )

    def weight_b(t, l):
        off, h, xfirst = TENSORS[t]
        peer = xpeer if xfirst else ypeer
        for k in (1, 2, 3):
            push(
                "B" + t + str(l), k - 1,
                r.own.at[l, :, pl.ds(off, h)],
                wref(t).at[l, y, x, :, half(h, c)],
                peer(k),
            )
        local_copy(t, l).start()

    def weight_c(t, l):
        _, h, xfirst = TENSORS[t]
        cols = half(h, c)
        local_copy(t, l).wait()
        for k in (1, 2, 3):
            if xfirst:
                arrived("B" + t + str(l), k - 1, wref(t).at[l, y, (x + 4 - k) % 4, :, cols])
            else:
                arrived("B" + t + str(l), k - 1, wref(t).at[l, (y + 4 - k) % 4, x, :, cols])
        line = wref(t).at[l, y, :, :, cols] if xfirst else wref(t).at[l, :, x, :, cols]
        peer = ypeer if xfirst else xpeer
        for k in (1, 2, 3):
            push("C" + t + str(l), k - 1, line, line, peer(k))

    def weight_d(t, l):
        _, h, xfirst = TENSORS[t]
        cols = half(h, c)
        for k in (1, 2, 3):
            if xfirst:
                line = wref(t).at[l, (y + 4 - k) % 4, :, :, cols]
            else:
                line = wref(t).at[l, :, (x + 4 - k) % 4, :, cols]
            arrived("C" + t + str(l), k - 1, line)
        mine = wref(t).at[l, :, :, :, cols]
        push("D" + t + str(l), 0, mine, mine, sib)

    def weight_done(t, l):
        _, h, _ = TENSORS[t]
        arrived("D" + t + str(l), 0, wref(t).at[l, :, :, :, half(h, 1 - c)])

    def spread(group, at, slots, value, peer):
        r.vsend[at] = value
        for k in (1, 2, 3):
            push(group, k - 1, r.vsend.at[at], r.vrecv.at[slots + k - 1], peer(k))

    def gathered(group, slots, value):
        for k in (1, 2, 3):
            arrived(group, k - 1, r.vrecv.at[slots + k - 1])
        return value + (r.vrecv[slots] + (r.vrecv[slots + 1] + r.vrecv[slots + 2]))

    own_copy.wait()
    arrived("A", 0, r.own.at[1 - c])
    weight_b("q", 0)
    arrived("va", 0, r.vrecv.at[0])
    v = vin[...] + r.vrecv[0]
    spread("vx", 0, 1, v, xpeer)
    weight_b("o", 0)
    weight_b("u", 0)
    weight_b("d", 0)
    xhat0, _ = normalise(x_in[...].astype(F32))
    v = gathered("vx", 1, v)
    spread("vy", 1, 4, v, ypeer)
    weight_c("q", 0)
    v = gathered("vy", 4, v)
    r.vec[...] = v

    def gain(l, row):
        return r.vec[4 * l + row : 4 * l + row + 1, :]

    def send_block(group, ref):
        for k in (1, 2, 3):
            push(group, k - 1, ref.at[z], ref.at[z], zpeer(k))

    def flat(value):
        return value.reshape(N, value.shape[-1])

    def weight(t, l, cols):
        return wref(t)[l, :, :, :, cols].reshape(D, -1)

    lanes = lax.broadcasted_iota(jnp.int32, (1, 128), 1)
    low_lanes = lanes < 64

    def mask_head(value, head):
        keep = low_lanes if head == 0 else jnp.logical_not(low_lanes)
        return jnp.where(keep, value, jnp.zeros_like(value))

    RS = {"m0": 0, "m1": 1, "dh21": 2, "dh11": 3, "dh20": 4, "dh10": 5}

    def rs_slot(group, k, blk, start):
        i = RS[group]
        return copy(
            group, 3 - k,
            r.stage.at[i % 2, blk], r.part.at[i, 3 - k],
            {"seq": blk},
        )

    def rs_put(group, k, blk, make):
        i = RS[group]
        for j in range(4):
            val = make(j)

            @pl.when(k == 0)
            def _():
                r.mine[:, 256 * j : 256 * j + 256] = val

            @pl.when(k > 0)
            def _():
                r.stage[i % 2, blk, :, 256 * j : 256 * j + 256] = val.astype(BF)

        @pl.when(k > 0)
        def _():
            rs_slot(group, k, blk, True).start()

    def rs_sum(group):
        i = RS[group]
        for s in range(3):
            arrived(group, s, r.part.at[i, s])
        return r.mine[...] + (
            r.part[i, 0].astype(F32) + (r.part[i, 1].astype(F32) + r.part[i, 2].astype(F32))
        )

    def rs_sent(group):
        i = RS[group]
        for k in (1, 2, 3):
            rs_slot(group, k, (z + 4 - k) % 4, False).wait_send()

    def ag_wait(group, ref, k, blk):
        @pl.when(k > 0)
        def _():
            copy(group, k - 1, ref.at[blk], ref.at[blk], sib).wait_recv()

    def attn_forward(l, xhat, xin, gap_a, gap_b):
        r.h1[l, z] = (xhat * gain(l, 0)).astype(BF)
        send_block("h1" + str(l), r.h1.at[l])
        gap_a()
        weight_done("q", l)

        @pl.loop(0, 4)
        def _(k):
            blk = (z + 4 - k) % 4
            ag_wait("h1" + str(l), r.h1.at[l], k, blk)
            for j in range(3):
                cols = pl.ds(256 * j, 256)
                r.qkv[l, blk, :, cols] = dot(r.h1[l, blk], weight("q", l, cols)).astype(BF)

        gap_b()
        same = idc[...] == idr[...]

        @pl.loop(0, 2)
        def _(pair):
            base = pl.multiple_of(pair * 384, 128)
            q = flat(r.qkv[l, :, :, pl.ds(base, 128)])
            kk = flat(r.qkv[l, :, :, pl.ds(pl.multiple_of(base + 128, 128), 128)])
            vv = flat(r.qkv[l, :, :, pl.ds(pl.multiple_of(base + 256, 128), 128)])
            q = q * jnp.asarray(0.125, BF)
            res = []
            for head in range(2):
                s = dot_cols(mask_head(q, head), kk)
                s = jnp.where(same, s, NEG)
                e = jnp.exp(s - jnp.max(s, axis=-1, keepdims=True))
                pb = (e * (1.0 / jnp.sum(e, axis=-1, keepdims=True))).astype(BF)
                r.prob[l, 2 * pair + head] = pb
                res.append(dot(pb, vv))
            o = jnp.where(low_lanes, res[0], res[1]).astype(BF)
            r.osend[l, :, :, pl.ds(pl.multiple_of(pair * 128, 128), 128)] = o.reshape(4, ROWS, 128)

        for k in (1, 2, 3):
            blk = (z + k) % 4
            push("o" + str(l), k - 1, r.osend.at[l, blk], r.ojoin.at[l, z], zpeer(k))
        r.ojoin[l, z] = r.osend[l, z]

    def out_proj(l, xin):
        weight_done("o", l)
        for k in (1, 2, 3):
            arrived("o" + str(l), k - 1, r.ojoin.at[l, (z + 4 - k) % 4])
        for j in range(4):
            cols = pl.ds(256 * j, 256)
            acc = None
            for b in range(4):
                w = wref("o")[l, b, :, :, cols].reshape(256, 256)
                term = dot(r.ojoin[l, b], w)
                acc = term if acc is None else acc + term
            r.a[l, :, cols] = acc
        y1 = xin + gain(l, 1) * r.a[l]
        r.y1[l] = y1
        yhat, _ = normalise(y1)
        r.h2[l, z] = (yhat * gain(l, 2)).astype(BF)
        send_block("h2" + str(l), r.h2.at[l])

    def mlp_forward(l, gap_a):
        gap_a()
        weight_done("u", l)
        weight_done("d", l)

        @pl.loop(0, 4)
        def _(k):
            blk = (z + 4 - k) % 4
            ag_wait("h2" + str(l), r.h2.at[l], k, blk)
            for j in range(4):
                cols = pl.ds(256 * j, 256)
                u = dot(r.h2[l, blk], weight("u", l, cols))
                g, slope = gelu_parts(u)
                r.g[l, blk, :, cols] = g.astype(BF)
                r.slope[l, blk, :, cols] = slope.astype(BF)

            def make(j):
                return dot(r.g[l, blk], weight("d", l, pl.ds(256 * j, 256)))

            rs_put("m" + str(l), k, blk, make)

    def finish_layer(l):
        m = rs_sum("m" + str(l))
        r.m[l] = m
        r.zout[l] = (r.y1[l] + gain(l, 3) * m).astype(BF)

    def grad_first(t, l, left, right):
        _, h, _ = TENSORS[t]
        gs = getattr(r, "gs" + t)

        @pl.loop(0, 4)
        def _(b):
            gs[b] = dot_rows(left(b), right(half(h, 1 - c))).astype(BF).reshape(4, 64, h)

        push("ga" + t + str(l), 0, gs, getattr(r, "ra" + t).at[l], sib)

    def grad_second(t, l, left, right):
        _, h, xfirst = TENSORS[t]
        ra = getattr(r, "ra" + t)
        arrived("ga" + t + str(l), 0, ra.at[l])

        @pl.loop(0, 4)
        def _(b):
            val = dot_rows(left(b), right(half(h, c))).reshape(4, 64, h)
            ra[l, b] = (val + ra[l, b].astype(F32)).astype(BF)

        for k in (1, 2, 3):
            if xfirst:
                src, dev = ra.at[l, (y + k) % 4], ypeer(k)
            else:
                src, dev = ra.at[l, :, (x + k) % 4], xpeer(k)
            push("gb" + t + str(l), k - 1, src, getattr(r, "rb" + t).at[l, k - 1], dev)

    def grad_third(t, l):
        _, h, xfirst = TENSORS[t]
        ra, rb = getattr(r, "ra" + t), getattr(r, "rb" + t)
        for k in (1, 2, 3):
            arrived("gb" + t + str(l), k - 1, rb.at[l, k - 1])

        @pl.loop(0, 4)
        def _(i):
            yy, xx = (y, i) if xfirst else (i, x)
            val = ra[l, yy, xx].astype(F32) + rb[l, 0, i].astype(F32)
            val = val + (rb[l, 1, i].astype(F32) + rb[l, 2, i].astype(F32))
            ra[l, yy, xx] = val.astype(BF)

        for k in (1, 2, 3):
            if xfirst:
                src, dev = ra.at[l, y, (x + k) % 4], xpeer(k)
            else:
                src, dev = ra.at[l, (y + k) % 4, x], ypeer(k)
            push("gc" + t + str(l), k - 1, src, getattr(r, "rc" + t).at[l, k - 1], dev)

    def grad_fourth(t, l):
        off, h, xfirst = TENSORS[t]
        ra, rc = getattr(r, "ra" + t), getattr(r, "rc" + t)
        for k in (1, 2, 3):
            arrived("gc" + t + str(l), k - 1, rc.at[l, k - 1])
        val = ra[l, y, x].astype(F32) + rc[l, 0].astype(F32)
        val = val + (rc[l, 1].astype(F32) + rc[l, 2].astype(F32))
        r.fin[l, z, :, off : off + h] = val.astype(BF)
        block = r.fin.at[l, z, :, pl.ds(off, h)]
        for k in (1, 2, 3):
            push("ge" + t + str(l), k - 1, block, block, zpeer(k))

    def grad_done(t, l):
        off, h, _ = TENSORS[t]
        for k in (1, 2, 3):
            arrived("ge" + t + str(l), k - 1, r.fin.at[l, (z + 4 - k) % 4, :, pl.ds(off, h)])

    def mlp_backward(l, dz, gap_a, gap_b):
        r.dm[l, z] = (gain(l, 3) * dz).astype(BF)
        send_block("dm" + str(l), r.dm.at[l])
        r.vgrad[4 * l + 3 : 4 * l + 4, :] = jnp.sum(dz * r.m[l], axis=0, keepdims=True)
        r.dy1[...] = dz
        gap_a()

        @pl.loop(0, 4)
        def _(k):
            blk = (z + 4 - k) % 4
            ag_wait("dm" + str(l), r.dm.at[l], k, blk)
            for b in range(4):
                w = wref("d")[l, b].reshape(256, D)
                cols = pl.ds(256 * b, 256)
                grad = dot_cols(r.dm[l, blk], w)
                r.du[blk, :, cols] = (grad * r.slope[l, blk, :, cols].astype(F32)).astype(BF)

            def make(b):
                return dot_cols(r.du[blk], wref("u")[l, b].reshape(256, D))

            rs_put("dh2" + str(l), k, blk, make)

        def tile(ref):
            return lambda b: flat(ref[:, :, pl.ds(pl.multiple_of(b * 256, 256), 256)])

        def cols_of(ref):
            return lambda cols: flat(ref[:, :, cols])

        g_l, h2_l, dm_l = r.g.at[l], r.h2.at[l], r.dm.at[l]
        grad_first("d", l, tile(g_l), cols_of(dm_l))
        grad_first("u", l, tile(h2_l), cols_of(r.du))
        gap_b()
        dh2 = rs_sum("dh2" + str(l))
        dn, dg2 = norm_back(dh2, r.y1[l], gain(l, 2))
        r.vgrad[4 * l + 2 : 4 * l + 3, :] = dg2
        dy1 = r.dy1[...] + dn
        r.dy1[...] = dy1
        r.da[...] = (gain(l, 1) * dy1).astype(BF)
        for b in range(4):
            w = wref("o")[l, b].reshape(256, D)
            r.dosend[l, b] = dot_cols(r.da[...], w).astype(BF)
        for k in (1, 2, 3):
            push("do" + str(l), k - 1, r.dosend.at[l, (z + k) % 4], r.dojoin.at[l, z], zpeer(k))
        r.dojoin[l, z] = r.dosend[l, z]
        r.vgrad[4 * l + 1 : 4 * l + 2, :] = jnp.sum(dy1 * r.a[l], axis=0, keepdims=True)
        grad_second("d", l, tile(g_l), cols_of(dm_l))
        grad_second("u", l, tile(h2_l), cols_of(r.du))

    def attn_backward(l, gap_a, gap_b):
        gap_a()
        for k in (1, 2, 3):
            arrived("do" + str(l), k - 1, r.dojoin.at[l, (z + 4 - k) % 4])

        @pl.loop(0, 2)
        def _(pair):
            base = pl.multiple_of(pair * 384, 128)
            c_k = pl.ds(pl.multiple_of(base + 128, 128), 128)
            c_v = pl.ds(pl.multiple_of(base + 256, 128), 128)
            q = flat(r.qkv[l, :, :, pl.ds(base, 128)]) * jnp.asarray(0.125, BF)
            kk = flat(r.qkv[l, :, :, c_k])
            vv = flat(r.qkv[l, :, :, c_v])
            do = flat(r.dojoin[l, :, :, pl.ds(pl.multiple_of(pair * 128, 128), 128)])
            dq, dk, dv = [], [], []
            for head in range(2):
                pb = r.prob[l, 2 * pair + head]
                pf = pb.astype(F32)
                dp = dot_cols(mask_head(do, head), vv)
                dv.append(dot_rows(pb, do))
                ds = (pf * (dp - jnp.sum(pf * dp, axis=-1, keepdims=True))).astype(BF)
                dq.append(dot(ds, kk))
                dk.append(dot_rows(ds, q))

            def put(cols, both, scale):
                val = jnp.where(low_lanes, both[0], both[1])
                if scale is not None:
                    val = val * scale
                r.dqkv[:, :, cols] = val.astype(BF).reshape(4, ROWS, 128)

            put(pl.ds(base, 128), dq, 0.125)
            put(c_k, dk, None)
            put(c_v, dv, None)

        @pl.loop(0, 4)
        def _(k):
            blk = (z + 4 - k) % 4

            def make(b):
                return dot_cols(r.dqkv[blk], wref("q")[l, b].reshape(256, 768))

            rs_put("dh1" + str(l), k, blk, make)

        def left_q(b):
            return flat(r.h1[l, :, :, pl.ds(pl.multiple_of(b * 256, 256), 256)])

        def right_q(cols):
            return flat(r.dqkv[:, :, cols])

        def left_o(b):
            return r.ojoin[l, b]

        def right_o(cols):
            return r.da[:, cols]

        grad_first("q", l, left_q, right_q)
        grad_first("o", l, left_o, right_o)
        gap_b()
        grad_second("q", l, left_q, right_q)
        grad_second("o", l, left_o, right_o)
        dh1 = rs_sum("dh1" + str(l))
        xin = (r.x[...] if l == 0 else r.zout[0]).astype(F32)
        dn, dg1 = norm_back(dh1, xin, gain(l, 0))
        r.vgrad[4 * l : 4 * l + 1, :] = dg1
        dx = (r.dy1[...] + dn).astype(BF)
        r.gout[l] = dx
        return dx

    r.x[...] = x_in[...]

    def gap_f0a():
        weight_c("o", 0)
        weight_d("q", 0)
        weight_c("u", 0)
        weight_c("d", 0)

    def gap_f0b():
        weight_d("o", 0)
        weight_b("q", 1)
        weight_b("o", 1)

    attn_forward(0, xhat0, None, gap_f0a, gap_f0b)
    weight_d("u", 0)
    weight_b("u", 1)
    weight_b("d", 1)
    out_proj(0, x_in[...].astype(F32))

    def gap_f0c():
        weight_d("d", 0)
        weight_c("q", 1)
        weight_c("o", 1)

    mlp_forward(0, gap_f0c)
    weight_d("q", 1)
    weight_c("u", 1)
    weight_c("d", 1)
    finish_layer(0)
    x1 = r.zout[0].astype(F32)
    xhat1, _ = normalise(x1)

    def gap_f1b():
        weight_d("o", 1)

    attn_forward(1, xhat1, None, lambda: None, gap_f1b)
    weight_d("u", 1)
    out_proj(1, r.zout[0].astype(F32))

    def gap_f1c():
        weight_d("d", 1)

    mlp_forward(1, gap_f1c)
    finish_layer(1)
    push("zo", 0, r.zout.at[1 - c], r.zother, sib)

    rs_sent("m0")
    mlp_backward(1, dz_in[...].astype(F32), lambda: None, lambda: None)
    rs_sent("m1")

    def gap_b1b():
        grad_third("d", 1)
        grad_third("u", 1)

    attn_backward(1, lambda: None, gap_b1b)
    for t in "qoud":
        sent("ga" + t + "1")
    rs_sent("dh21")

    def gap_b0a():
        grad_fourth("d", 1)
        grad_fourth("u", 1)

    def gap_b0b():
        grad_third("q", 1)
        grad_third("o", 1)

    mlp_backward(0, r.gout[1].astype(F32), gap_b0a, gap_b0b)
    rs_sent("dh11")

    def gap_b0c():
        grad_fourth("q", 1)
        grad_fourth("o", 1)

    def gap_b0d():
        grad_third("d", 0)
        grad_third("u", 0)

    attn_backward(0, gap_b0c, gap_b0d)

    push("go", 0, r.gout.at[1 - c], r.gother, sib)
    gv = r.vgrad[...]
    r.vsend[2] = gv
    push("ga", 0, r.vsend.at[2], r.vrecv.at[7], sib)
    grad_fourth("d", 0)
    grad_fourth("u", 0)
    arrived("ga", 0, r.vrecv.at[7])
    gv = gv + r.vrecv[7]
    spread("gx", 3, 8, gv, xpeer)
    grad_third("q", 0)
    grad_third("o", 0)
    gv = gathered("gx", 8, gv)
    spread("gy", 4, 11, gv, ypeer)
    grad_fourth("q", 0)
    grad_fourth("o", 0)
    gv = gathered("gy", 11, gv)
    spread("gz", 5, 14, gv, zpeer)
    for l in (1, 0):
        for t in "duqo":
            grad_done(t, l)
    push("fo", 0, r.fin.at[1 - c], r.fother, sib)
    arrived("zo", 0, r.zother)
    lo_ref[c] = r.zout[c, :TOK]
    lo_ref[1 - c] = r.zother[:TOK]
    arrived("go", 0, r.gother)
    gi_ref[c] = r.gout[c, :TOK]
    gi_ref[1 - c] = r.gother[:TOK]
    gv_ref[...] = gathered("gz", 14, gv)

    def assemble(get, which):
        for zz in range(4):
            for t in range(3):
                col = pl.multiple_of(t * 1024 + zz * 256 + which * 128, 128)
                gq_ref[:, pl.ds(col, 128)] = get(zz, t * 128, 128).astype(F32)
            gd_ref[64 * zz : 64 * zz + 64, half(512, which)] = get(zz, 1408, 512).astype(F32)
        total = get(0, 384, 512).astype(F32)
        for zz in range(1, 4):
            total = total + get(zz, 384, 512).astype(F32)
        go_ref[:, half(512, which)] = total
        ups = [get(zz, 896, 512).astype(F32) for zz in range(4)]
        for j in range(8):
            row = jnp.concatenate([u[:, 64 * j : 64 * j + 64] for u in ups], axis=1)
            gu_ref[:, pl.ds(pl.multiple_of((which * 8 + j) * 256, 256), 256)] = row

    assemble(lambda zz, at, n: r.fin[c, zz, :, at : at + n], c)
    arrived("fo", 0, r.fother)
    assemble(lambda zz, at, n: r.fother[zz, :, at : at + n], 1 - c)
    rs_sent("dh20")
    rs_sent("dh10")
    for group in {k[0]: None for k in list(pending)}:
        sent(group)


def local(acts_in, cotangent, qkv_weight, out_weight, up_weight, down_weight, vectors, image_ids):
    c = lax.axis_index("section")
    z = lax.axis_index("seq")
    p = lax.axis_index("shard")

    def halves(w):
        n = w.shape[1] // 2
        return w.reshape(64, 2, n).transpose(1, 0, 2)

    qkv = lax.dynamic_index_in_dim(qkv_weight[0].reshape(64, 3, 4, 2, 128), z, 2, False)
    qkv = qkv.transpose(2, 0, 1, 3).reshape(2, 64, 384)
    up = lax.dynamic_index_in_dim(up_weight[0].reshape(64, 16, 4, 64), z, 2, False).reshape(64, D)
    down = lax.dynamic_index_in_dim(down_weight[0].reshape(4, 64, D), z, 0, False)
    wown = jnp.concatenate([qkv, halves(out_weight[0]), halves(up), halves(down)], axis=2)
    vin = lax.dynamic_update_slice(
        jnp.zeros((8, D), F32), vectors[0].astype(F32), (4 * c, 64 * p)
    )

    def mine(a):
        a = lax.dynamic_index_in_dim(a, c, 0, False)[0]
        return jnp.pad(a, ((0, ROWS - TOK), (0, 0)))

    ids = lax.dynamic_index_in_dim(image_ids, c, 0, False)[0]
    ids = jnp.pad(ids.reshape(4, TOK), ((0, 0), (0, ROWS - TOK)), constant_values=-1).reshape(N)
    vmem = pl.BlockSpec(memory_space=pltpu.VMEM)
    out = pl.pallas_call(
        kernel,
        out_shape=(
            jax.ShapeDtypeStruct((2, TOK, D), BF),
            jax.ShapeDtypeStruct((2, TOK, D), BF),
            jax.ShapeDtypeStruct((64, 3072), F32),
            jax.ShapeDtypeStruct((64, D), F32),
            jax.ShapeDtypeStruct((64, 4096), F32),
            jax.ShapeDtypeStruct((256, D), F32),
            jax.ShapeDtypeStruct((8, D), F32),
        ),
        in_specs=[vmem, vmem, pl.BlockSpec(memory_space=pl.ANY), vmem, vmem, vmem],
        out_specs=(vmem,) * 7,
        scratch_shapes=[pltpu.VMEM(s, t) for s, t in SCRATCH.values()]
        + [pltpu.SemaphoreType.DMA((len(GROUP), 3)), pltpu.SemaphoreType.DMA((len(GROUP), 3))],
        compiler_params=pltpu.CompilerParams(
            collective_id=0, has_side_effects=True, vmem_limit_bytes=64 * 1024 * 1024 - 65536
        ),
    )(mine(acts_in), mine(cotangent), wown, vin, ids[:, None], ids[None, :])
    gv = lax.dynamic_slice(out[6], (4 * c, 64 * p), (4, 64))
    return (
        out[0][None, :, None],
        out[1][None, :, None],
        out[2][None],
        out[3][None],
        out[4][None],
        out[5][None],
        gv[None],
    )


def solution(mesh):
    placed = (
        P(None, "shard", "seq", None),
        P(None, "shard", "seq", None),
        P("section", "shard", None),
        P("section", "shard", None),
        P("section", "shard", None),
        P("section", "shard", None),
        P("section", None, "shard"),
        P(None, "shard", None),
    )
    return jax.shard_map(
        local,
        mesh=mesh,
        in_specs=placed,
        out_specs=(
            P("section", None, "shard", "seq", None),
            P("section", None, "shard", "seq", None),
            P("section", "shard", None),
            P("section", "shard", None),
            P("section", "shard", None),
            P("section", "shard", None),
            P("section", None, "shard"),
        ),
        check_vma=False,
    )
```

time: 1550 us -> 240 us (0.15)
  waiting for transfers between devices: 1110 us -> 0 us
  Pallas kernels: 0 us -> 218 us
  blocking collectives: 206 us -> 0 us
  matrix products: 71.9 us -> 0 us
  local copies, waits for them, and re-layouts: 75.3 us -> 20.1 us
  other arithmetic: 40.9 us -> 0.83 us
  starting transfers between devices: 16.7 us -> 0 us
  between operations: 16.4 us -> 0.8 us
    reduce_scatter x20 -> x0, waiting for transfers between devices: 799 us -> none  [the longest x8 598 us: reduce_pieces(): own = lax.psum_scatter(half, 'shard', scatter_dimension=0, tiled=True)]
    pallas_call x0 -> x1, Pallas kernels: none -> 218 us  [local(): pl.pallas_call(kernel, out_shape=(jax.ShapeDtypeStruct((2, TOK, D), BF),...]
    all_gather x15 -> x0, waiting for transfers between devices: 196 us -> none  [the longest x6 153 us: gather_weights(): whole = lax.all_gather(p[layer], 'shard', axis=0, tiled=True)]
    all_gather x9 -> x0, blocking collectives: 179 us -> none  [the longest x6 71.5 us: gather_tokens(): return lax.all_gather(rows, 'seq', axis=0, tiled=True)]
    unnamed x41 -> x0, waiting for transfers between devices: 104 us -> none
    dot_general x36 -> x0, matrix products: 71.9 us -> none  [the longest x8 24.5 us: dot(): return jnp.dot(a, b, preferred_element_type=F32)]
    all_to_all x6 -> x0, blocking collectives: 27 us -> none  [the longest x4 16.4 us: gather_weights(): lax.all_to_all(p, 'section', split_axis=0, concat_axis=0, tiled=True)]
    unnamed x216 -> x28, local copies, waits for them, and re-layouts: 34.5 us -> 9.89 us
  transfers between devices with their start and end apart: 42 -> 0, of which waited for: 32 -> 0; matrix products, arithmetic and copies ran while one was open for 5% -> 0% of each run, Pallas kernels for 0% -> 0%
where the time goes in v2:
time: 240 us
  Pallas kernels  218 us (91%)
  local copies, waits for them, and re-layouts  20.1 us (8%)
    pallas_call x1, Pallas kernels, local(): pl.pallas_call(kernel, out_shape=(jax.ShapeDtypeStruct((2, TOK, D), BF),...  218 us
    unnamed x28, local copies, waits for them, and re-layouts  9.89 us

profile of v2, /device:TPU:1, one launch (start us, length us, event | category | flops | bytes accessed | tf_op | source)
XLA Modules:
  0.0 239.8 jit_solution(7843713699970921187)
XLA Ops:
  0.7 0.7 copy-done.9
  1.3 0.0 copy-done.10
  1.4 0.1 reshape_squeeze.19
  1.5 0.6 broadcast_in_dim_reshape.7.idr
  2.1 0.2 dynamic_update_slice.3.vin
  2.4 0.6 copy-done.6
  3.0 1.0 reshape_squeeze.16
  4.0 1.0 constant_dynamic-slice_fusion
  5.0 0.1 reshape.28
  5.1 0.8 broadcast_in_dim_reshape.8.idc
  5.9 0.0 copy-start.4
  5.9 0.7 pad.12.dz_in
  6.6 0.7 pad.11.x_in
  7.3 0.3 reshape_squeeze.15
  7.6 0.0 copy-start.3
  7.6 0.1 constant_dynamic-slice_fusion.1
  7.7 0.1 reshape.27
  7.8 0.8 copy-done.3
  8.6 1.1 reshape_squeeze.17
  9.8 1.7 dynamic-slice_reduce_fusion
  11.5 0.2 reshape_reshape.3
  11.7 0.8 pad_maximum_fusion.wown
  12.5 218.1 %shard_map.135 = (bf16[2,72,1024]{2,1,0:T(8,128)(2,1)}, bf16[2,72,1024]{2,1,0:T(8,128)(2,1)}, f32[64,3072]{1,0:T(8,128)}, f32[64,1024]{1,0:T(8,128)}, f32[64,409...) custom-call(bf16[80,1024]{1,0:T(8,128)(2,1)} %pad.11.x_in, bf16[80,1024]{1,0:T(8,128)(2,1)} %pad.12.dz_in, ...), custom_call_target="tpu_custom_call" | custom-call | tf_op jit(solution)/shard_map/pallas_call | solution.py:736
  230.7 1.4 dynamic-slice_bitcast_fusion.2
  232.1 1.7 copy.40
  233.8 1.7 copy.41
  235.5 0.9 copy.42
  236.3 0.2 copy-done.5
  236.6 0.7 copy.43
  237.3 1.0 copy.44
  238.2 0.6 copy-done
  238.9 1.0 copy.45
  (22 shorter events, 0.2 us)
Async XLA Ops:
  0.6 0.7 copy-start.9
  0.6 0.7 copy-start.10
  2.4 0.6 copy-start.6
  4.0 1.9 copy-start.7
  4.0 1.9 copy-start.8
  5.9 1.4 copy-start.4
  7.6 1.0 copy-start.3
  230.7 4.8 %copy-start.2 = (f32[64,3072]{1,0:T(8,128)S(1)}, f32[64,3072]{1,0:T(8,128)}, u32[]{:S(2)}) copy-start(f32[64,3072]{1,0:T(8,128)} %get-tuple-element.16) | copy-start | bytes 2359300
  235.5 1.1 copy-start.5
  235.5 1.8 copy-start.1
  237.3 1.6 copy-start

commit v3 on v2

--- a/solution.py
+++ b/solution.py
@@ -11,8 +11,7 @@
 F32 = jnp.float32
 MESH = pl.DeviceIdType.MESH
 D = 1024
-ROWS = 80
-TOK = 72
+ROWS = 72
 N = 4 * ROWS
 TENSORS = {"q": (0, 384, True), "o": (384, 512, False), "u": (896, 512, True), "d": (1408, 512, False)}
 HALF = 1920
@@ -54,16 +53,14 @@
 
 
 SCRATCH = dict(
-    own=((2, 64, HALF), BF),
-    wq=((2, 4, 4, 64, 768), BF),
-    wo=((2, 4, 4, 64, D), BF),
-    wu=((2, 4, 4, 64, D), BF),
-    wd=((2, 4, 4, 64, D), BF),
-    vsend=((6, 8, D), F32),
+    ustage=((16, 64, 128), BF),
+    usend=((64, 512), BF),
+    xin=((ROWS, D), BF),
+    dzin=((ROWS, D), BF),
+    vsend=((7, 8, D), F32),
     vrecv=((17, 8, D), F32),
     vec=((8, D), F32),
     vgrad=((8, D), F32),
-    x=((80, D), BF),
     h1=((2, 4, ROWS, D), BF),
     qkv=((2, 4, ROWS, 768), BF),
     prob=((2, 4, N, N), BF),
@@ -93,14 +90,16 @@
     fother=((4, 64, HALF), BF),
 )
 for _t, (_, _h, _x) in TENSORS.items():
+    SCRATCH["own" + _t] = ((2, 64, _h), BF)
+    SCRATCH["w" + _t] = ((2, 2, 4, 4, 64, _h), BF)
     SCRATCH["gs" + _t] = ((4, 4, 64, _h), BF)
     SCRATCH["ra" + _t] = ((2, 4, 4, 64, _h), BF)
     SCRATCH["rb" + _t] = ((2, 3, 4, 64, _h), BF)
     SCRATCH["rc" + _t] = ((2, 3, 64, _h), BF)
 
 GROUPS = (
-    ["A", "Alocal", "va", "vx", "vy", "ga", "gx", "gy", "gz", "zo", "go", "fo"]
-    + [n + t + str(l) for n in ("B", "Bl", "C", "D", "ga", "gb", "gc", "ge") for t in "qoud" for l in (0, 1)]
+    ["x", "dz", "us", "va", "vx", "vy", "ga", "gx", "gy", "gz", "zo", "go", "fo"]
+    + [n + t + str(l) for n in ("A", "L", "B", "Bl", "C", "D", "ga", "gb", "gc", "ge") for t in "qoud" for l in (0, 1)]
     + [n + str(l) for n in ("h1", "h2", "o", "m", "dm", "dh2", "do", "dh1") for l in (0, 1)]
 )
 GROUP = {n: i for i, n in enumerate(dict.fromkeys(GROUPS))}
@@ -110,7 +109,7 @@
     pass
 
 
-def kernel(x_in, dz_in, wown, vin, idc, idr, lo_ref, gi_ref, gq_ref, go_ref, gu_ref, gd_ref, gv_ref, *scratch):
+def kernel(acts, cot, wq, wo, wu, wd, vectors, ids, fin_ref, fother_ref, lo_ref, gi_ref, gv_ref, *scratch):
     r = Refs()
     for name, ref in zip(SCRATCH, scratch):
         setattr(r, name, ref)
@@ -154,71 +153,122 @@
     def arrived(group, slot, dst):
         copy(group, slot, dst, dst, sib).wait_recv()
 
+    def local_start(group, slot, src, dst):
+        pltpu.make_async_copy(src, dst, ssem.at[GROUP[group], slot]).start()
+
+    def local_wait(group, slot, dst):
+        pltpu.make_async_copy(dst, dst, ssem.at[GROUP[group], slot]).wait()
+
+    def piece(t, which):
+        if t == "q":
+            return [
+                (wq.at[0, :, pl.ds(pl.multiple_of(n * 1024 + z * 256 + which * 128, 128), 128)], n * 128, 128)
+                for n in range(3)
+            ]
+        cols = pl.ds(pl.multiple_of(which * 512, 512), 512)
+        if t == "o":
+            return [(wo.at[0, :, cols], 0, 512)]
+        return [(wd.at[0, pl.ds(pl.multiple_of(z * 64, 64), 64), cols], 0, 512)]
+
+    def own(t):
+        return getattr(r, "own" + t)
+
+    local_start("x", 0, acts.at[c, 0], r.xin)
+
+    @pl.loop(0, 16)
+    def _(n):
+        col = pl.multiple_of(n * 256 + (z // 2) * 128, 128)
+        local_start("us", 0, wu.at[0, :, pl.ds(col, 128)], r.ustage.at[n])
+
+    for t in "qod":
+        for n, (src, at, width) in enumerate(piece(t, c)):
+            local_start("L" + t + "0", n, src, own(t).at[c, :, pl.ds(at, width)])
+    local_start("dz", 0, cot.at[c, 0], r.dzin)
+
     barrier = pltpu.get_barrier_semaphore()
     for dev in [sib] + [f(k) for f in (xpeer, ypeer, zpeer) for k in (1, 2, 3)]:
         pl.semaphore_signal(barrier, inc=1, device_id=dev, device_id_type=MESH)
+    rows8 = lax.broadcasted_iota(jnp.int32, (8, 128), 0)
+    lanes8 = lax.broadcasted_iota(jnp.int32, (8, 128), 1)
+    vown = vectors[0].astype(F32)
+    vown = jnp.concatenate([vown, vown], axis=0)
+    vown = jnp.concatenate([vown, vown], axis=1)
+    keep = jnp.logical_and(rows8 // 4 == c, lanes8 // 64 == p % 2)
+    r.vsend[6] = jnp.zeros((8, D), F32)
+    r.vsend[6, :, pl.ds(pl.multiple_of((p // 2) * 128, 128), 128)] = jnp.where(keep, vown, 0.0)
     pl.semaphore_wait(barrier, 10)
 
     def half(h, which):
         return pl.ds(pl.multiple_of(which * h, 128), h)
 
-    push("A", 0, wown.at[1 - c], r.own.at[c], sib)
-    own_copy = pltpu.make_async_copy(wown.at[c], r.own.at[c], ssem.at[GROUP["Alocal"], 0])
-    own_copy.start()
-    push("va", 0, vin, r.vrecv.at[0], sib)
+    for t in "qod":
+        for n, (src, at, width) in enumerate(piece(t, 1 - c)):
+            push("A" + t + "0", n, src, own(t).at[c, :, pl.ds(at, width)], sib)
+    push("va", 0, r.vsend.at[6], r.vrecv.at[0], sib)
+    local_wait("us", 0, r.ustage)
+
+    def up_half(which):
+        lower = lax.broadcasted_iota(jnp.int32, (64, 128), 1) < 64
+        tiles = []
+        for n in range(4):
+            first = r.ustage[8 * which + 2 * n].astype(F32)
+            second = r.ustage[8 * which + 2 * n + 1].astype(F32)
+            even = jnp.where(lower, first, pltpu.roll(second, 64, 1))
+            odd = jnp.where(lower, pltpu.roll(first, 64, 1), second)
+            tiles.append(jnp.where(z % 2 == 0, even, odd).astype(BF))
+        return jnp.concatenate(tiles, axis=1)
+
+    r.usend[...] = up_half(1 - c)
+    push("Au0", 0, r.usend, own("u").at[c], sib)
+    r.ownu[c] = up_half(c)
+
+    def own_ready(t):
+        for n, (_, at, width) in enumerate(piece(t, c) if t != "u" else [(None, 0, 512)]):
+            if t != "u":
+                local_wait("L" + t + "0", n, own(t).at[c, :, pl.ds(at, width)])
+            arrived("A" + t + "0", n, own(t).at[1 - c, :, pl.ds(at, width)])
 
     def wref(t):
         return getattr(r, "w" + t)
 
     def local_copy(t, l):
-        off, h, _ = TENSORS[t]
         return pltpu.make_async_copy(
-            r.own.at[l, :, pl.ds(off, h)],
-            wref(t).at[l, y, x, :, half(h, c)],
-            ssem.at[GROUP["Bl" + t + str(l)], 0],
+            own(t).at[l], wref(t).at[l, c, y, x], ssem.at[GROUP["Bl" + t + str(l)], 0]
         )
 
     def weight_b(t, l):
-        off, h, xfirst = TENSORS[t]
+        _, h, xfirst = TENSORS[t]
         peer = xpeer if xfirst else ypeer
-        for k in (1, 2, 3):
-            push(
-                "B" + t + str(l), k - 1,
-                r.own.at[l, :, pl.ds(off, h)],
-                wref(t).at[l, y, x, :, half(h, c)],
-                peer(k),
-            )
+        for k in (1, 3, 2):
+            push("B" + t + str(l), k - 1, own(t).at[l], wref(t).at[l, c, y, x], peer(k))
         local_copy(t, l).start()
 
     def weight_c(t, l):
         _, h, xfirst = TENSORS[t]
-        cols = half(h, c)
         local_copy(t, l).wait()
         for k in (1, 2, 3):
             if xfirst:
-                arrived("B" + t + str(l), k - 1, wref(t).at[l, y, (x + 4 - k) % 4, :, cols])
+                arrived("B" + t + str(l), k - 1, wref(t).at[l, c, y, (x + 4 - k) % 4])
             else:
-                arrived("B" + t + str(l), k - 1, wref(t).at[l, (y + 4 - k) % 4, x, :, cols])
-        line = wref(t).at[l, y, :, :, cols] if xfirst else wref(t).at[l, :, x, :, cols]
+                arrived("B" + t + str(l), k - 1, wref(t).at[l, c, (y + 4 - k) % 4, x])
+        line = wref(t).at[l, c, y] if xfirst else wref(t).at[l, c, :, x]
         peer = ypeer if xfirst else xpeer
-        for k in (1, 2, 3):
+        for k in (1, 3, 2):
             push("C" + t + str(l), k - 1, line, line, peer(k))
 
     def weight_d(t, l):
         _, h, xfirst = TENSORS[t]
-        cols = half(h, c)
         for k in (1, 2, 3):
             if xfirst:
-                line = wref(t).at[l, (y + 4 - k) % 4, :, :, cols]
+                line = wref(t).at[l, c, (y + 4 - k) % 4]
             else:
-                line = wref(t).at[l, :, (x + 4 - k) % 4, :, cols]
+                line = wref(t).at[l, c, :, (x + 4 - k) % 4]
             arrived("C" + t + str(l), k - 1, line)
-        mine = wref(t).at[l, :, :, :, cols]
+        mine = wref(t).at[l, c]
         push("D" + t + str(l), 0, mine, mine, sib)
 
     def weight_done(t, l):
-        _, h, _ = TENSORS[t]
-        arrived("D" + t + str(l), 0, wref(t).at[l, :, :, :, half(h, 1 - c)])
+        arrived("D" + t + str(l), 0, wref(t).at[l, 1 - c])
 
     def spread(group, at, slots, value, peer):
         r.vsend[at] = value
@@ -230,16 +280,19 @@
             arrived(group, k - 1, r.vrecv.at[slots + k - 1])
         return value + (r.vrecv[slots] + (r.vrecv[slots + 1] + r.vrecv[slots + 2]))
 
-    own_copy.wait()
-    arrived("A", 0, r.own.at[1 - c])
+    own_ready("q")
     weight_b("q", 0)
     arrived("va", 0, r.vrecv.at[0])
-    v = vin[...] + r.vrecv[0]
+    v = r.vsend[6] + r.vrecv[0]
     spread("vx", 0, 1, v, xpeer)
+    own_ready("o")
     weight_b("o", 0)
+    own_ready("u")
     weight_b("u", 0)
+    own_ready("d")
     weight_b("d", 0)
-    xhat0, _ = normalise(x_in[...].astype(F32))
+    local_wait("x", 0, r.xin)
+    xhat0, _ = normalise(r.xin[...].astype(F32))
     v = gathered("vx", 1, v)
     spread("vy", 1, 4, v, ypeer)
     weight_c("q", 0)
@@ -256,8 +309,20 @@
     def flat(value):
         return value.reshape(N, value.shape[-1])
 
-    def weight(t, l, cols):
-        return wref(t)[l, :, :, :, cols].reshape(D, -1)
+    def weight(t, l, j):
+        return wref(t)[l, j // 2, :, :, :, 256 * (j % 2) : 256 * (j % 2) + 256].reshape(D, 256)
+
+    def dot_weight_rows(rows, t, l, b):
+        _, h, _ = TENSORS[t]
+        first = dot_cols(rows[:, :h], wref(t)[l, 0, b].reshape(256, h))
+        return first + dot_cols(rows[:, h:], wref(t)[l, 1, b].reshape(256, h))
+
+    def image(axis):
+        row = ids[c]
+        place = lax.broadcasted_iota(jnp.int32, (N, 1) if axis == 0 else (1, N), axis)
+        one = jnp.sum((row < 1).astype(jnp.int32), axis=1, keepdims=True)
+        two = jnp.sum((row < 2).astype(jnp.int32), axis=1, keepdims=True)
+        return (place >= one).astype(jnp.int32) + (place >= two).astype(jnp.int32)
 
     lanes = lax.broadcasted_iota(jnp.int32, (1, 128), 1)
     low_lanes = lanes < 64
@@ -311,7 +376,7 @@
         def _():
             copy(group, k - 1, ref.at[blk], ref.at[blk], sib).wait_recv()
 
-    def attn_forward(l, xhat, xin, gap_a, gap_b):
+    def attn_forward(l, xhat, gap_a, gap_b):
         r.h1[l, z] = (xhat * gain(l, 0)).astype(BF)
         send_block("h1" + str(l), r.h1.at[l])
         gap_a()
@@ -321,12 +386,12 @@
         def _(k):
             blk = (z + 4 - k) % 4
             ag_wait("h1" + str(l), r.h1.at[l], k, blk)
-            for j in range(3):
-                cols = pl.ds(256 * j, 256)
-                r.qkv[l, blk, :, cols] = dot(r.h1[l, blk], weight("q", l, cols)).astype(BF)
+            for j in range(2):
+                w = wref("q")[l, j].reshape(D, 384)
+                r.qkv[l, blk, :, 384 * j : 384 * j + 384] = dot(r.h1[l, blk], w).astype(BF)
 
         gap_b()
-        same = idc[...] == idr[...]
+        same = image(0) == image(1)
 
         @pl.loop(0, 2)
         def _(pair):
@@ -359,7 +424,7 @@
             cols = pl.ds(256 * j, 256)
             acc = None
             for b in range(4):
-                w = wref("o")[l, b, :, :, cols].reshape(256, 256)
+                w = wref("o")[l, j // 2, b, :, :, 256 * (j % 2) : 256 * (j % 2) + 256].reshape(256, 256)
                 term = dot(r.ojoin[l, b], w)
                 acc = term if acc is None else acc + term
             r.a[l, :, cols] = acc
@@ -380,13 +445,13 @@
             ag_wait("h2" + str(l), r.h2.at[l], k, blk)
             for j in range(4):
                 cols = pl.ds(256 * j, 256)
-                u = dot(r.h2[l, blk], weight("u", l, cols))
+                u = dot(r.h2[l, blk], weight("u", l, j))
                 g, slope = gelu_parts(u)
                 r.g[l, blk, :, cols] = g.astype(BF)
                 r.slope[l, blk, :, cols] = slope.astype(BF)
 
             def make(j):
-                return dot(r.g[l, blk], weight("d", l, pl.ds(256 * j, 256)))
+                return dot(r.g[l, blk], weight("d", l, j))
 
             rs_put("m" + str(l), k, blk, make)
 
@@ -471,13 +536,12 @@
             blk = (z + 4 - k) % 4
             ag_wait("dm" + str(l), r.dm.at[l], k, blk)
             for b in range(4):
-                w = wref("d")[l, b].reshape(256, D)
                 cols = pl.ds(256 * b, 256)
-                grad = dot_cols(r.dm[l, blk], w)
+                grad = dot_weight_rows(r.dm[l, blk], "d", l, b)
                 r.du[blk, :, cols] = (grad * r.slope[l, blk, :, cols].astype(F32)).astype(BF)
 
             def make(b):
-                return dot_cols(r.du[blk], wref("u")[l, b].reshape(256, D))
+                return dot_weight_rows(r.du[blk], "u", l, b)
 
             rs_put("dh2" + str(l), k, blk, make)
 
@@ -498,8 +562,7 @@
         r.dy1[...] = dy1
         r.da[...] = (gain(l, 1) * dy1).astype(BF)
         for b in range(4):
-            w = wref("o")[l, b].reshape(256, D)
-            r.dosend[l, b] = dot_cols(r.da[...], w).astype(BF)
+            r.dosend[l, b] = dot_weight_rows(r.da[...], "o", l, b).astype(BF)
         for k in (1, 2, 3):
             push("do" + str(l), k - 1, r.dosend.at[l, (z + k) % 4], r.dojoin.at[l, z], zpeer(k))
         r.dojoin[l, z] = r.dosend[l, z]
@@ -546,7 +609,7 @@
             blk = (z + 4 - k) % 4
 
             def make(b):
-                return dot_cols(r.dqkv[blk], wref("q")[l, b].reshape(256, 768))
+                return dot_weight_rows(r.dqkv[blk], "q", l, b)
 
             rs_put("dh1" + str(l), k, blk, make)
 
@@ -568,15 +631,13 @@
         grad_second("q", l, left_q, right_q)
         grad_second("o", l, left_o, right_o)
         dh1 = rs_sum("dh1" + str(l))
-        xin = (r.x[...] if l == 0 else r.zout[0]).astype(F32)
+        xin = (r.xin[...] if l == 0 else r.zout[0]).astype(F32)
         dn, dg1 = norm_back(dh1, xin, gain(l, 0))
         r.vgrad[4 * l : 4 * l + 1, :] = dg1
         dx = (r.dy1[...] + dn).astype(BF)
         r.gout[l] = dx
         return dx
 
-    r.x[...] = x_in[...]
-
     def gap_f0a():
         weight_c("o", 0)
         weight_d("q", 0)
@@ -585,36 +646,32 @@
 
     def gap_f0b():
         weight_d("o", 0)
-        weight_b("q", 1)
-        weight_b("o", 1)
-
-    attn_forward(0, xhat0, None, gap_f0a, gap_f0b)
-    weight_d("u", 0)
-    weight_b("u", 1)
-    weight_b("d", 1)
-    out_proj(0, x_in[...].astype(F32))
+
+    attn_forward(0, xhat0, gap_f0a, gap_f0b)
+    weight_b("q", 1)
+    weight_b("o", 1)
+    out_proj(0, r.xin[...].astype(F32))
 
     def gap_f0c():
+        weight_d("u", 0)
         weight_d("d", 0)
         weight_c("q", 1)
         weight_c("o", 1)
+        weight_b("u", 1)
+        weight_b("d", 1)
 
     mlp_forward(0, gap_f0c)
     weight_d("q", 1)
+    weight_d("o", 1)
     weight_c("u", 1)
     weight_c("d", 1)
     finish_layer(0)
-    x1 = r.zout[0].astype(F32)
-    xhat1, _ = normalise(x1)
-
-    def gap_f1b():
-        weight_d("o", 1)
-
-    attn_forward(1, xhat1, None, lambda: None, gap_f1b)
-    weight_d("u", 1)
+    xhat1, _ = normalise(r.zout[0].astype(F32))
+    attn_forward(1, xhat1, lambda: None, lambda: None)
     out_proj(1, r.zout[0].astype(F32))
 
     def gap_f1c():
+        weight_d("u", 1)
         weight_d("d", 1)
 
     mlp_forward(1, gap_f1c)
@@ -622,7 +679,8 @@
     push("zo", 0, r.zout.at[1 - c], r.zother, sib)
 
     rs_sent("m0")
-    mlp_backward(1, dz_in[...].astype(F32), lambda: None, lambda: None)
+    local_wait("dz", 0, r.dzin)
+    mlp_backward(1, r.dzin[...].astype(F32), lambda: None, lambda: None)
     rs_sent("m1")
 
     def gap_b1b():
@@ -677,91 +735,82 @@
             grad_done(t, l)
     push("fo", 0, r.fin.at[1 - c], r.fother, sib)
     arrived("zo", 0, r.zother)
-    lo_ref[c] = r.zout[c, :TOK]
-    lo_ref[1 - c] = r.zother[:TOK]
+    lo_ref[c] = r.zout[c]
+    lo_ref[1 - c] = r.zother[...]
     arrived("go", 0, r.gother)
-    gi_ref[c] = r.gout[c, :TOK]
-    gi_ref[1 - c] = r.gother[:TOK]
+    gi_ref[c] = r.gout[c]
+    gi_ref[1 - c] = r.gother[...]
+    fin_ref[...] = r.fin[c]
     gv_ref[...] = gathered("gz", 14, gv)
-
-    def assemble(get, which):
-        for zz in range(4):
-            for t in range(3):
-                col = pl.multiple_of(t * 1024 + zz * 256 + which * 128, 128)
-                gq_ref[:, pl.ds(col, 128)] = get(zz, t * 128, 128).astype(F32)
-            gd_ref[64 * zz : 64 * zz + 64, half(512, which)] = get(zz, 1408, 512).astype(F32)
-        total = get(0, 384, 512).astype(F32)
-        for zz in range(1, 4):
-            total = total + get(zz, 384, 512).astype(F32)
-        go_ref[:, half(512, which)] = total
-        ups = [get(zz, 896, 512).astype(F32) for zz in range(4)]
-        for j in range(8):
-            row = jnp.concatenate([u[:, 64 * j : 64 * j + 64] for u in ups], axis=1)
-            gu_ref[:, pl.ds(pl.multiple_of((which * 8 + j) * 256, 256), 256)] = row
-
-    assemble(lambda zz, at, n: r.fin[c, zz, :, at : at + n], c)
     arrived("fo", 0, r.fother)
-    assemble(lambda zz, at, n: r.fother[zz, :, at : at + n], 1 - c)
+    fother_ref[...] = r.fother[...]
     rs_sent("dh20")
     rs_sent("dh10")
     for group in {k[0]: None for k in list(pending)}:
         sent(group)
 
 
+def assemble(fin, fother, lo, gi, gv, lo_ref, gi_ref, gq_ref, go_ref, gu_ref, gd_ref, gv_ref):
+    c = lax.axis_index("section")
+    p = lax.axis_index("shard")
+    for m in range(2):
+        lo_ref[0, m, 0] = lo[m]
+        gi_ref[0, m, 0] = gi[m]
+    both = gv[:, pl.ds(pl.multiple_of((p // 2) * 128, 128), 128)]
+    both = jnp.where(c == 0, both[:4], both[4:])
+    gv_ref[0] = jnp.where(p % 2 == 0, both[:, :64], both[:, 64:])
+    for ref, which in ((fin, c), (fother, 1 - c)):
+        wide = pl.ds(pl.multiple_of(which * 512, 512), 512)
+        for zz in range(4):
+            for t in range(3):
+                col = pl.multiple_of(t * 1024 + zz * 256 + which * 128, 128)
+                gq_ref[0, :, pl.ds(col, 128)] = ref[zz, :, t * 128 : t * 128 + 128].astype(F32)
+            gd_ref[0, 64 * zz : 64 * zz + 64, wide] = ref[zz, :, 1408:1920].astype(F32)
+        total = ref[0, :, 384:896].astype(F32)
+        for zz in range(1, 4):
+            total = total + ref[zz, :, 384:896].astype(F32)
+        go_ref[0, :, wide] = total
+        ups = [ref[zz, :, 896:1408].astype(F32) for zz in range(4)]
+        for n in range(8):
+            row = jnp.concatenate([u[:, 64 * n : 64 * n + 64] for u in ups], axis=1)
+            gu_ref[0, :, pl.ds(pl.multiple_of((which * 8 + n) * 256, 256), 256)] = row
+
+
 def local(acts_in, cotangent, qkv_weight, out_weight, up_weight, down_weight, vectors, image_ids):
-    c = lax.axis_index("section")
-    z = lax.axis_index("seq")
-    p = lax.axis_index("shard")
-
-    def halves(w):
-        n = w.shape[1] // 2
-        return w.reshape(64, 2, n).transpose(1, 0, 2)
-
-    qkv = lax.dynamic_index_in_dim(qkv_weight[0].reshape(64, 3, 4, 2, 128), z, 2, False)
-    qkv = qkv.transpose(2, 0, 1, 3).reshape(2, 64, 384)
-    up = lax.dynamic_index_in_dim(up_weight[0].reshape(64, 16, 4, 64), z, 2, False).reshape(64, D)
-    down = lax.dynamic_index_in_dim(down_weight[0].reshape(4, 64, D), z, 0, False)
-    wown = jnp.concatenate([qkv, halves(out_weight[0]), halves(up), halves(down)], axis=2)
-    vin = lax.dynamic_update_slice(
-        jnp.zeros((8, D), F32), vectors[0].astype(F32), (4 * c, 64 * p)
-    )
-
-    def mine(a):
-        a = lax.dynamic_index_in_dim(a, c, 0, False)[0]
-        return jnp.pad(a, ((0, ROWS - TOK), (0, 0)))
-
-    ids = lax.dynamic_index_in_dim(image_ids, c, 0, False)[0]
-    ids = jnp.pad(ids.reshape(4, TOK), ((0, 0), (0, ROWS - TOK)), constant_values=-1).reshape(N)
     vmem = pl.BlockSpec(memory_space=pltpu.VMEM)
+    hbm = pl.BlockSpec(memory_space=pl.ANY)
     out = pl.pallas_call(
         kernel,
         out_shape=(
-            jax.ShapeDtypeStruct((2, TOK, D), BF),
-            jax.ShapeDtypeStruct((2, TOK, D), BF),
-            jax.ShapeDtypeStruct((64, 3072), F32),
-            jax.ShapeDtypeStruct((64, D), F32),
-            jax.ShapeDtypeStruct((64, 4096), F32),
-            jax.ShapeDtypeStruct((256, D), F32),
+            jax.ShapeDtypeStruct((4, 64, HALF), BF),
+            jax.ShapeDtypeStruct((4, 64, HALF), BF),
+            jax.ShapeDtypeStruct((2, ROWS, D), BF),
+            jax.ShapeDtypeStruct((2, ROWS, D), BF),
             jax.ShapeDtypeStruct((8, D), F32),
         ),
-        in_specs=[vmem, vmem, pl.BlockSpec(memory_space=pl.ANY), vmem, vmem, vmem],
-        out_specs=(vmem,) * 7,
+        in_specs=[hbm] * 6 + [vmem] * 2,
+        out_specs=(vmem,) * 5,
         scratch_shapes=[pltpu.VMEM(s, t) for s, t in SCRATCH.values()]
         + [pltpu.SemaphoreType.DMA((len(GROUP), 3)), pltpu.SemaphoreType.DMA((len(GROUP), 3))],
         compiler_params=pltpu.CompilerParams(
             collective_id=0, has_side_effects=True, vmem_limit_bytes=64 * 1024 * 1024 - 65536
         ),
-    )(mine(acts_in), mine(cotangent), wown, vin, ids[:, None], ids[None, :])
-    gv = lax.dynamic_slice(out[6], (4 * c, 64 * p), (4, 64))
-    return (
-        out[0][None, :, None],
-        out[1][None, :, None],
-        out[2][None],
-        out[3][None],
-        out[4][None],
-        out[5][None],
-        gv[None],
-    )
+    )(acts_in, cotangent, qkv_weight, out_weight, up_weight, down_weight, vectors, image_ids)
+    return pl.pallas_call(
+        assemble,
+        out_shape=(
+            jax.ShapeDtypeStruct((1, 2, 1, ROWS, D), BF),
+            jax.ShapeDtypeStruct((1, 2, 1, ROWS, D), BF),
+            jax.ShapeDtypeStruct((1, 64, 3072), F32),
+            jax.ShapeDtypeStruct((1, 64, D), F32),
+            jax.ShapeDtypeStruct((1, 64, 4096), F32),
+            jax.ShapeDtypeStruct((1, 256, D), F32),
+            jax.ShapeDtypeStruct((1, 4, 64), F32),
+        ),
+        in_specs=[vmem] * 5,
+        out_specs=(vmem,) * 7,
+        compiler_params=pltpu.CompilerParams(vmem_limit_bytes=32 * 1024 * 1024),
+    )(*out)
 
 
 def solution(mesh):

time: 240 us -> 221 us (0.921)
  local copies, waits for them, and re-layouts: 20.1 us -> 5.08 us
  Pallas kernels: 218 us -> 215 us
    unnamed x28 -> x10, local copies, waits for them, and re-layouts: 9.89 us -> 5.08 us
    another operation x8 -> x0, local copies, waits for them, and re-layouts: 4.14 us -> none  [the longest x3 1.19 us: halves(): return w.reshape(64, 2, n).transpose(1, 0, 2)]
    dynamic_slice x5 -> x0, local copies, waits for them, and re-layouts: 2.84 us -> none  [the longest x1 1.73 us: local(): lax.dynamic_index_in_dim(up_weight[0].reshape(64, 16, 4, 64), z, 2, False)]
    pallas_call x1 -> x2, Pallas kernels: 218 us -> 215 us  [the longest x1 213 us: local(): pl.pallas_call(kernel, out_shape=(jax.ShapeDtypeStruct((4, 64, HALF), BF)...]
where the time goes in v3:
time: 221 us
  Pallas kernels  215 us (97%)
  local copies, waits for them, and re-layouts  5.08 us (2%)
    pallas_call x1, Pallas kernels, local(): pl.pallas_call(kernel, out_shape=(jax.ShapeDtypeStruct((4, 64, HALF), BF)...  213 us
    unnamed x10, local copies, waits for them, and re-layouts  5.08 us

profile of v3, /device:TPU:1, one launch (start us, length us, event | category | flops | bytes accessed | tf_op | source)
XLA Modules:
  0.0 221.0 jit_solution(5646938987191637753)
XLA Ops:
  0.6 213.2 %shard_map.135 = (bf16[4,64,1920]{2,1,0:T(8,128)(2,1)}, bf16[4,64,1920]{2,1,0:T(8,128)(2,1)}, bf16[2,72,1024]{2,1,0:T(8,128)(2,1)}, bf16[2,72,1024]{2,1,0:T(8,128)(2,1)}, f32[8,1024]{1,0:T(8,128)}) custom-call(bf16[2,1,72,1024]{3,2,1,0:T(8,128)(2,1)} %acts.1, bf16[2,1,72,1024]{3,2,1,0:T(8,128)(2,1)} %cot.1, bf16[1,64,3072]{2,1,0:T(8,128)(2,1)} %wq.1, ...), custom_call_target="tpu_custom_call" | custom-call | tf_op jit(solution)/shard_map/pallas_call | solution.py:782
  213.8 0.0 copy-start
  213.8 1.2 copy-done
  215.0 0.0 copy-start.1
  215.0 1.2 copy-done.1
  216.2 0.0 copy-start.2
  216.2 1.0 copy-done.2
  217.2 0.0 copy-start.3
  217.2 1.0 copy-done.3
  218.1 0.0 copy-start.4
  218.1 0.8 copy-done.4
  218.9 2.1 shard_map.136
Async XLA Ops:
  213.8 1.2 copy-start
  215.0 1.2 copy-start.1
  216.2 1.0 copy-start.2
  217.2 1.0 copy-start.3
  218.1 0.8 copy-start.4

commit v4 on v3

--- a/solution.py
+++ b/solution.py
@@ -53,6 +53,8 @@
 
 
 SCRATCH = dict(
+    vectors=((1, 4, 64), BF),
+    ids=((1, N), jnp.int32),
     ustage=((16, 64, 128), BF),
     usend=((64, 512), BF),
     xin=((ROWS, D), BF),
@@ -64,6 +66,7 @@
     h1=((2, 4, ROWS, D), BF),
     qkv=((2, 4, ROWS, 768), BF),
     prob=((2, 4, N, N), BF),
+    wqt=((2, 768, D), BF),
     osend=((2, 4, ROWS, 256), BF),
     ojoin=((2, 4, ROWS, 256), BF),
     a=((2, ROWS, D), F32),
@@ -84,22 +87,20 @@
     dqkv=((4, ROWS, 768), BF),
     zout=((2, ROWS, D), BF),
     gout=((2, ROWS, D), BF),
-    zother=((ROWS, D), BF),
-    gother=((ROWS, D), BF),
     fin=((2, 4, 64, HALF), BF),
-    fother=((4, 64, HALF), BF),
 )
 for _t, (_, _h, _x) in TENSORS.items():
     SCRATCH["own" + _t] = ((2, 64, _h), BF)
     SCRATCH["w" + _t] = ((2, 2, 4, 4, 64, _h), BF)
+    SCRATCH["lt" + _t] = ((4, 256, 4 * ROWS), BF)
     SCRATCH["gs" + _t] = ((4, 4, 64, _h), BF)
     SCRATCH["ra" + _t] = ((2, 4, 4, 64, _h), BF)
     SCRATCH["rb" + _t] = ((2, 3, 4, 64, _h), BF)
     SCRATCH["rc" + _t] = ((2, 3, 64, _h), BF)
 
 GROUPS = (
-    ["x", "dz", "us", "va", "vx", "vy", "ga", "gx", "gy", "gz", "zo", "go", "fo"]
-    + [n + t + str(l) for n in ("A", "L", "B", "Bl", "C", "D", "ga", "gb", "gc", "ge") for t in "qoud" for l in (0, 1)]
+    ["x", "dz", "us", "vin", "iin", "out", "out2", "out3", "va", "vx", "vy", "ga", "gx", "gy", "gz", "zo", "go", "fo"]
+    + [n + t + str(l) for n in ("A", "L", "B", "Bl", "C", "E", "D", "ga", "gb", "gc", "ge") for t in "qoud" for l in (0, 1)]
     + [n + str(l) for n in ("h1", "h2", "o", "m", "dm", "dh2", "do", "dh1") for l in (0, 1)]
 )
 GROUP = {n: i for i, n in enumerate(dict.fromkeys(GROUPS))}
@@ -109,7 +110,7 @@
     pass
 
 
-def kernel(acts, cot, wq, wo, wu, wd, vectors, ids, fin_ref, fother_ref, lo_ref, gi_ref, gv_ref, *scratch):
+def kernel(acts, cot, wq, wo, wu, wd, vectors_in, ids_in, fin_ref, fother_ref, lo_ref, gi_ref, gv_ref, *scratch):
     r = Refs()
     for name, ref in zip(SCRATCH, scratch):
         setattr(r, name, ref)
@@ -173,6 +174,8 @@
     def own(t):
         return getattr(r, "own" + t)
 
+    local_start("vin", 0, vectors_in, r.vectors)
+    local_start("iin", 0, ids_in.at[c], r.ids)
     local_start("x", 0, acts.at[c, 0], r.xin)
 
     @pl.loop(0, 16)
@@ -190,7 +193,8 @@
         pl.semaphore_signal(barrier, inc=1, device_id=dev, device_id_type=MESH)
     rows8 = lax.broadcasted_iota(jnp.int32, (8, 128), 0)
     lanes8 = lax.broadcasted_iota(jnp.int32, (8, 128), 1)
-    vown = vectors[0].astype(F32)
+    local_wait("vin", 0, r.vectors)
+    vown = r.vectors[0].astype(F32)
     vown = jnp.concatenate([vown, vown], axis=0)
     vown = jnp.concatenate([vown, vown], axis=1)
     keep = jnp.logical_and(rows8 // 4 == c, lanes8 // 64 == p % 2)
@@ -253,17 +257,26 @@
                 arrived("B" + t + str(l), k - 1, wref(t).at[l, c, (y + 4 - k) % 4, x])
         line = wref(t).at[l, c, y] if xfirst else wref(t).at[l, c, :, x]
         peer = ypeer if xfirst else xpeer
-        for k in (1, 3, 2):
+        for k in (1, 3):
             push("C" + t + str(l), k - 1, line, line, peer(k))
 
+    def line_of(t, l, back, part=None):
+        if TENSORS[t][2]:
+            ref = wref(t).at[l, c, (y + 4 - back) % 4]
+            return ref if part is None else ref.at[pl.ds(2 * part, 2)]
+        if part is None:
+            return wref(t).at[l, c, :, (x + 4 - back) % 4]
+        return wref(t).at[l, c, pl.ds(2 * part, 2), (x + 4 - back) % 4]
+
+    def weight_e(t, l):
+        peer = ypeer if TENSORS[t][2] else xpeer
+        for k, part in ((1, 0), (3, 1)):
+            arrived("C" + t + str(l), k - 1, line_of(t, l, k))
+            push("E" + t + str(l), k - 1, line_of(t, l, k, part), line_of(t, l, k, part), peer(k))
+
     def weight_d(t, l):
-        _, h, xfirst = TENSORS[t]
-        for k in (1, 2, 3):
-            if xfirst:
-                line = wref(t).at[l, c, (y + 4 - k) % 4]
-            else:
-                line = wref(t).at[l, c, :, (x + 4 - k) % 4]
-            arrived("C" + t + str(l), k - 1, line)
+        for k, part in ((1, 0), (3, 1)):
+            arrived("E" + t + str(l), k - 1, line_of(t, l, 2, part))
         mine = wref(t).at[l, c]
         push("D" + t + str(l), 0, mine, mine, sib)
 
@@ -292,6 +305,7 @@
     own_ready("d")
     weight_b("d", 0)
     local_wait("x", 0, r.xin)
+    local_wait("iin", 0, r.ids)
     xhat0, _ = normalise(r.xin[...].astype(F32))
     v = gathered("vx", 1, v)
     spread("vy", 1, 4, v, ypeer)
@@ -312,13 +326,30 @@
     def weight(t, l, j):
         return wref(t)[l, j // 2, :, :, :, 256 * (j % 2) : 256 * (j % 2) + 256].reshape(D, 256)
 
-    def dot_weight_rows(rows, t, l, b):
-        _, h, _ = TENSORS[t]
-        first = dot_cols(rows[:, :h], wref(t)[l, 0, b].reshape(256, h))
-        return first + dot_cols(rows[:, h:], wref(t)[l, 1, b].reshape(256, h))
+    def turn(t, l):
+        for n in "CED":
+            sent(n + t + str(l))
+
+        def tile(a, b):
+            return wref(t).at[l, b // 2, a, :, :, pl.ds(256 * (b % 2), 256)]
+
+        for a in range(4):
+            for b in range(a, 4):
+                upper = tile(a, b)[...].reshape(256, 256)
+                if a < b:
+                    lower = tile(b, a)[...].reshape(256, 256)
+                    tile(a, b)[...] = lower.T.reshape(4, 64, 256)
+                tile(b, a)[...] = upper.T.reshape(4, 64, 256)
+
+    def turn_qkv(l):
+        for h in range(2):
+            for n in range(3):
+                for a in range(4):
+                    w = wref("q")[l, h, a, :, :, 128 * n : 128 * n + 128].reshape(256, 128)
+                    r.wqt[l, 384 * h + 128 * n : 384 * h + 128 * n + 128, 256 * a : 256 * a + 256] = w.T
 
     def image(axis):
-        row = ids[c]
+        row = r.ids[...]
         place = lax.broadcasted_iota(jnp.int32, (N, 1) if axis == 0 else (1, N), axis)
         one = jnp.sum((row < 1).astype(jnp.int32), axis=1, keepdims=True)
         two = jnp.sum((row < 2).astype(jnp.int32), axis=1, keepdims=True)
@@ -462,22 +493,25 @@
 
     def grad_first(t, l, left, right):
         _, h, _ = TENSORS[t]
-        gs = getattr(r, "gs" + t)
+        gs, lt = getattr(r, "gs" + t), getattr(r, "lt" + t)
 
         @pl.loop(0, 4)
         def _(b):
-            gs[b] = dot_rows(left(b), right(half(h, 1 - c))).astype(BF).reshape(4, 64, h)
+            turned = left(b).T
+            lt[b, :, : turned.shape[1]] = turned
+            gs[b] = dot(turned, right(half(h, 1 - c))).astype(BF).reshape(4, 64, h)
 
         push("ga" + t + str(l), 0, gs, getattr(r, "ra" + t).at[l], sib)
 
-    def grad_second(t, l, left, right):
+    def grad_second(t, l, right):
         _, h, xfirst = TENSORS[t]
-        ra = getattr(r, "ra" + t)
+        ra, lt = getattr(r, "ra" + t), getattr(r, "lt" + t)
+        depth = ROWS if t == "o" else N
         arrived("ga" + t + str(l), 0, ra.at[l])
 
         @pl.loop(0, 4)
         def _(b):
-            val = dot_rows(left(b), right(half(h, c))).reshape(4, 64, h)
+            val = dot(lt[b, :, :depth], right(half(h, c))).reshape(4, 64, h)
             ra[l, b] = (val + ra[l, b].astype(F32)).astype(BF)
 
         for k in (1, 2, 3):
@@ -537,11 +571,11 @@
             ag_wait("dm" + str(l), r.dm.at[l], k, blk)
             for b in range(4):
                 cols = pl.ds(256 * b, 256)
-                grad = dot_weight_rows(r.dm[l, blk], "d", l, b)
+                grad = dot(r.dm[l, blk], weight("d", l, b))
                 r.du[blk, :, cols] = (grad * r.slope[l, blk, :, cols].astype(F32)).astype(BF)
 
             def make(b):
-                return dot_weight_rows(r.du[blk], "u", l, b)
+                return dot(r.du[blk], weight("u", l, b))
 
             rs_put("dh2" + str(l), k, blk, make)
 
@@ -562,13 +596,13 @@
         r.dy1[...] = dy1
         r.da[...] = (gain(l, 1) * dy1).astype(BF)
         for b in range(4):
-            r.dosend[l, b] = dot_weight_rows(r.da[...], "o", l, b).astype(BF)
+            r.dosend[l, b] = dot(r.da[...], weight("o", l, b)).astype(BF)
         for k in (1, 2, 3):
             push("do" + str(l), k - 1, r.dosend.at[l, (z + k) % 4], r.dojoin.at[l, z], zpeer(k))
         r.dojoin[l, z] = r.dosend[l, z]
         r.vgrad[4 * l + 1 : 4 * l + 2, :] = jnp.sum(dy1 * r.a[l], axis=0, keepdims=True)
-        grad_second("d", l, tile(g_l), cols_of(dm_l))
-        grad_second("u", l, tile(h2_l), cols_of(r.du))
+        grad_second("d", l, cols_of(dm_l))
+        grad_second("u", l, cols_of(r.du))
 
     def attn_backward(l, gap_a, gap_b):
         gap_a()
@@ -609,7 +643,7 @@
             blk = (z + 4 - k) % 4
 
             def make(b):
-                return dot_weight_rows(r.dqkv[blk], "q", l, b)
+                return dot(r.dqkv[blk], r.wqt[l, :, 256 * b : 256 * b + 256])
 
             rs_put("dh1" + str(l), k, blk, make)
 
@@ -628,8 +662,8 @@
         grad_first("q", l, left_q, right_q)
         grad_first("o", l, left_o, right_o)
         gap_b()
-        grad_second("q", l, left_q, right_q)
-        grad_second("o", l, left_o, right_o)
+        grad_second("q", l, right_q)
+        grad_second("o", l, right_o)
         dh1 = rs_sum("dh1" + str(l))
         xin = (r.xin[...] if l == 0 else r.zout[0]).astype(F32)
         dn, dg1 = norm_back(dh1, xin, gain(l, 0))
@@ -640,9 +674,11 @@
 
     def gap_f0a():
         weight_c("o", 0)
-        weight_d("q", 0)
+        weight_e("q", 0)
+        weight_e("o", 0)
         weight_c("u", 0)
         weight_c("d", 0)
+        weight_d("q", 0)
 
     def gap_f0b():
         weight_d("o", 0)
@@ -650,33 +686,51 @@
     attn_forward(0, xhat0, gap_f0a, gap_f0b)
     weight_b("q", 1)
     weight_b("o", 1)
+    turn_qkv(0)
+    weight_e("u", 0)
+    weight_e("d", 0)
     out_proj(0, r.xin[...].astype(F32))
 
     def gap_f0c():
+        weight_c("q", 1)
+        weight_c("o", 1)
+        turn("o", 0)
         weight_d("u", 0)
         weight_d("d", 0)
-        weight_c("q", 1)
-        weight_c("o", 1)
         weight_b("u", 1)
         weight_b("d", 1)
 
     mlp_forward(0, gap_f0c)
+    weight_e("q", 1)
+    weight_e("o", 1)
+    weight_c("u", 1)
+    weight_c("d", 1)
+    turn("u", 0)
     weight_d("q", 1)
     weight_d("o", 1)
-    weight_c("u", 1)
-    weight_c("d", 1)
+    turn("d", 0)
     finish_layer(0)
     xhat1, _ = normalise(r.zout[0].astype(F32))
-    attn_forward(1, xhat1, lambda: None, lambda: None)
+
+    def gap_f1b():
+        weight_e("u", 1)
+        weight_e("d", 1)
+
+    attn_forward(1, xhat1, lambda: None, gap_f1b)
+    turn_qkv(1)
     out_proj(1, r.zout[0].astype(F32))
 
     def gap_f1c():
+        turn("o", 1)
         weight_d("u", 1)
         weight_d("d", 1)
 
     mlp_forward(1, gap_f1c)
+    turn("u", 1)
+    turn("d", 1)
     finish_layer(1)
-    push("zo", 0, r.zout.at[1 - c], r.zother, sib)
+    push("zo", 0, r.zout.at[1 - c], lo_ref.at[c], sib)
+    local_start("out", 0, r.zout.at[c], lo_ref.at[c])
 
     rs_sent("m0")
     local_wait("dz", 0, r.dzin)
@@ -713,7 +767,8 @@
 
     attn_backward(0, gap_b0c, gap_b0d)
 
-    push("go", 0, r.gout.at[1 - c], r.gother, sib)
+    push("go", 0, r.gout.at[1 - c], gi_ref.at[c], sib)
+    local_start("out", 1, r.gout.at[c], gi_ref.at[c])
     gv = r.vgrad[...]
     r.vsend[2] = gv
     push("ga", 0, r.vsend.at[2], r.vrecv.at[7], sib)
@@ -733,33 +788,38 @@
     for l in (1, 0):
         for t in "duqo":
             grad_done(t, l)
-    push("fo", 0, r.fin.at[1 - c], r.fother, sib)
-    arrived("zo", 0, r.zother)
-    lo_ref[c] = r.zout[c]
-    lo_ref[1 - c] = r.zother[...]
-    arrived("go", 0, r.gother)
-    gi_ref[c] = r.gout[c]
-    gi_ref[1 - c] = r.gother[...]
-    fin_ref[...] = r.fin[c]
-    gv_ref[...] = gathered("gz", 14, gv)
-    arrived("fo", 0, r.fother)
-    fother_ref[...] = r.fother[...]
+    push("fo", 0, r.fin.at[1 - c], fother_ref, sib)
+    local_start("out", 2, r.fin.at[c], fin_ref)
+    r.vgrad[...] = gathered("gz", 14, gv)
+    local_start("out2", 0, r.vgrad, gv_ref)
+    arrived("zo", 0, lo_ref.at[1 - c])
+    arrived("go", 0, gi_ref.at[1 - c])
+    arrived("fo", 0, fother_ref)
+    local_wait("out", 0, lo_ref.at[c])
+    local_wait("out", 1, gi_ref.at[c])
+    local_wait("out", 2, fin_ref)
+    local_wait("out2", 0, gv_ref)
     rs_sent("dh20")
     rs_sent("dh10")
     for group in {k[0]: None for k in list(pending)}:
         sent(group)
 
 
-def assemble(fin, fother, lo, gi, gv, lo_ref, gi_ref, gq_ref, go_ref, gu_ref, gd_ref, gv_ref):
+def assemble(fin_in, fother_in, lo, gi, gv_in, lo_ref, gi_ref, gq_ref, go_ref, gu_ref, gd_ref, gv_ref, fin, fother, gv, sem):
     c = lax.axis_index("section")
     p = lax.axis_index("shard")
-    for m in range(2):
-        lo_ref[0, m, 0] = lo[m]
-        gi_ref[0, m, 0] = gi[m]
+    pairs = [(fin_in, fin), (fother_in, fother), (gv_in, gv)]
+    pairs += [(lo.at[m], lo_ref.at[0, m, 0]) for m in range(2)]
+    pairs += [(gi.at[m], gi_ref.at[0, m, 0]) for m in range(2)]
+    moves = [pltpu.make_async_copy(a, b, sem.at[n]) for n, (a, b) in enumerate(pairs)]
+    for move in moves:
+        move.start()
+    moves[2].wait()
     both = gv[:, pl.ds(pl.multiple_of((p // 2) * 128, 128), 128)]
     both = jnp.where(c == 0, both[:4], both[4:])
     gv_ref[0] = jnp.where(p % 2 == 0, both[:, :64], both[:, 64:])
-    for ref, which in ((fin, c), (fother, 1 - c)):
+    for n, ref, which in ((0, fin, c), (1, fother, 1 - c)):
+        moves[n].wait()
         wide = pl.ds(pl.multiple_of(which * 512, 512), 512)
         for zz in range(4):
             for t in range(3):
@@ -774,6 +834,8 @@
         for n in range(8):
             row = jnp.concatenate([u[:, 64 * n : 64 * n + 64] for u in ups], axis=1)
             gu_ref[0, :, pl.ds(pl.multiple_of((which * 8 + n) * 256, 256), 256)] = row
+    for move in moves[3:]:
+        move.wait()
 
 
 def local(acts_in, cotangent, qkv_weight, out_weight, up_weight, down_weight, vectors, image_ids):
@@ -788,8 +850,8 @@
             jax.ShapeDtypeStruct((2, ROWS, D), BF),
             jax.ShapeDtypeStruct((8, D), F32),
         ),
-        in_specs=[hbm] * 6 + [vmem] * 2,
-        out_specs=(vmem,) * 5,
+        in_specs=[hbm] * 8,
+        out_specs=(hbm,) * 5,
         scratch_shapes=[pltpu.VMEM(s, t) for s, t in SCRATCH.values()]
         + [pltpu.SemaphoreType.DMA((len(GROUP), 3)), pltpu.SemaphoreType.DMA((len(GROUP), 3))],
         compiler_params=pltpu.CompilerParams(
@@ -807,8 +869,14 @@
             jax.ShapeDtypeStruct((1, 256, D), F32),
             jax.ShapeDtypeStruct((1, 4, 64), F32),
         ),
-        in_specs=[vmem] * 5,
-        out_specs=(vmem,) * 7,
+        in_specs=[hbm] * 5,
+        out_specs=(hbm,) * 2 + (vmem,) * 5,
+        scratch_shapes=[
+            pltpu.VMEM((4, 64, HALF), BF),
+            pltpu.VMEM((4, 64, HALF), BF),
+            pltpu.VMEM((8, D), F32),
+            pltpu.SemaphoreType.DMA((7,)),
+        ],
         compiler_params=pltpu.CompilerParams(vmem_limit_bytes=32 * 1024 * 1024),
     )(*out)
 

time: 221 us -> 215 us (0.973)
  Pallas kernels: 215 us -> 209 us
    pallas_call x1, Pallas kernels: 213 us -> 206 us  [local(): pl.pallas_call(kernel, out_shape=(jax.ShapeDtypeStruct((4, 64, HALF), BF)...]
where the time goes in v4:
time: 215 us
  Pallas kernels  209 us (97%)
  local copies, waits for them, and re-layouts  5.08 us (2%)
    pallas_call x1, Pallas kernels, local(): pl.pallas_call(kernel, out_shape=(jax.ShapeDtypeStruct((4, 64, HALF), BF)...  206 us
    unnamed x10, local copies, waits for them, and re-layouts  5.08 us

profile of v4, /device:TPU:1, one launch (start us, length us, event | category | flops | bytes accessed | tf_op | source)
XLA Modules:
  0.0 214.8 jit_solution(7366423244350103573)
XLA Ops:
  0.6 205.7 %shard_map.135 = (bf16[4,64,1920]{2,1,0:T(8,128)(2,1)}, bf16[4,64,1920]{2,1,0:T(8,128)(2,1)}, bf16[2,72,1024]{2,1,0:T(8,128)(2,1)}, bf16[2,72,1024]{2,1,0:T(8,128)(2,1)}, f32[8,1024]{1,0:T(8,128)}) custom-call(bf16[2,1,72,1024]{3,2,1,0:T(8,128)(2,1)} %acts.1, bf16[2,1,72,1024]{3,2,1,0:T(8,128)(2,1)} %cot.1, bf16[1,64,3072]{2,1,0:T(8,128)(2,1)} %wq.1, ...), custom_call_target="tpu_custom_call" | custom-call | tf_op jit(solution)/shard_map/pallas_call | solution.py:844
  206.4 0.0 copy-start
  206.4 1.2 copy-done
  207.6 0.0 copy-start.1
  207.6 1.2 copy-done.1
  208.8 0.0 copy-start.2
  208.8 1.0 copy-done.2
  209.7 0.0 copy-start.3
  209.7 1.0 copy-done.3
  210.7 0.0 copy-start.4
  210.7 0.8 copy-done.4
  211.4 3.2 %shard_map.136 = (bf16[1,2,1,72,1024]{4,3,2,1,0:T(8,128)(2,1)}, bf16[1,2,1,72,1024]{4,3,2,1,0:T(8,128)(2,1)}, f32[1,64,3072]{2,1,0:T(8,128)}, f32[1,64,1024]{2,1...) custom-call(bf16[4,64,1920]{2,1,0:T(8,128)(2,1)S(1)} %copy-done, ...), custom_call_target="tpu_custom_call" | custom-call | tf_op jit(solution)/shard_map/pallas_call | solution.py:861
Async XLA Ops:
  206.4 1.2 copy-start
  207.6 1.2 copy-start.1
  208.8 1.0 copy-start.2
  209.7 1.0 copy-start.3
  210.7 0.8 copy-start.4

commit v5 on v4

--- a/solution.py
+++ b/solution.py
@@ -57,7 +57,8 @@
     ids=((1, N), jnp.int32),
     ustage=((16, 64, 128), BF),
     usend=((64, 512), BF),
-    xin=((ROWS, D), BF),
+    xall=((4, ROWS, D), BF),
+    rdq=((16, 64, 384), BF),
     dzin=((ROWS, D), BF),
     vsend=((7, 8, D), F32),
     vrecv=((17, 8, D), F32),
@@ -103,6 +104,8 @@
     + [n + t + str(l) for n in ("A", "L", "B", "Bl", "C", "E", "D", "ga", "gb", "gc", "ge") for t in "qoud" for l in (0, 1)]
     + [n + str(l) for n in ("h1", "h2", "o", "m", "dm", "dh2", "do", "dh1") for l in (0, 1)]
 )
+ORDER = (1, 3, 4, 12, 5, 7, 13, 15, 2, 8, 6, 14, 9, 11, 10)
+DIRECT = {"Q": 0, "R": 1}
 GROUP = {n: i for i, n in enumerate(dict.fromkeys(GROUPS))}
 
 
@@ -114,7 +117,7 @@
     r = Refs()
     for name, ref in zip(SCRATCH, scratch):
         setattr(r, name, ref)
-    ssem, rsem = scratch[len(SCRATCH) :]
+    ssem, rsem, ssem16, rsem16 = scratch[len(SCRATCH) :]
     c = lax.axis_index("section")
     z = lax.axis_index("seq")
     p = lax.axis_index("shard")
@@ -130,14 +133,21 @@
     def ypeer(k):
         return {"shard": ((y + k) % 4) * 4 + x}
 
+    def any_peer(n):
+        return {"shard": ((y + n // 4) % 4) * 4 + (x + n % 4) % 4}
+
     pending = {}
 
     def copy(group, slot, src, dst, dev):
+        if group in DIRECT:
+            at, send, recv = DIRECT[group], ssem16, rsem16
+        else:
+            at, send, recv = GROUP[group], ssem, rsem
         return pltpu.make_async_remote_copy(
             src_ref=src,
             dst_ref=dst,
-            send_sem=ssem.at[GROUP[group], slot],
-            recv_sem=rsem.at[GROUP[group], slot],
+            send_sem=send.at[at, slot],
+            recv_sem=recv.at[at, slot],
             device_id=dev,
             device_id_type=MESH,
         )
@@ -176,7 +186,7 @@
 
     local_start("vin", 0, vectors_in, r.vectors)
     local_start("iin", 0, ids_in.at[c], r.ids)
-    local_start("x", 0, acts.at[c, 0], r.xin)
+    local_start("x", 0, acts.at[c, 0], r.xall.at[z])
 
     @pl.loop(0, 16)
     def _(n):
@@ -189,7 +199,7 @@
     local_start("dz", 0, cot.at[c, 0], r.dzin)
 
     barrier = pltpu.get_barrier_semaphore()
-    for dev in [sib] + [f(k) for f in (xpeer, ypeer, zpeer) for k in (1, 2, 3)]:
+    for dev in [sib] + [zpeer(k) for k in (1, 2, 3)] + [any_peer(n) for n in ORDER]:
         pl.semaphore_signal(barrier, inc=1, device_id=dev, device_id_type=MESH)
     rows8 = lax.broadcasted_iota(jnp.int32, (8, 128), 0)
     lanes8 = lax.broadcasted_iota(jnp.int32, (8, 128), 1)
@@ -200,14 +210,20 @@
     keep = jnp.logical_and(rows8 // 4 == c, lanes8 // 64 == p % 2)
     r.vsend[6] = jnp.zeros((8, D), F32)
     r.vsend[6, :, pl.ds(pl.multiple_of((p // 2) * 128, 128), 128)] = jnp.where(keep, vown, 0.0)
-    pl.semaphore_wait(barrier, 10)
+    pl.semaphore_wait(barrier, 19)
 
     def half(h, which):
         return pl.ds(pl.multiple_of(which * h, 128), h)
 
-    for t in "qod":
+    def push_own(t):
         for n, (src, at, width) in enumerate(piece(t, 1 - c)):
             push("A" + t + "0", n, src, own(t).at[c, :, pl.ds(at, width)], sib)
+
+    push_own("q")
+    for k in (1, 3):
+        push("h10", k - 1, acts.at[c, 0], r.xall.at[z], zpeer(k))
+    push_own("o")
+    push_own("d")
     push("va", 0, r.vsend.at[6], r.vrecv.at[0], sib)
     local_wait("us", 0, r.ustage)
 
@@ -294,31 +310,56 @@
         return value + (r.vrecv[slots] + (r.vrecv[slots + 1] + r.vrecv[slots + 2]))
 
     own_ready("q")
-    weight_b("q", 0)
+    for n in ORDER:
+        push("Q", n, own("q").at[0], wref("q").at[0, c, y, x], any_peer(n))
+    local_copy("q", 0).start()
     arrived("va", 0, r.vrecv.at[0])
     v = r.vsend[6] + r.vrecv[0]
     spread("vx", 0, 1, v, xpeer)
+    push("h10", 1, acts.at[c, 0], r.xall.at[z], zpeer(2))
     own_ready("o")
     weight_b("o", 0)
     own_ready("u")
     weight_b("u", 0)
     own_ready("d")
     weight_b("d", 0)
-    local_wait("x", 0, r.xin)
-    local_wait("iin", 0, r.ids)
-    xhat0, _ = normalise(r.xin[...].astype(F32))
     v = gathered("vx", 1, v)
     spread("vy", 1, 4, v, ypeer)
-    weight_c("q", 0)
+    local_wait("iin", 0, r.ids)
+    local_wait("x", 0, r.xall.at[z])
+    weight_c("o", 0)
+    weight_c("u", 0)
+    weight_c("d", 0)
     v = gathered("vy", 4, v)
     r.vec[...] = v
 
+    def first_qkv():
+        local_copy("q", 0).wait()
+        for n in ORDER:
+            arrived("Q", n, wref("q").at[0, c, (y + 4 - n // 4) % 4, (x + 4 - n % 4) % 4])
+        mine = wref("q").at[0, c]
+        push("Dq0", 0, mine, mine, sib)
+
     def gain(l, row):
         return r.vec[4 * l + row : 4 * l + row + 1, :]
 
     def send_block(group, ref):
-        for k in (1, 2, 3):
+        for k in (1, 3):
             push(group, k - 1, ref.at[z], ref.at[z], zpeer(k))
+        pending[(group, 1)] = (ref.at[z], beyond)
+
+    beyond = zpeer(2)
+
+    def send_beyond(group, ref, k):
+        @pl.when(k == 0)
+        def _():
+            copy(group, 1, ref.at[z], ref.at[z], beyond).start()
+
+    def each_block(body):
+        @pl.loop(0, 4)
+        def _(n):
+            k = jnp.where(n == 2, 3, jnp.where(n == 3, 2, n))
+            body(k, (z + 4 - k) % 4)
 
     def flat(value):
         return value.reshape(N, value.shape[-1])
@@ -408,18 +449,26 @@
             copy(group, k - 1, ref.at[blk], ref.at[blk], sib).wait_recv()
 
     def attn_forward(l, xhat, gap_a, gap_b):
-        r.h1[l, z] = (xhat * gain(l, 0)).astype(BF)
-        send_block("h1" + str(l), r.h1.at[l])
+        if l > 0:
+            r.h1[l, z] = (xhat * gain(l, 0)).astype(BF)
+            send_block("h1" + str(l), r.h1.at[l])
         gap_a()
         weight_done("q", l)
 
-        @pl.loop(0, 4)
-        def _(k):
-            blk = (z + 4 - k) % 4
-            ag_wait("h1" + str(l), r.h1.at[l], k, blk)
+        def body(k, blk):
+            if l > 0:
+                ag_wait("h1" + str(l), r.h1.at[l], k, blk)
+            else:
+                ag_wait("h10", r.xall, k, blk)
+                hat, _ = normalise(r.xall[blk].astype(F32))
+                r.h1[0, blk] = (hat * gain(0, 0)).astype(BF)
             for j in range(2):
                 w = wref("q")[l, j].reshape(D, 384)
                 r.qkv[l, blk, :, 384 * j : 384 * j + 384] = dot(r.h1[l, blk], w).astype(BF)
+            if l > 0:
+                send_beyond("h1" + str(l), r.h1.at[l], k)
+
+        each_block(body)
 
         gap_b()
         same = image(0) == image(1)
@@ -470,9 +519,7 @@
         weight_done("u", l)
         weight_done("d", l)
 
-        @pl.loop(0, 4)
-        def _(k):
-            blk = (z + 4 - k) % 4
+        def body(k, blk):
             ag_wait("h2" + str(l), r.h2.at[l], k, blk)
             for j in range(4):
                 cols = pl.ds(256 * j, 256)
@@ -485,6 +532,9 @@
                 return dot(r.g[l, blk], weight("d", l, j))
 
             rs_put("m" + str(l), k, blk, make)
+            send_beyond("h2" + str(l), r.h2.at[l], k)
+
+        each_block(body)
 
     def finish_layer(l):
         m = rs_sum("m" + str(l))
@@ -514,6 +564,11 @@
             val = dot(lt[b, :, :depth], right(half(h, c))).reshape(4, 64, h)
             ra[l, b] = (val + ra[l, b].astype(F32)).astype(BF)
 
+        if t == "q" and l == 0:
+            for n in ORDER:
+                src = ra.at[0, (y + n // 4) % 4, (x + n % 4) % 4]
+                push("R", n, src, r.rdq.at[n], any_peer(n))
+            return
         for k in (1, 2, 3):
             if xfirst:
                 src, dev = ra.at[l, (y + k) % 4], ypeer(k)
@@ -544,10 +599,15 @@
     def grad_fourth(t, l):
         off, h, xfirst = TENSORS[t]
         ra, rc = getattr(r, "ra" + t), getattr(r, "rc" + t)
-        for k in (1, 2, 3):
-            arrived("gc" + t + str(l), k - 1, rc.at[l, k - 1])
-        val = ra[l, y, x].astype(F32) + rc[l, 0].astype(F32)
-        val = val + (rc[l, 1].astype(F32) + rc[l, 2].astype(F32))
+        val = ra[l, y, x].astype(F32)
+        if t == "q" and l == 0:
+            for n in ORDER:
+                arrived("R", n, r.rdq.at[n])
+                val = val + r.rdq[n].astype(F32)
+        else:
+            for k in (1, 2, 3):
+                arrived("gc" + t + str(l), k - 1, rc.at[l, k - 1])
+            val = val + (rc[l, 0].astype(F32) + (rc[l, 1].astype(F32) + rc[l, 2].astype(F32)))
         r.fin[l, z, :, off : off + h] = val.astype(BF)
         block = r.fin.at[l, z, :, pl.ds(off, h)]
         for k in (1, 2, 3):
@@ -558,16 +618,14 @@
         for k in (1, 2, 3):
             arrived("ge" + t + str(l), k - 1, r.fin.at[l, (z + 4 - k) % 4, :, pl.ds(off, h)])
 
-    def mlp_backward(l, dz, gap_a, gap_b):
+    def mlp_backward(l, dz, gap_a, gap_b, gap_c):
         r.dm[l, z] = (gain(l, 3) * dz).astype(BF)
         send_block("dm" + str(l), r.dm.at[l])
         r.vgrad[4 * l + 3 : 4 * l + 4, :] = jnp.sum(dz * r.m[l], axis=0, keepdims=True)
         r.dy1[...] = dz
         gap_a()
 
-        @pl.loop(0, 4)
-        def _(k):
-            blk = (z + 4 - k) % 4
+        def body(k, blk):
             ag_wait("dm" + str(l), r.dm.at[l], k, blk)
             for b in range(4):
                 cols = pl.ds(256 * b, 256)
@@ -578,6 +636,9 @@
                 return dot(r.du[blk], weight("u", l, b))
 
             rs_put("dh2" + str(l), k, blk, make)
+            send_beyond("dm" + str(l), r.dm.at[l], k)
+
+        each_block(body)
 
         def tile(ref):
             return lambda b: flat(ref[:, :, pl.ds(pl.multiple_of(b * 256, 256), 256)])
@@ -588,6 +649,8 @@
         g_l, h2_l, dm_l = r.g.at[l], r.h2.at[l], r.dm.at[l]
         grad_first("d", l, tile(g_l), cols_of(dm_l))
         grad_first("u", l, tile(h2_l), cols_of(r.du))
+        grad_second("d", l, cols_of(dm_l))
+        grad_second("u", l, cols_of(r.du))
         gap_b()
         dh2 = rs_sum("dh2" + str(l))
         dn, dg2 = norm_back(dh2, r.y1[l], gain(l, 2))
@@ -601,8 +664,13 @@
             push("do" + str(l), k - 1, r.dosend.at[l, (z + k) % 4], r.dojoin.at[l, z], zpeer(k))
         r.dojoin[l, z] = r.dosend[l, z]
         r.vgrad[4 * l + 1 : 4 * l + 2, :] = jnp.sum(dy1 * r.a[l], axis=0, keepdims=True)
-        grad_second("d", l, cols_of(dm_l))
-        grad_second("u", l, cols_of(r.du))
+
+        def right_o(cols):
+            return r.da[:, cols]
+
+        grad_first("o", l, lambda b: r.ojoin[l, b], right_o)
+        gap_c()
+        grad_second("o", l, right_o)
 
     def attn_backward(l, gap_a, gap_b):
         gap_a()
@@ -638,34 +706,25 @@
             put(c_k, dk, None)
             put(c_v, dv, None)
 
-        @pl.loop(0, 4)
-        def _(k):
-            blk = (z + 4 - k) % 4
-
+        def body(k, blk):
             def make(b):
                 return dot(r.dqkv[blk], r.wqt[l, :, 256 * b : 256 * b + 256])
 
             rs_put("dh1" + str(l), k, blk, make)
 
+        each_block(body)
+
         def left_q(b):
             return flat(r.h1[l, :, :, pl.ds(pl.multiple_of(b * 256, 256), 256)])
 
         def right_q(cols):
             return flat(r.dqkv[:, :, cols])
 
-        def left_o(b):
-            return r.ojoin[l, b]
-
-        def right_o(cols):
-            return r.da[:, cols]
-
         grad_first("q", l, left_q, right_q)
-        grad_first("o", l, left_o, right_o)
         gap_b()
         grad_second("q", l, right_q)
-        grad_second("o", l, right_o)
         dh1 = rs_sum("dh1" + str(l))
-        xin = (r.xin[...] if l == 0 else r.zout[0]).astype(F32)
+        xin = (r.xall[z] if l == 0 else r.zout[0]).astype(F32)
         dn, dg1 = norm_back(dh1, xin, gain(l, 0))
         r.vgrad[4 * l : 4 * l + 1, :] = dg1
         dx = (r.dy1[...] + dn).astype(BF)
@@ -673,23 +732,19 @@
         return dx
 
     def gap_f0a():
-        weight_c("o", 0)
-        weight_e("q", 0)
         weight_e("o", 0)
-        weight_c("u", 0)
-        weight_c("d", 0)
-        weight_d("q", 0)
+        first_qkv()
 
     def gap_f0b():
         weight_d("o", 0)
-
-    attn_forward(0, xhat0, gap_f0a, gap_f0b)
-    weight_b("q", 1)
-    weight_b("o", 1)
+        weight_e("u", 0)
+        weight_e("d", 0)
+        weight_b("q", 1)
+        weight_b("o", 1)
+
+    attn_forward(0, None, gap_f0a, gap_f0b)
     turn_qkv(0)
-    weight_e("u", 0)
-    weight_e("d", 0)
-    out_proj(0, r.xin[...].astype(F32))
+    out_proj(0, r.xall[z].astype(F32))
 
     def gap_f0c():
         weight_c("q", 1)
@@ -733,56 +788,53 @@
     local_start("out", 0, r.zout.at[c], lo_ref.at[c])
 
     rs_sent("m0")
+    def nothing():
+        pass
+
     local_wait("dz", 0, r.dzin)
-    mlp_backward(1, r.dzin[...].astype(F32), lambda: None, lambda: None)
+    mlp_backward(1, r.dzin[...].astype(F32), nothing, nothing, nothing)
     rs_sent("m1")
-
-    def gap_b1b():
+    attn_backward(1, nothing, nothing)
+
+    def gap_b0a():
         grad_third("d", 1)
         grad_third("u", 1)
-
-    attn_backward(1, lambda: None, gap_b1b)
-    for t in "qoud":
-        sent("ga" + t + "1")
-    rs_sent("dh21")
-
-    def gap_b0a():
+        grad_third("o", 1)
+        for t in "qoud":
+            sent("ga" + t + "1")
+        rs_sent("dh21")
+
+    def gap_b0b():
+        grad_third("q", 1)
+
+    def gap_b0c():
         grad_fourth("d", 1)
         grad_fourth("u", 1)
-
-    def gap_b0b():
-        grad_third("q", 1)
-        grad_third("o", 1)
-
-    mlp_backward(0, r.gout[1].astype(F32), gap_b0a, gap_b0b)
+        grad_fourth("o", 1)
+
+    mlp_backward(0, r.gout[1].astype(F32), gap_b0a, gap_b0b, gap_b0c)
     rs_sent("dh11")
 
-    def gap_b0c():
-        grad_fourth("q", 1)
-        grad_fourth("o", 1)
-
-    def gap_b0d():
-        grad_third("d", 0)
-        grad_third("u", 0)
-
-    attn_backward(0, gap_b0c, gap_b0d)
+    attn_backward(0, nothing, nothing)
 
     push("go", 0, r.gout.at[1 - c], gi_ref.at[c], sib)
     local_start("out", 1, r.gout.at[c], gi_ref.at[c])
     gv = r.vgrad[...]
     r.vsend[2] = gv
     push("ga", 0, r.vsend.at[2], r.vrecv.at[7], sib)
-    grad_fourth("d", 0)
-    grad_fourth("u", 0)
+    grad_fourth("q", 1)
+    grad_third("d", 0)
+    grad_third("u", 0)
     arrived("ga", 0, r.vrecv.at[7])
     gv = gv + r.vrecv[7]
     spread("gx", 3, 8, gv, xpeer)
-    grad_third("q", 0)
     grad_third("o", 0)
+    grad_fourth("d", 0)
+    grad_fourth("u", 0)
     gv = gathered("gx", 8, gv)
     spread("gy", 4, 11, gv, ypeer)
+    grad_fourth("o", 0)
     grad_fourth("q", 0)
-    grad_fourth("o", 0)
     gv = gathered("gy", 11, gv)
     spread("gz", 5, 14, gv, zpeer)
     for l in (1, 0):
@@ -853,7 +905,8 @@
         in_specs=[hbm] * 8,
         out_specs=(hbm,) * 5,
         scratch_shapes=[pltpu.VMEM(s, t) for s, t in SCRATCH.values()]
-        + [pltpu.SemaphoreType.DMA((len(GROUP), 3)), pltpu.SemaphoreType.DMA((len(GROUP), 3))],
+        + [pltpu.SemaphoreType.DMA((len(GROUP), 3)), pltpu.SemaphoreType.DMA((len(GROUP), 3))]
+        + [pltpu.SemaphoreType.DMA((2, 16)), pltpu.SemaphoreType.DMA((2, 16))],
         compiler_params=pltpu.CompilerParams(
             collective_id=0, has_side_effects=True, vmem_limit_bytes=64 * 1024 * 1024 - 65536
         ),
@@ -877,7 +930,7 @@
             pltpu.VMEM((8, D), F32),
             pltpu.SemaphoreType.DMA((7,)),
         ],
-        compiler_params=pltpu.CompilerParams(vmem_limit_bytes=32 * 1024 * 1024),
+        compiler_params=pltpu.CompilerParams(vmem_limit_bytes=64 * 1024 * 1024 - 65536),
     )(*out)
 
 

time: 215 us -> 241 us (1.12)
  Pallas kernels: 209 us -> 240 us
  local copies, waits for them, and re-layouts: 5.08 us -> 0 us
    pallas_call x1, Pallas kernels: 3.18 us -> 20.7 us  [local(): pl.pallas_call(assemble, out_shape=(jax.ShapeDtypeStruct((1, 2, 1, ROWS,...]
    pallas_call x1, Pallas kernels: 206 us -> 219 us  [local(): pl.pallas_call(kernel, out_shape=(jax.ShapeDtypeStruct((4, 64, HALF), BF)...]
    unnamed x10 -> x0, local copies, waits for them, and re-layouts: 5.08 us -> none
where the time goes in v5:
time: 241 us
  Pallas kernels  240 us (100%)
    pallas_call x1, Pallas kernels, local(): pl.pallas_call(kernel, out_shape=(jax.ShapeDtypeStruct((4, 64, HALF), BF)...  219 us
    pallas_call x1, Pallas kernels, local(): pl.pallas_call(assemble, out_shape=(jax.ShapeDtypeStruct((1, 2, 1, ROWS,...  20.7 us

profile of v5, /device:TPU:1, one launch (start us, length us, event | category | flops | bytes accessed | tf_op | source)
XLA Modules:
  0.0 240.7 jit_solution(14635031060940151971)
XLA Ops:
  0.6 219.2 %shard_map.135 = (bf16[4,64,1920]{2,1,0:T(8,128)(2,1)}, bf16[4,64,1920]{2,1,0:T(8,128)(2,1)}, bf16[2,72,1024]{2,1,0:T(8,128)(2,1)}, bf16[2,72,1024]{2,1,0:T(8,128)(2,1)}, f32[8,1024]{1,0:T(8,128)}) custom-call(bf16[2,1,72,1024]{3,2,1,0:T(8,128)(2,1)} %acts.1, bf16[2,1,72,1024]{3,2,1,0:T(8,128)(2,1)} %cot.1, bf16[1,64,3072]{2,1,0:T(8,128)(2,1)} %wq.1, ...), custom_call_target="tpu_custom_call" | custom-call | tf_op jit(solution)/shard_map/pallas_call | solution.py:896
  219.9 20.7 %shard_map.136 = (bf16[1,2,1,72,1024]{4,3,2,1,0:T(8,128)(2,1)}, bf16[1,2,1,72,1024]{4,3,2,1,0:T(8,128)(2,1)}, f32[1,64,3072]{2,1,0:T(8,128)}, f32[1,64,1024]{2,1...) custom-call(bf16[4,64,1920]{2,1,0:T(8,128)(2,1)} %get-tuple-element.12.fin_in, ...), custom_call_target="tpu_custom_call" | custom-call | tf_op jit(solution)/shard_map/pallas_call | solution.py:914

commit v6 on v4

--- a/solution.py
+++ b/solution.py
@@ -301,15 +301,16 @@
     own_ready("o")
     weight_b("o", 0)
     own_ready("u")
-    weight_b("u", 0)
     own_ready("d")
-    weight_b("d", 0)
     local_wait("x", 0, r.xin)
     local_wait("iin", 0, r.ids)
     xhat0, _ = normalise(r.xin[...].astype(F32))
     v = gathered("vx", 1, v)
     spread("vy", 1, 4, v, ypeer)
     weight_c("q", 0)
+    weight_c("o", 0)
+    weight_b("u", 0)
+    weight_b("d", 0)
     v = gathered("vy", 4, v)
     r.vec[...] = v
 
@@ -317,8 +318,14 @@
         return r.vec[4 * l + row : 4 * l + row + 1, :]
 
     def send_block(group, ref):
-        for k in (1, 2, 3):
+        for k in (1, 3, 2):
             push(group, k - 1, ref.at[z], ref.at[z], zpeer(k))
+
+    def each_block(body):
+        @pl.loop(0, 4)
+        def _(n):
+            k = jnp.where(n == 2, 3, jnp.where(n == 3, 2, n))
+            body(k, (z + 4 - k) % 4)
 
     def flat(value):
         return value.reshape(N, value.shape[-1])
@@ -413,13 +420,13 @@
         gap_a()
         weight_done("q", l)
 
-        @pl.loop(0, 4)
-        def _(k):
-            blk = (z + 4 - k) % 4
+        def body(k, blk):
             ag_wait("h1" + str(l), r.h1.at[l], k, blk)
             for j in range(2):
                 w = wref("q")[l, j].reshape(D, 384)
                 r.qkv[l, blk, :, 384 * j : 384 * j + 384] = dot(r.h1[l, blk], w).astype(BF)
+
+        each_block(body)
 
         gap_b()
         same = image(0) == image(1)
@@ -470,9 +477,7 @@
         weight_done("u", l)
         weight_done("d", l)
 
-        @pl.loop(0, 4)
-        def _(k):
-            blk = (z + 4 - k) % 4
+        def body(k, blk):
             ag_wait("h2" + str(l), r.h2.at[l], k, blk)
             for j in range(4):
                 cols = pl.ds(256 * j, 256)
@@ -486,6 +491,8 @@
 
             rs_put("m" + str(l), k, blk, make)
 
+        each_block(body)
+
     def finish_layer(l):
         m = rs_sum("m" + str(l))
         r.m[l] = m
@@ -565,9 +572,7 @@
         r.dy1[...] = dz
         gap_a()
 
-        @pl.loop(0, 4)
-        def _(k):
-            blk = (z + 4 - k) % 4
+        def body(k, blk):
             ag_wait("dm" + str(l), r.dm.at[l], k, blk)
             for b in range(4):
                 cols = pl.ds(256 * b, 256)
@@ -578,6 +583,8 @@
                 return dot(r.du[blk], weight("u", l, b))
 
             rs_put("dh2" + str(l), k, blk, make)
+
+        each_block(body)
 
         def tile(ref):
             return lambda b: flat(ref[:, :, pl.ds(pl.multiple_of(b * 256, 256), 256)])
@@ -638,14 +645,13 @@
             put(c_k, dk, None)
             put(c_v, dv, None)
 
-        @pl.loop(0, 4)
-        def _(k):
-            blk = (z + 4 - k) % 4
-
+        def body(k, blk):
             def make(b):
                 return dot(r.dqkv[blk], r.wqt[l, :, 256 * b : 256 * b + 256])
 
             rs_put("dh1" + str(l), k, blk, make)
+
+        each_block(body)
 
         def left_q(b):
             return flat(r.h1[l, :, :, pl.ds(pl.multiple_of(b * 256, 256), 256)])
@@ -673,7 +679,6 @@
         return dx
 
     def gap_f0a():
-        weight_c("o", 0)
         weight_e("q", 0)
         weight_e("o", 0)
         weight_c("u", 0)
@@ -737,18 +742,17 @@
     mlp_backward(1, r.dzin[...].astype(F32), lambda: None, lambda: None)
     rs_sent("m1")
 
-    def gap_b1b():
-        grad_third("d", 1)
-        grad_third("u", 1)
-
-    attn_backward(1, lambda: None, gap_b1b)
+    def nothing():
+        pass
+
+    attn_backward(1, nothing, nothing)
     for t in "qoud":
         sent("ga" + t + "1")
     rs_sent("dh21")
 
     def gap_b0a():
-        grad_fourth("d", 1)
-        grad_fourth("u", 1)
+        grad_third("d", 1)
+        grad_third("u", 1)
 
     def gap_b0b():
         grad_third("q", 1)
@@ -758,10 +762,12 @@
     rs_sent("dh11")
 
     def gap_b0c():
+        grad_fourth("d", 1)
+        grad_fourth("u", 1)
+
+    def gap_b0d():
         grad_fourth("q", 1)
         grad_fourth("o", 1)
-
-    def gap_b0d():
         grad_third("d", 0)
         grad_third("u", 0)
 
@@ -870,14 +876,14 @@
             jax.ShapeDtypeStruct((1, 4, 64), F32),
         ),
         in_specs=[hbm] * 5,
-        out_specs=(hbm,) * 2 + (vmem,) * 5,
+        out_specs=(vmem,) * 7,
         scratch_shapes=[
             pltpu.VMEM((4, 64, HALF), BF),
             pltpu.VMEM((4, 64, HALF), BF),
             pltpu.VMEM((8, D), F32),
             pltpu.SemaphoreType.DMA((7,)),
         ],
-        compiler_params=pltpu.CompilerParams(vmem_limit_bytes=32 * 1024 * 1024),
+        compiler_params=pltpu.CompilerParams(vmem_limit_bytes=64 * 1024 * 1024 - 65536),
     )(*out)
 
 

time: 215 us -> 205 us (0.953)
  local copies, waits for them, and re-layouts: 5.08 us -> 0 us
  Pallas kernels: 209 us -> 204 us
    pallas_call x1, Pallas kernels: 206 us -> 201 us  [local(): pl.pallas_call(kernel, out_shape=(jax.ShapeDtypeStruct((4, 64, HALF), BF)...]
    unnamed x10 -> x0, local copies, waits for them, and re-layouts: 5.08 us -> none
where the time goes in v6:
time: 205 us
  Pallas kernels  204 us (100%)
    pallas_call x1, Pallas kernels, local(): pl.pallas_call(kernel, out_shape=(jax.ShapeDtypeStruct((4, 64, HALF), BF)...  201 us

profile of v6, /device:TPU:1, one launch (start us, length us, event | category | flops | bytes accessed | tf_op | source)
XLA Modules:
  0.0 205.2 jit_solution(15105618586716946757)
XLA Ops:
  0.6 200.5 %shard_map.135 = (bf16[4,64,1920]{2,1,0:T(8,128)(2,1)}, bf16[4,64,1920]{2,1,0:T(8,128)(2,1)}, bf16[2,72,1024]{2,1,0:T(8,128)(2,1)}, bf16[2,72,1024]{2,1,0:T(8,128)(2,1)}, f32[8,1024]{1,0:T(8,128)}) custom-call(bf16[2,1,72,1024]{3,2,1,0:T(8,128)(2,1)} %acts.1, bf16[2,1,72,1024]{3,2,1,0:T(8,128)(2,1)} %cot.1, bf16[1,64,3072]{2,1,0:T(8,128)(2,1)} %wq.1, ...), custom_call_target="tpu_custom_call" | custom-call | tf_op jit(solution)/shard_map/pallas_call | solution.py:850
  201.2 3.9 %shard_map.136 = (bf16[1,2,1,72,1024]{4,3,2,1,0:T(8,128)(2,1)}, bf16[1,2,1,72,1024]{4,3,2,1,0:T(8,128)(2,1)}, f32[1,64,3072]{2,1,0:T(8,128)}, f32[1,64,1024]{2,1...) custom-call(bf16[4,64,1920]{2,1,0:T(8,128)(2,1)} %get-tuple-element.12.fin_in, ...), custom_call_target="tpu_custom_call" | custom-call | tf_op jit(solution)/shard_map/pallas_call | solution.py:867

commit v7 on v6

--- a/solution.py
+++ b/solution.py
@@ -57,7 +57,7 @@
     ids=((1, N), jnp.int32),
     ustage=((16, 64, 128), BF),
     usend=((64, 512), BF),
-    xin=((ROWS, D), BF),
+    xall=((4, ROWS, D), BF),
     dzin=((ROWS, D), BF),
     vsend=((7, 8, D), F32),
     vrecv=((17, 8, D), F32),
@@ -76,7 +76,6 @@
     g=((2, 4, ROWS, D), BF),
     stage=((2, 4, ROWS, D), BF),
     part=((6, 3, ROWS, D), BF),
-    mine=((ROWS, D), F32),
     m=((2, ROWS, D), F32),
     dm=((2, 4, ROWS, D), BF),
     du=((4, ROWS, D), BF),
@@ -176,7 +175,7 @@
 
     local_start("vin", 0, vectors_in, r.vectors)
     local_start("iin", 0, ids_in.at[c], r.ids)
-    local_start("x", 0, acts.at[c, 0], r.xin)
+    local_start("x", 0, acts.at[c, 0], r.xall.at[z])
 
     @pl.loop(0, 16)
     def _(n):
@@ -205,10 +204,13 @@
     def half(h, which):
         return pl.ds(pl.multiple_of(which * h, 128), h)
 
+    push("va", 0, r.vsend.at[6], r.vrecv.at[0], sib)
     for t in "qod":
         for n, (src, at, width) in enumerate(piece(t, 1 - c)):
             push("A" + t + "0", n, src, own(t).at[c, :, pl.ds(at, width)], sib)
-    push("va", 0, r.vsend.at[6], r.vrecv.at[0], sib)
+    local_wait("x", 0, r.xall.at[z])
+    for k in (1, 3, 2):
+        push("h10", k - 1, r.xall.at[z], r.xall.at[z], zpeer(k))
     local_wait("us", 0, r.ustage)
 
     def up_half(which):
@@ -293,24 +295,22 @@
             arrived(group, k - 1, r.vrecv.at[slots + k - 1])
         return value + (r.vrecv[slots] + (r.vrecv[slots + 1] + r.vrecv[slots + 2]))
 
-    own_ready("q")
-    weight_b("q", 0)
     arrived("va", 0, r.vrecv.at[0])
     v = r.vsend[6] + r.vrecv[0]
     spread("vx", 0, 1, v, xpeer)
+    own_ready("q")
+    weight_b("q", 0)
     own_ready("o")
     weight_b("o", 0)
-    own_ready("u")
-    own_ready("d")
-    local_wait("x", 0, r.xin)
-    local_wait("iin", 0, r.ids)
-    xhat0, _ = normalise(r.xin[...].astype(F32))
     v = gathered("vx", 1, v)
     spread("vy", 1, 4, v, ypeer)
     weight_c("q", 0)
     weight_c("o", 0)
+    own_ready("u")
+    own_ready("d")
     weight_b("u", 0)
     weight_b("d", 0)
+    local_wait("iin", 0, r.ids)
     v = gathered("vy", 4, v)
     r.vec[...] = v
 
@@ -321,8 +321,8 @@
         for k in (1, 3, 2):
             push(group, k - 1, ref.at[z], ref.at[z], zpeer(k))
 
-    def each_block(body):
-        @pl.loop(0, 4)
+    def each_block(body, first=0, last=4):
+        @pl.loop(first, last)
         def _(n):
             k = jnp.where(n == 2, 3, jnp.where(n == 3, 2, n))
             body(k, (z + 4 - k) % 4)
@@ -382,15 +382,7 @@
     def rs_put(group, k, blk, make):
         i = RS[group]
         for j in range(4):
-            val = make(j)
-
-            @pl.when(k == 0)
-            def _():
-                r.mine[:, 256 * j : 256 * j + 256] = val
-
-            @pl.when(k > 0)
-            def _():
-                r.stage[i % 2, blk, :, 256 * j : 256 * j + 256] = val.astype(BF)
+            r.stage[i % 2, blk, :, 256 * j : 256 * j + 256] = make(j).astype(BF)
 
         @pl.when(k > 0)
         def _():
@@ -400,7 +392,7 @@
         i = RS[group]
         for s in range(3):
             arrived(group, s, r.part.at[i, s])
-        return r.mine[...] + (
+        return r.stage[i % 2, z].astype(F32) + (
             r.part[i, 0].astype(F32) + (r.part[i, 1].astype(F32) + r.part[i, 2].astype(F32))
         )
 
@@ -415,13 +407,19 @@
             copy(group, k - 1, ref.at[blk], ref.at[blk], sib).wait_recv()
 
     def attn_forward(l, xhat, gap_a, gap_b):
-        r.h1[l, z] = (xhat * gain(l, 0)).astype(BF)
-        send_block("h1" + str(l), r.h1.at[l])
+        if l > 0:
+            r.h1[l, z] = (xhat * gain(l, 0)).astype(BF)
+            send_block("h1" + str(l), r.h1.at[l])
         gap_a()
         weight_done("q", l)
 
         def body(k, blk):
-            ag_wait("h1" + str(l), r.h1.at[l], k, blk)
+            if l > 0:
+                ag_wait("h1" + str(l), r.h1.at[l], k, blk)
+            else:
+                ag_wait("h10", r.xall, k, blk)
+                hat, _ = normalise(r.xall[blk].astype(F32))
+                r.h1[0, blk] = (hat * gain(0, 0)).astype(BF)
             for j in range(2):
                 w = wref("q")[l, j].reshape(D, 384)
                 r.qkv[l, blk, :, 384 * j : 384 * j + 384] = dot(r.h1[l, blk], w).astype(BF)
@@ -472,7 +470,7 @@
         r.h2[l, z] = (yhat * gain(l, 2)).astype(BF)
         send_block("h2" + str(l), r.h2.at[l])
 
-    def mlp_forward(l, gap_a):
+    def mlp_forward(l, gap_a, gap_b):
         gap_a()
         weight_done("u", l)
         weight_done("d", l)
@@ -491,7 +489,12 @@
 
             rs_put("m" + str(l), k, blk, make)
 
-        each_block(body)
+        if gap_b is None:
+            each_block(body)
+        else:
+            each_block(body, 0, 2)
+            gap_b()
+            each_block(body, 2, 4)
 
     def finish_layer(l):
         m = rs_sum("m" + str(l))
@@ -671,7 +674,7 @@
         grad_second("q", l, right_q)
         grad_second("o", l, right_o)
         dh1 = rs_sum("dh1" + str(l))
-        xin = (r.xin[...] if l == 0 else r.zout[0]).astype(F32)
+        xin = (r.xall[z] if l == 0 else r.zout[0]).astype(F32)
         dn, dg1 = norm_back(dh1, xin, gain(l, 0))
         r.vgrad[4 * l : 4 * l + 1, :] = dg1
         dx = (r.dy1[...] + dn).astype(BF)
@@ -680,21 +683,21 @@
 
     def gap_f0a():
         weight_e("q", 0)
+        weight_c("u", 0)
         weight_e("o", 0)
-        weight_c("u", 0)
         weight_c("d", 0)
         weight_d("q", 0)
 
     def gap_f0b():
         weight_d("o", 0)
-
-    attn_forward(0, xhat0, gap_f0a, gap_f0b)
-    weight_b("q", 1)
-    weight_b("o", 1)
+        weight_e("u", 0)
+        weight_e("d", 0)
+        weight_b("q", 1)
+        weight_b("o", 1)
+
+    attn_forward(0, None, gap_f0a, gap_f0b)
     turn_qkv(0)
-    weight_e("u", 0)
-    weight_e("d", 0)
-    out_proj(0, r.xin[...].astype(F32))
+    out_proj(0, r.xall[z].astype(F32))
 
     def gap_f0c():
         weight_c("q", 1)
@@ -705,32 +708,32 @@
         weight_b("u", 1)
         weight_b("d", 1)
 
-    mlp_forward(0, gap_f0c)
-    weight_e("q", 1)
-    weight_e("o", 1)
-    weight_c("u", 1)
-    weight_c("d", 1)
-    turn("u", 0)
+    def gap_f0d():
+        weight_e("q", 1)
+        weight_e("o", 1)
+        weight_c("u", 1)
+        weight_c("d", 1)
+
+    mlp_forward(0, gap_f0c, gap_f0d)
     weight_d("q", 1)
     weight_d("o", 1)
+    turn("u", 0)
+    weight_e("u", 1)
+    weight_e("d", 1)
     turn("d", 0)
     finish_layer(0)
     xhat1, _ = normalise(r.zout[0].astype(F32))
 
-    def gap_f1b():
-        weight_e("u", 1)
-        weight_e("d", 1)
-
-    attn_forward(1, xhat1, lambda: None, gap_f1b)
+    attn_forward(1, xhat1, lambda: None, lambda: None)
+    weight_d("u", 1)
+    weight_d("d", 1)
     turn_qkv(1)
     out_proj(1, r.zout[0].astype(F32))
 
     def gap_f1c():
         turn("o", 1)
-        weight_d("u", 1)
-        weight_d("d", 1)
-
-    mlp_forward(1, gap_f1c)
+
+    mlp_forward(1, gap_f1c, None)
     turn("u", 1)
     turn("d", 1)
     finish_layer(1)
@@ -768,8 +771,6 @@
     def gap_b0d():
         grad_fourth("q", 1)
         grad_fourth("o", 1)
-        grad_third("d", 0)
-        grad_third("u", 0)
 
     attn_backward(0, gap_b0c, gap_b0d)
 
@@ -778,13 +779,19 @@
     gv = r.vgrad[...]
     r.vsend[2] = gv
     push("ga", 0, r.vsend.at[2], r.vrecv.at[7], sib)
-    grad_fourth("d", 0)
-    grad_fourth("u", 0)
+    grad_third("d", 0)
+    grad_third("u", 0)
     arrived("ga", 0, r.vrecv.at[7])
     gv = gv + r.vrecv[7]
     spread("gx", 3, 8, gv, xpeer)
+    late = ["go"] + [n + t + "0" for n in ("ga", "gb", "gc", "ge") for t in "qoud"]
+    for group in {k[0]: None for k in list(pending)}:
+        if group not in late and group not in ("ga", "gx"):
+            sent(group)
     grad_third("q", 0)
     grad_third("o", 0)
+    grad_fourth("d", 0)
+    grad_fourth("u", 0)
     gv = gathered("gx", 8, gv)
     spread("gy", 4, 11, gv, ypeer)
     grad_fourth("q", 0)

time: 205 us -> 202 us (0.985)
  Pallas kernels: 204 us -> 201 us
    pallas_call x1, Pallas kernels: 201 us -> 197 us  [local(): pl.pallas_call(kernel, out_shape=(jax.ShapeDtypeStruct((4, 64, HALF), BF)...]
where the time goes in v7:
time: 202 us
  Pallas kernels  201 us (100%)
    pallas_call x1, Pallas kernels, local(): pl.pallas_call(kernel, out_shape=(jax.ShapeDtypeStruct((4, 64, HALF), BF)...  197 us

profile of v7, /device:TPU:1, one launch (start us, length us, event | category | flops | bytes accessed | tf_op | source)
XLA Modules:
  0.0 201.6 jit_solution(11244549554040872890)
XLA Ops:
  0.6 196.9 %shard_map.135 = (bf16[4,64,1920]{2,1,0:T(8,128)(2,1)}, bf16[4,64,1920]{2,1,0:T(8,128)(2,1)}, bf16[2,72,1024]{2,1,0:T(8,128)(2,1)}, bf16[2,72,1024]{2,1,0:T(8,128)(2,1)}, f32[8,1024]{1,0:T(8,128)}) custom-call(bf16[2,1,72,1024]{3,2,1,0:T(8,128)(2,1)} %acts.1, bf16[2,1,72,1024]{3,2,1,0:T(8,128)(2,1)} %cot.1, bf16[1,64,3072]{2,1,0:T(8,128)(2,1)} %wq.1, ...), custom_call_target="tpu_custom_call" | custom-call | tf_op jit(solution)/shard_map/pallas_call | solution.py:857
  197.6 3.9 %shard_map.136 = (bf16[1,2,1,72,1024]{4,3,2,1,0:T(8,128)(2,1)}, bf16[1,2,1,72,1024]{4,3,2,1,0:T(8,128)(2,1)}, f32[1,64,3072]{2,1,0:T(8,128)}, f32[1,64,1024]{2,1...) custom-call(bf16[4,64,1920]{2,1,0:T(8,128)(2,1)} %get-tuple-element.12.fin_in, ...), custom_call_target="tpu_custom_call" | custom-call | tf_op jit(solution)/shard_map/pallas_call | solution.py:874

commit v8 on v7

--- a/solution.py
+++ b/solution.py
@@ -605,10 +605,13 @@
         dy1 = r.dy1[...] + dn
         r.dy1[...] = dy1
         r.da[...] = (gain(l, 1) * dy1).astype(BF)
-        for b in range(4):
-            r.dosend[l, b] = dot(r.da[...], weight("o", l, b)).astype(BF)
-        for k in (1, 2, 3):
-            push("do" + str(l), k - 1, r.dosend.at[l, (z + k) % 4], r.dojoin.at[l, z], zpeer(k))
+        for k in (2, 1, 3, 0):
+            blk = (z + k) % 4
+            cols = pl.ds(pl.multiple_of(256 * (blk % 2), 256), 256)
+            w = wref("o")[l, blk // 2, :, :, :, cols].reshape(D, 256)
+            r.dosend[l, blk] = dot(r.da[...], w).astype(BF)
+            if k > 0:
+                push("do" + str(l), k - 1, r.dosend.at[l, blk], r.dojoin.at[l, z], zpeer(k))
         r.dojoin[l, z] = r.dosend[l, z]
         r.vgrad[4 * l + 1 : 4 * l + 2, :] = jnp.sum(dy1 * r.a[l], axis=0, keepdims=True)
         grad_second("d", l, cols_of(dm_l))

time: 202 us -> 204 us (level)
  no operation moved by 1% of the time
where the time goes in v8:
time: 204 us
  Pallas kernels  203 us (100%)
    pallas_call x1, Pallas kernels, local(): pl.pallas_call(kernel, out_shape=(jax.ShapeDtypeStruct((4, 64, HALF), BF)...  199 us

profile of v8, /device:TPU:1, one launch (start us, length us, event | category | flops | bytes accessed | tf_op | source)
XLA Modules:
  0.0 203.6 jit_solution(12132647091818697711)
XLA Ops:
  0.6 198.9 %shard_map.135 = (bf16[4,64,1920]{2,1,0:T(8,128)(2,1)}, bf16[4,64,1920]{2,1,0:T(8,128)(2,1)}, bf16[2,72,1024]{2,1,0:T(8,128)(2,1)}, bf16[2,72,1024]{2,1,0:T(8,128)(2,1)}, f32[8,1024]{1,0:T(8,128)}) custom-call(bf16[2,1,72,1024]{3,2,1,0:T(8,128)(2,1)} %acts.1, bf16[2,1,72,1024]{3,2,1,0:T(8,128)(2,1)} %cot.1, bf16[1,64,3072]{2,1,0:T(8,128)(2,1)} %wq.1, ...), custom_call_target="tpu_custom_call" | custom-call | tf_op jit(solution)/shard_map/pallas_call | solution.py:860
  199.6 3.9 %shard_map.136 = (bf16[1,2,1,72,1024]{4,3,2,1,0:T(8,128)(2,1)}, bf16[1,2,1,72,1024]{4,3,2,1,0:T(8,128)(2,1)}, f32[1,64,3072]{2,1,0:T(8,128)}, f32[1,64,1024]{2,1...) custom-call(bf16[4,64,1920]{2,1,0:T(8,128)(2,1)} %get-tuple-element.12.fin_in, ...), custom_call_target="tpu_custom_call" | custom-call | tf_op jit(solution)/shard_map/pallas_call | solution.py:877
